TPU v7x, 512 devices: a whole 4x8x8 slice. The times are simulated.
512 devices in a mesh: leaf: 32 (over x, z), task: 16 (over y, core).
Axes of the slice: x: 4, y: 8, z: 8, core: 2. Of those that a mesh axis runs over, the one named last changes fastest.
Arguments:
- points: bfloat16 [2097152, 64], P(('leaf', 'task')), may hold values from -6 to 6
- weights: bfloat16 [2097152, 64], P(('leaf', 'task')), may hold values from -4 to 4
- point_order: int32 [32, 16, 4096], P('leaf', 'task'), may hold values from 0 to 4095, each once within a row
- node_order: int32 [32, 16, 4096], P('leaf', 'task'), may hold values from 0 to 4095, each once within a row
- merge_order: int32 [32, 16, 2, 1024], P('leaf', 'task'), may hold values from 0 to 1023, as said below
- far_list: int32 [32, 16, 4, 3], P('leaf', 'task'), may hold values 0 or 1
- task_target: int32 [32, 16, 16, 1], P('leaf', 'task'), may hold values from -1 to 3, as said below
- task_source: int32 [32, 16, 16, 1], P('leaf', 'task'), may hold values from 0 to 3
Outputs:
- potentials: float32 [2097152, 64], P(('leaf', 'task'))
Inputs may be any that keep to these rules, and one draw needn't show every extreme that they name: `merge_order`: each row is a permutation of 0 to 1023; rows [i, j, b] are equal for all i with the same i // 2 ** (b + 1). `task_target`: -1 marks an empty slot; every device of every draw has a slab toward which all 1 slots are used.
All inputs are finite; a program needn't handle non-finite values. No bound on the sum of `far_list` on one device may be relied on, other than what follows from the above.
Results may differ from a plain program's by a relative error of at most 0.002.
Values may be sent and summed in bfloat16 or wider, within the bound.
No kernel may reach another device: no remote copies, remote signals or barrier semaphores. Data moves between devices by JAX's collectives and lax.ppermute only.
A program may use at most 64 MiB of HBM per device.

v0:
```python
import jax
import jax.numpy as jnp
from jax import lax
from jax.sharding import PartitionSpec as P

LEAF_PTS = 1024
SKEL = 512
LEVELS = 3
LEAF_DEV = 4


KERNEL_SCALE = 1.5


def partner(value, axis, stride):
    mask = 2**stride
    pairs = [(source, source ^ mask) for source in range(lax.axis_size(axis))]
    return lax.ppermute(value, axis, pairs)


def kernel(left_pts, right_pts):
    cross_term = jnp.einsum(
        "...mf,...nf->...mn", left_pts, right_pts, preferred_element_type=jnp.float32
    )
    left_norm = jnp.sum(jnp.square(left_pts.astype(jnp.float32)), axis=-1)
    right_norm = jnp.sum(jnp.square(right_pts.astype(jnp.float32)), axis=-1)
    distance = left_norm[..., :, None] + right_norm[..., None, :] - 2.0 * cross_term
    return jnp.exp(-KERNEL_SCALE / left_pts.shape[-1] * distance)


def anterpolate(skel_x, rest_x, skel_w, rest_w):
    dense = kernel(skel_x, rest_x)
    spread = (dense / jnp.sum(dense, axis=0, keepdims=True)).astype(jnp.bfloat16)
    summed = skel_w.astype(jnp.float32) + jnp.dot(
        spread, rest_w, preferred_element_type=jnp.float32
    )
    return summed.astype(jnp.bfloat16)


def merge_joined(picked, features):
    head = picked[:SKEL]
    tail = picked[SKEL:]
    merged_w = anterpolate(
        head[:, :features], tail[:, :features], head[:, features:], tail[:, features:]
    )
    return jnp.concatenate([head[:, :features], merged_w], axis=1)


def pair_terms(target_x, source_x, source_w):
    dense = kernel(target_x, source_x).astype(jnp.bfloat16)
    return jnp.einsum("ktu,kue->kte", dense, source_w, preferred_element_type=jnp.float32)


def body(points, weights, point_order, node_order, merge_order, far_list, task_target, task_source):
    features = points.shape[1]
    columns = weights.shape[1]
    point_rows = points.shape[0]
    joined = jnp.concatenate([points, weights], axis=1)
    width = joined.shape[1]
    tree = joined[point_order[0, 0]]
    node = merge_joined(tree[node_order[0, 0]], features)
    position = lax.axis_index("leaf")
    siblings = []
    for level_index in range(LEVELS):
        other = partner(node, "leaf", level_index)
        siblings.append(other)
        if level_index < LEVELS - 1:
            upper = position >> level_index & 1 == 1
            cat_rows = jnp.where(
                upper,
                jnp.concatenate([other, node], axis=0),
                jnp.concatenate([node, other], axis=0),
            )
            node = merge_joined(cat_rows[merge_order[0, 0, level_index]], features)
    tree_x = tree[:, :features]
    far_field = jnp.zeros((LEAF_DEV, LEAF_PTS, columns), jnp.float32)
    for level_index in range(LEVELS):
        other = siblings[level_index]
        dense = kernel(tree_x, other[:, :features]).astype(jnp.bfloat16)
        far_part = jnp.dot(dense, other[:, features:], preferred_element_type=jnp.float32)
        flags = far_list[0, 0, :, level_index].astype(jnp.float32)
        far_field = far_field + far_part.reshape(LEAF_DEV, LEAF_PTS, columns) * flags[:, None, None]
    leaves = tree.reshape(LEAF_DEV, LEAF_PTS, width)
    target = task_target[0, 0]
    source = task_source[0, 0]
    is_live = target >= 0
    slot_leaf = jnp.maximum(target, 0)
    requested = lax.all_to_all(source, "task", split_axis=0, concat_axis=0, tiled=True)
    arrived = lax.all_to_all(leaves[requested], "task", split_axis=0, concat_axis=0, tiled=True)

    def local_peer(group):
        own_rows, peer_rows = group
        return pair_terms(
            own_rows[..., :features], peer_rows[..., :features], peer_rows[..., features:]
        )

    slot_terms = lax.map(local_peer, (leaves[slot_leaf], arrived))
    onehot = (
        (slot_leaf[..., None] == jnp.arange(LEAF_DEV)[None, None, :]) & is_live[..., None]
    ).astype(jnp.float32)
    near_field = jnp.einsum("pcl,pcte->lte", onehot, slot_terms, precision=lax.Precision.HIGHEST)
    return (far_field + near_field).reshape(point_rows, columns)


def solution(mesh):
    return jax.shard_map(
        body,
        mesh=mesh,
        in_specs=(
            P(("leaf", "task"), None),
            P(("leaf", "task"), None),
            P("leaf", "task", None),
            P("leaf", "task", None),
            P("leaf", "task", None, None),
            P("leaf", "task", None, None),
            P("leaf", "task", None, None),
            P("leaf", "task", None, None),
        ),
        out_specs=P(("leaf", "task"), None),
        check_vma=False,
    )
```

profile of v0, /device:TPU:1, one launch (start us, length us, event | category | flops | bytes accessed | tf_op | source)
XLA Modules:
  0.0 214.7 jit_solution(16820968094093626211)
XLA Ops:
  1.3 10.1 %all-to-all-start = ((s32[16,1,1]{2,1,0:T(1,128)}), s32[16,1,1]{2,1,0:T(1,128)S(1)}, u32[]{:S(2)}, u32[]{:S(2)}) async-start(s32[16,1,1]{2,1,0:T(1,128)} %copy.53), calls=%async_computation | async-start | bytes 16384 | tf_op jit(solution)/shard_map/all_to_all | solution.py:88
  16.6 12.1 %gather_fusion = bf16[4096,128]{1,0:T(8,128)(2,1)S(1)} fusion(bf16[4096,128]{1,0:T(8,128)(2,1)S(1)} %pad_maximum_fusion, s32[4096]{0:T(1024)S(1)} %broadcast_clamp_fusion.1), kind=kCustom, calls=%fused_computation | custom fusion | bytes 2113536 | tf_op jit(solution)/shard_map/gather | solution.py:60
  28.8 12.1 %gather_fusion.1 = bf16[4096,128]{1,0:T(8,128)(2,1)S(1)} fusion(bf16[4096,128]{1,0:T(8,128)(2,1)S(1)} %gather_fusion, s32[4096]{0:T(1024)S(1)} %broadcast_clamp_fusion), kind=kCustom, calls=%fused_computation.1 | custom fusion | bytes 2113536 | tf_op jit(solution)/shard_map/gather | solution.py:61
  41.3 3.0 %gather_fusion.5 = bf16[16,1024,128]{2,1,0:T(8,128)(2,1)} fusion(bf16[4,1024,128]{2,1,0:T(8,128)(2,1)S(1)} %bitcast.71, s32[1024]{0:T(1024)S(1)} %pad_clamp_fusion), kind=kCustom, calls=%fused_computation.5 | custom fusion | bytes 8388672 | tf_op jit(solution)/shard_map/gather | solution.py:89
  44.3 7.3 %all-to-all-start.1 = ((bf16[16,1,1024,128]{3,2,1,0:T(8,128)(2,1)}), bf16[16,1,1024,128]{3,2,1,0:T(8,128)(2,1)}, u32[]{:S(2)}, u32[]{:S(2)}) async-start(bf16[16,1,1024,128]{3,2,1,0:T(8,128)(2,1)} %bitcast.73), calls=%async_computation.1 | async-start | bytes 8388608 | tf_op jit(solution)/shard_map/all_to_all | solution.py:89
  56.1 2.4 %collective-permute-start = (bf16[512,128]{0,1:T(8,128)(2,1)S(1)}, bf16[512,128]{0,1:T(8,128)(2,1)S(1)}, u32[]{:S(2)}, u32[]{:S(2)}) collective-permute-start(bf16[512,128]{0,1:T(8,128)(2,1)S(1)} %pad_maximum_fusion.1), channel_id=1, source_target_pairs={{0,16},{16,0},{32,48},{48,32},{64,80},{80,64},{96,112},{112,96},{1... | collective-permute-start | bytes 393224 | tf_op jit(solution)/shard_map/ppermute | solution.py:18
  58.6 3.1 %gather_fusion.4 = bf16[16,1024,128]{2,1,0:T(8,128)(2,1)} fusion(bf16[4,1024,128]{2,1,0:T(8,128)(2,1)S(1)} %bitcast.72, s32[1024]{0:T(1024)S(1)} %pad_clamp_fusion.1), kind=kCustom, calls=%fused_computation.4 | custom fusion | bytes 8388672 | tf_op jit(solution)/shard_map/gather | solution.py:97
  64.4 3.2 %gather_fusion.2 = bf16[1024,128]{1,0:T(8,128)(2,1)S(1)} fusion(bf16[1024,128]{1,0:T(8,128)(2,1)S(1)} %copy.47, s32[1024]{0:T(1024)S(1)} %broadcast_clamp_fusion.3), kind=kCustom, calls=%fused_computation.2 | custom fusion | bytes 528384 | tf_op jit(solution)/shard_map/gather | solution.py:74
  68.9 6.0 %collective-permute-start.1 = (bf16[512,128]{0,1:T(8,128)(2,1)S(1)}, bf16[512,128]{0,1:T(8,128)(2,1)S(1)}, u32[]{:S(2)}, u32[]{:S(2)}) collective-permute-start(bf16[512,128]{0,1:T(8,128)(2,1)S(1)} %pad_maximum_fusion.2), channel_id=1, source_target_pairs={{0,32},{16,48},{32,0},{48,16},{64,96},{80,112},{96,64},{112,80},{1... | collective-permute-start | bytes 393224 | tf_op jit(solution)/shard_map/ppermute | solution.py:18
  74.9 2.9 %fusion.16 = f32[4096,64]{0,1:T(8,128)S(1)} fusion(f32[512]{0:T(512)S(1)} %multiply_reduce_fusion.10, f32[4096]{0:T(1024)S(1)} %multiply_reduce_fusion.2, bf16[4096,128]{1,0:T(8,128)(2,1)S(1)} %gather_fusion, bf16[512,128]{0,1:T(8,128)(2,1)S(1)} %collective-permute-done), kind=kOutput, calls=%fused_computation.31 | convolution fusion | flops 547356672 | bytes 2246656 | tf_op jit(solution)/shard_map/dot_general | solution.py:80
  78.5 2.8 %collective-permute-done.1 = bf16[512,128]{0,1:T(8,128)(2,1)S(1)} collective-permute-done((bf16[512,128]{0,1:T(8,128)(2,1)S(1)}, bf16[512,128]{0,1:T(8,128)(2,1)S(1)}, u32[]{:S(2)}, u32[]{:S(2)}) %collective-permute-start.1) | collective-permute-done | bytes 131104 | tf_op jit(solution)/shard_map/ppermute | solution.py:18
  81.6 3.7 %gather_fusion.3 = bf16[1024,128]{1,0:T(8,128)(2,1)S(1)} fusion(bf16[1024,128]{1,0:T(8,128)(2,1)S(1)} %copy.50, s32[1024]{0:T(1024)} %broadcast_clamp_fusion.2), kind=kCustom, calls=%fused_computation.3 | custom fusion | bytes 528384 | tf_op jit(solution)/shard_map/gather | solution.py:74
  86.6 8.4 %collective-permute-start.2 = (bf16[512,128]{0,1:T(8,128)(2,1)S(1)}, bf16[512,128]{0,1:T(8,128)(2,1)}, u32[]{:S(2)}, u32[]{:S(2)}) collective-permute-start(bf16[512,128]{0,1:T(8,128)(2,1)S(1)} %pad_maximum_fusion.3), channel_id=1, source_target_pairs={{0,64},{16,80},{32,96},{48,112},{64,0},{80,16},{96,32},{112,48},{1... | collective-permute-start | bytes 393224 | tf_op jit(solution)/shard_map/ppermute | solution.py:18
  95.1 3.8 %fusion.17 = f32[4096,64]{0,1:T(8,128)} fusion(f32[512]{0:T(512)S(1)} %multiply_reduce_fusion.8, f32[4096]{0:T(1024)S(1)} %multiply_reduce_fusion.2, bf16[4096,128]{1,0:T(8,128)(2,1)S(1)} %gather_fusion, bf16[512,128]{0,1:T(8,128)(2,1)S(1)} %collective-permute-done.1), kind=kOutput, calls=%fused_computation.32 | convolution fusion | flops 547356672 | bytes 2246656 | tf_op jit(solution)/shard_map/dot_general | solution.py:80
  102.4 4.7 %fusion.18 = f32[4096,64]{0,1:T(8,128)} fusion(f32[512]{0:T(512)S(1)} %multiply_reduce_fusion.6, f32[4096]{0:T(1024)S(1)} %multiply_reduce_fusion.2, bf16[4096,128]{1,0:T(8,128)(2,1)S(1)} %gather_fusion, bf16[512,128]{0,1:T(8,128)(2,1)} %collective-permute-done.2), kind=kOutput, calls=%fused_computation.33 | convolution fusion | flops 547356672 | bytes 2246656 | tf_op jit(solution)/shard_map/dot_general | solution.py:80
  107.1 2.9 %reshape.301 = f32[4,1024,64]{1,0,2:T(4,128)} reshape(f32[4096,64]{0,1:T(8,128)} %fusion.18) | data formatting | bytes 2097152 | tf_op jit(solution)/shard_map/reshape | solution.py:82
  110.0 35.2 %all-to-all-done.1 = bf16[16,1,1024,128]{3,2,1,0:T(8,128)(2,1)} async-done(((bf16[16,1,1024,128]{3,2,1,0:T(8,128)(2,1)}), bf16[16,1,1024,128]{3,2,1,0:T(8,128)(2,1)}, u32[]{:S(2)}, u32[]{:S(2)}) %all-to-all-start.1) | async-done | bytes 4194336 | tf_op jit(solution)/shard_map/all_to_all | solution.py:89
  145.2 60.8 %while.10 = (s32[]{:T(128)}, f32[16,1,1024,64]{2,3,1,0:T(8,128)}, bf16[16,1,1024,128]{3,2,1,0:T(8,128)(2,1)}, bf16[16,1,1024,128]{3,2,1,0:T(8,128)(2,1)}, s32[]{:T(128)}) while((s32[]{:T(128)}, f32[16,1,1024,64]{2,3,1,0:T(8,128)}, bf16[16,1,1024,128]{3,2,1,0:T(8,128)(2,1)}, bf16[16,1,1024,128]{3,2,1,0:T(8,128)(2,1)}, s32[]{:T(128)}) %tuple.33), condition=%wide.region_16.17_spmd, body=%wide.region_13.16_spmd.sunk | while | flops 274069504 | bytes 2375757 | solution.py:97
  146.7 2.3 %fusion.76 = f32[16,1,1024,64]{2,3,1,0:T(8,128)} fusion(f32[16,1,1024,64]{2,3,1,0:T(8,128)} %get-tuple-element.90, s32[]{:T(128)S(6)} %copy.67, f32[1024]{0:T(1024)S(1)} %multiply_reduce_fusion.14, f32[1024]{0:T(1024)S(1)} %multiply_reduce_fusion.15, bf16[1,1024,128]{2,1,0:T(8,128)(2,1)S(1)} %get-tuple-element.82, ...), kind=kOutput, calls=%fused_computation.9.clone.1 | convolution fusion | flops 273678336 | bytes 1056772 | tf_op jit(solution)/shard_map/while/body/eval_jaxpr/ktu,kue->kte/dot_general | solution.py:51
  150.5 2.3 %fusion.76 = f32[16,1,1024,64]{2,3,1,0:T(8,128)} fusion(f32[16,1,1024,64]{2,3,1,0:T(8,128)} %get-tuple-element.90, s32[]{:T(128)S(6)} %copy.67, f32[1024]{0:T(1024)S(1)} %multiply_reduce_fusion.14, f32[1024]{0:T(1024)S(1)} %multiply_reduce_fusion.15, bf16[1,1024,128]{2,1,0:T(8,128)(2,1)S(1)} %get-tuple-element.82, ...), kind=kOutput, calls=%fused_computation.9.clone.1 | convolution fusion | flops 273678336 | bytes 1056772 | tf_op jit(solution)/shard_map/while/body/eval_jaxpr/ktu,kue->kte/dot_general | solution.py:51
  154.3 2.3 %fusion.76 = f32[16,1,1024,64]{2,3,1,0:T(8,128)} fusion(f32[16,1,1024,64]{2,3,1,0:T(8,128)} %get-tuple-element.90, s32[]{:T(128)S(6)} %copy.67, f32[1024]{0:T(1024)S(1)} %multiply_reduce_fusion.14, f32[1024]{0:T(1024)S(1)} %multiply_reduce_fusion.15, bf16[1,1024,128]{2,1,0:T(8,128)(2,1)S(1)} %get-tuple-element.82, ...), kind=kOutput, calls=%fused_computation.9.clone.1 | convolution fusion | flops 273678336 | bytes 1056772 | tf_op jit(solution)/shard_map/while/body/eval_jaxpr/ktu,kue->kte/dot_general | solution.py:51
  158.1 2.3 %fusion.76 = f32[16,1,1024,64]{2,3,1,0:T(8,128)} fusion(f32[16,1,1024,64]{2,3,1,0:T(8,128)} %get-tuple-element.90, s32[]{:T(128)S(6)} %copy.67, f32[1024]{0:T(1024)S(1)} %multiply_reduce_fusion.14, f32[1024]{0:T(1024)S(1)} %multiply_reduce_fusion.15, bf16[1,1024,128]{2,1,0:T(8,128)(2,1)S(1)} %get-tuple-element.82, ...), kind=kOutput, calls=%fused_computation.9.clone.1 | convolution fusion | flops 273678336 | bytes 1056772 | tf_op jit(solution)/shard_map/while/body/eval_jaxpr/ktu,kue->kte/dot_general | solution.py:51
  161.9 2.3 %fusion.76 = f32[16,1,1024,64]{2,3,1,0:T(8,128)} fusion(f32[16,1,1024,64]{2,3,1,0:T(8,128)} %get-tuple-element.90, s32[]{:T(128)S(6)} %copy.67, f32[1024]{0:T(1024)S(1)} %multiply_reduce_fusion.14, f32[1024]{0:T(1024)S(1)} %multiply_reduce_fusion.15, bf16[1,1024,128]{2,1,0:T(8,128)(2,1)S(1)} %get-tuple-element.82, ...), kind=kOutput, calls=%fused_computation.9.clone.1 | convolution fusion | flops 273678336 | bytes 1056772 | tf_op jit(solution)/shard_map/while/body/eval_jaxpr/ktu,kue->kte/dot_general | solution.py:51
  165.7 2.3 %fusion.76 = f32[16,1,1024,64]{2,3,1,0:T(8,128)} fusion(f32[16,1,1024,64]{2,3,1,0:T(8,128)} %get-tuple-element.90, s32[]{:T(128)S(6)} %copy.67, f32[1024]{0:T(1024)S(1)} %multiply_reduce_fusion.14, f32[1024]{0:T(1024)S(1)} %multiply_reduce_fusion.15, bf16[1,1024,128]{2,1,0:T(8,128)(2,1)S(1)} %get-tuple-element.82, ...), kind=kOutput, calls=%fused_computation.9.clone.1 | convolution fusion | flops 273678336 | bytes 1056772 | tf_op jit(solution)/shard_map/while/body/eval_jaxpr/ktu,kue->kte/dot_general | solution.py:51
  169.6 2.3 %fusion.76 = f32[16,1,1024,64]{2,3,1,0:T(8,128)} fusion(f32[16,1,1024,64]{2,3,1,0:T(8,128)} %get-tuple-element.90, s32[]{:T(128)S(6)} %copy.67, f32[1024]{0:T(1024)S(1)} %multiply_reduce_fusion.14, f32[1024]{0:T(1024)S(1)} %multiply_reduce_fusion.15, bf16[1,1024,128]{2,1,0:T(8,128)(2,1)S(1)} %get-tuple-element.82, ...), kind=kOutput, calls=%fused_computation.9.clone.1 | convolution fusion | flops 273678336 | bytes 1056772 | tf_op jit(solution)/shard_map/while/body/eval_jaxpr/ktu,kue->kte/dot_general | solution.py:51
  173.4 2.3 %fusion.76 = f32[16,1,1024,64]{2,3,1,0:T(8,128)} fusion(f32[16,1,1024,64]{2,3,1,0:T(8,128)} %get-tuple-element.90, s32[]{:T(128)S(6)} %copy.67, f32[1024]{0:T(1024)S(1)} %multiply_reduce_fusion.14, f32[1024]{0:T(1024)S(1)} %multiply_reduce_fusion.15, bf16[1,1024,128]{2,1,0:T(8,128)(2,1)S(1)} %get-tuple-element.82, ...), kind=kOutput, calls=%fused_computation.9.clone.1 | convolution fusion | flops 273678336 | bytes 1056772 | tf_op jit(solution)/shard_map/while/body/eval_jaxpr/ktu,kue->kte/dot_general | solution.py:51
  177.2 2.3 %fusion.76 = f32[16,1,1024,64]{2,3,1,0:T(8,128)} fusion(f32[16,1,1024,64]{2,3,1,0:T(8,128)} %get-tuple-element.90, s32[]{:T(128)S(6)} %copy.67, f32[1024]{0:T(1024)S(1)} %multiply_reduce_fusion.14, f32[1024]{0:T(1024)S(1)} %multiply_reduce_fusion.15, bf16[1,1024,128]{2,1,0:T(8,128)(2,1)S(1)} %get-tuple-element.82, ...), kind=kOutput, calls=%fused_computation.9.clone.1 | convolution fusion | flops 273678336 | bytes 1056772 | tf_op jit(solution)/shard_map/while/body/eval_jaxpr/ktu,kue->kte/dot_general | solution.py:51
  181.0 2.3 %fusion.76 = f32[16,1,1024,64]{2,3,1,0:T(8,128)} fusion(f32[16,1,1024,64]{2,3,1,0:T(8,128)} %get-tuple-element.90, s32[]{:T(128)S(6)} %copy.67, f32[1024]{0:T(1024)S(1)} %multiply_reduce_fusion.14, f32[1024]{0:T(1024)S(1)} %multiply_reduce_fusion.15, bf16[1,1024,128]{2,1,0:T(8,128)(2,1)S(1)} %get-tuple-element.82, ...), kind=kOutput, calls=%fused_computation.9.clone.1 | convolution fusion | flops 273678336 | bytes 1056772 | tf_op jit(solution)/shard_map/while/body/eval_jaxpr/ktu,kue->kte/dot_general | solution.py:51
  184.8 2.3 %fusion.76 = f32[16,1,1024,64]{2,3,1,0:T(8,128)} fusion(f32[16,1,1024,64]{2,3,1,0:T(8,128)} %get-tuple-element.90, s32[]{:T(128)S(6)} %copy.67, f32[1024]{0:T(1024)S(1)} %multiply_reduce_fusion.14, f32[1024]{0:T(1024)S(1)} %multiply_reduce_fusion.15, bf16[1,1024,128]{2,1,0:T(8,128)(2,1)S(1)} %get-tuple-element.82, ...), kind=kOutput, calls=%fused_computation.9.clone.1 | convolution fusion | flops 273678336 | bytes 1056772 | tf_op jit(solution)/shard_map/while/body/eval_jaxpr/ktu,kue->kte/dot_general | solution.py:51
  192.4 2.3 %fusion.76 = f32[16,1,1024,64]{2,3,1,0:T(8,128)} fusion(f32[16,1,1024,64]{2,3,1,0:T(8,128)} %get-tuple-element.90, s32[]{:T(128)S(6)} %copy.67, f32[1024]{0:T(1024)S(1)} %multiply_reduce_fusion.14, f32[1024]{0:T(1024)S(1)} %multiply_reduce_fusion.15, bf16[1,1024,128]{2,1,0:T(8,128)(2,1)S(1)} %get-tuple-element.82, ...), kind=kOutput, calls=%fused_computation.9.clone.1 | convolution fusion | flops 273678336 | bytes 1056772 | tf_op jit(solution)/shard_map/while/body/eval_jaxpr/ktu,kue->kte/dot_general | solution.py:51
  203.7 2.3 %fusion.76 = f32[16,1,1024,64]{2,3,1,0:T(8,128)} fusion(f32[16,1,1024,64]{2,3,1,0:T(8,128)} %get-tuple-element.90, s32[]{:T(128)S(6)} %copy.67, f32[1024]{0:T(1024)S(1)} %multiply_reduce_fusion.14, f32[1024]{0:T(1024)S(1)} %multiply_reduce_fusion.15, bf16[1,1024,128]{2,1,0:T(8,128)(2,1)S(1)} %get-tuple-element.82, ...), kind=kOutput, calls=%fused_computation.9.clone.1 | convolution fusion | flops 273678336 | bytes 1056772 | tf_op jit(solution)/shard_map/while/body/eval_jaxpr/ktu,kue->kte/dot_general | solution.py:51
  206.1 6.0 %fusion.13 = f32[4,1024,64]{1,0,2:T(4,128)S(1)} fusion(f32[16,1024,64]{1,2,0:T(8,128)} %bitcast.75, s32[16]{0:T(128)S(1)} %copy-done.3, pred[16]{0:T(512)(128)(4,1)S(1)} %copy-done.8), kind=kOutput, calls=%fused_computation.26 | convolution fusion | flops 50331776 | bytes 5242960 | tf_op jit(solution)/shard_map/pcl,pcte->lte/dot_general | solution.py:101
  (128 shorter events, 54.2 us)
Async XLA Ops:
  1.3 39.6 %all-to-all-start = ((s32[16,1,1]{2,1,0:T(1,128)}), s32[16,1,1]{2,1,0:T(1,128)S(1)}, u32[]{:S(2)}, u32[]{:S(2)}) async-start(s32[16,1,1]{2,1,0:T(1,128)} %copy.53), calls=%async_computation | async-start | bytes 16384 | tf_op jit(solution)/shard_map/all_to_all | solution.py:88
  44.3 100.9 %all-to-all-start.1 = ((bf16[16,1,1024,128]{3,2,1,0:T(8,128)(2,1)}), bf16[16,1,1024,128]{3,2,1,0:T(8,128)(2,1)}, u32[]{:S(2)}, u32[]{:S(2)}) async-start(bf16[16,1,1024,128]{3,2,1,0:T(8,128)(2,1)} %bitcast.73), calls=%async_computation.1 | async-start | bytes 8388608 | tf_op jit(solution)/shard_map/all_to_all | solution.py:89
  54.5 4.0 %copy-start.9 = (s32[1,1,16,1]{2,3,1,0:T(1,128)S(1)}, s32[1,1,16,1]{2,3,1,0:T(1,128)}, u32[]{:S(2)}) copy-start(s32[1,1,16,1]{2,3,1,0:T(1,128)} %param.16) | copy-start | bytes 196
  56.1 8.0 %collective-permute-start = (bf16[512,128]{0,1:T(8,128)(2,1)S(1)}, bf16[512,128]{0,1:T(8,128)(2,1)S(1)}, u32[]{:S(2)}, u32[]{:S(2)}) collective-permute-start(bf16[512,128]{0,1:T(8,128)(2,1)S(1)} %pad_maximum_fusion.1), channel_id=1, source_target_pairs={{0,16},{16,0},{32,48},{48,32},{64,80},{80,64},{96,112},{112,96},{1... | collective-permute-start | bytes 393224 | tf_op jit(solution)/shard_map/ppermute | solution.py:18
  58.6 3.1 %copy-start.2 = (s32[16]{0:T(128)}, s32[16]{0:T(128)S(1)}, u32[]{:S(2)}) copy-start(s32[16]{0:T(128)S(1)} %maximum_bitcast_fusion) | copy-start | bytes 196
  58.6 3.7 %copy-start.7 = (s32[1,1,4,3]{2,1,3,0:T(1,128)S(1)}, s32[1,1,4,3]{2,1,3,0:T(1,128)}, u32[]{:S(2)}) copy-start(s32[1,1,4,3]{2,1,3,0:T(1,128)} %param.15) | copy-start | bytes 148
  58.6 4.2 %copy-start.1 = (s32[1,1,2,1024]{3,2,1,0:T(2,128)S(1)}, s32[1,1,2,1024]{3,2,1,0:T(2,128)}, u32[]{:S(2)}) copy-start(s32[1,1,2,1024]{3,2,1,0:T(2,128)} %param.14) | copy-start | bytes 24580
  68.9 12.4 %collective-permute-start.1 = (bf16[512,128]{0,1:T(8,128)(2,1)S(1)}, bf16[512,128]{0,1:T(8,128)(2,1)S(1)}, u32[]{:S(2)}, u32[]{:S(2)}) collective-permute-start(bf16[512,128]{0,1:T(8,128)(2,1)S(1)} %pad_maximum_fusion.2), channel_id=1, source_target_pairs={{0,32},{16,48},{32,0},{48,16},{64,96},{80,112},{96,64},{112,80},{1... | collective-permute-start | bytes 393224 | tf_op jit(solution)/shard_map/ppermute | solution.py:18
  86.6 14.9 %collective-permute-start.2 = (bf16[512,128]{0,1:T(8,128)(2,1)S(1)}, bf16[512,128]{0,1:T(8,128)(2,1)}, u32[]{:S(2)}, u32[]{:S(2)}) collective-permute-start(bf16[512,128]{0,1:T(8,128)(2,1)S(1)} %pad_maximum_fusion.3), channel_id=1, source_target_pairs={{0,64},{16,80},{32,96},{48,112},{64,0},{80,16},{96,32},{112,48},{1... | collective-permute-start | bytes 393224 | tf_op jit(solution)/shard_map/ppermute | solution.py:18
  145.2 60.9 %copy-start.3 = (s32[16]{0:T(128)S(1)}, s32[16]{0:T(128)}, u32[]{:S(2)}) copy-start(s32[16]{0:T(128)} %copy-done.2) | copy-start | bytes 196
  145.2 60.9 %copy-start.8 = (pred[16]{0:T(512)(128)(4,1)S(1)}, pred[16]{0:T(512)(128)(4,1)}, u32[]{:S(2)}) copy-start(pred[16]{0:T(512)(128)(4,1)} %compare_bitcast_fusion) | copy-start | bytes 52
  206.1 6.0 %copy-start = (f32[4,1024,64]{1,0,2:T(4,128)S(1)}, f32[4,1024,64]{1,0,2:T(4,128)}, u32[]{:S(2)}) copy-start(f32[4,1024,64]{1,0,2:T(4,128)} %reshape.301) | copy-start | bytes 3145732
  206.1 6.0 %copy-start.4 = (f32[4]{0:T(128)S(1)}, f32[4]{0:T(128)}, u32[]{:S(2)}) copy-start(f32[4]{0:T(128)} %get-tuple-element.46) | copy-start | bytes 52
  206.1 6.0 %copy-start.5 = (f32[4]{0:T(128)S(1)}, f32[4]{0:T(128)}, u32[]{:S(2)}) copy-start(f32[4]{0:T(128)} %get-tuple-element.47) | copy-start | bytes 52
  206.1 6.1 %copy-start.6 = (f32[4]{0:T(128)S(1)}, f32[4]{0:T(128)}, u32[]{:S(2)}) copy-start(f32[4]{0:T(128)} %get-tuple-element.48) | copy-start | bytes 52
where the time goes:
time: 216 us; the launch traced here: 215 us
  local copies, waits for them, and re-layouts  67.1 us (31%)
  matrix products  59.3 us (27%)
  waiting for transfers between devices  38.7 us (18%)
  starting transfers between devices  34.2 us (16%)
  other arithmetic  14.7 us (7%)
    dot_general x16, matrix products, pair_terms(): jnp.einsum('ktu,kue->kte', dense, source_w, preferred_element_type=jnp.fl...  36.8 us
    all_to_all x1, waiting for transfers between devices, body(): lax.all_to_all(leaves[requested], 'task', split_axis=0, concat_axis=0, ti...  35.2 us
    squeeze x16, local copies, waits for them, and re-layouts, body(): slot_terms = lax.map(local_peer, (leaves[slot_leaf], arrived))  17 us
    ppermute x3, starting transfers between devices, partner(): return lax.ppermute(value, axis, pairs)  16.8 us
    gather x1, local copies, waits for them, and re-layouts, body(): node = merge_joined(tree[node_order[0, 0]], features)  12.1 us
    gather x1, local copies, waits for them, and re-layouts, body(): tree = joined[point_order[0, 0]]  12.1 us
    dot_general x3, matrix products, body(): jnp.dot(dense, other[:, features:], preferred_element_type=jnp.float32)  11.4 us
    all_to_all x1, starting transfers between devices, body(): lax.all_to_all(source, 'task', split_axis=0, concat_axis=0, tiled=True)  10.1 us
  transfers between devices with their start and end apart: 5, of which 3 were waited for; matrix products, arithmetic and copies ran while one was open for 31% of the time, Pallas kernels for 0%

commit v1 on v0

v1 whole, which is shorter than its diff:
```python
import functools
import math

import jax
import jax.numpy as jnp
from jax import lax
from jax.experimental import pallas as pl
from jax.experimental.pallas import tpu as pltpu
from jax.sharding import PartitionSpec as P

LEAF_PTS = 1024
SKEL = 512
LEVELS = 3
LEAF_DEV = 4
F = 64
PTS = LEAF_PTS * LEAF_DEV
RATE = 1.5 / 64 * math.log2(math.e)
VMEM = pl.BlockSpec(memory_space=pltpu.VMEM)
SMEM = pl.BlockSpec(memory_space=pltpu.SMEM)
PARAMS = pltpu.CompilerParams(vmem_limit_bytes=40 * 2**20)


def split3(value):
    one = value.astype(jnp.bfloat16).astype(jnp.float32)
    rest = value - one
    two = rest.astype(jnp.bfloat16).astype(jnp.float32)
    return one, two, rest - two


def gather_rows(src_ref, index_ref, dst_ref, count, unroll=16):
    def step(i, _):
        for k in range(unroll):
            at = i * unroll + k
            dst_ref[pl.ds(at, 1), :] = src_ref[pl.ds(index_ref[at], 1), :]
        return 0

    lax.fori_loop(0, count // unroll, step, 0)


def sort_kernel(order_ref, points_ref, weights_ref, out_ref, raw, tree):
    for c in range(8):
        cols = pl.ds(c * 512, 512)
        block = jnp.concatenate([points_ref[:, cols], weights_ref[:, cols]], axis=0)
        raw[pl.ds(c * 512, 512), :] = block.astype(jnp.float32).T
    gather_rows(raw, order_ref, tree, PTS)
    for leaf in range(LEAF_DEV):
        rows = tree[pl.ds(leaf * LEAF_PTS, LEAF_PTS), :]
        out_ref[leaf] = rows.T.astype(jnp.bfloat16)


def sort_leaves(order, points_t, weights_t):
    return pl.pallas_call(
        sort_kernel,
        out_shape=jax.ShapeDtypeStruct((LEAF_DEV, 2 * F, LEAF_PTS), jnp.bfloat16),
        in_specs=[SMEM, VMEM, VMEM],
        out_specs=VMEM,
        scratch_shapes=[pltpu.VMEM((PTS, 2 * F), jnp.float32), pltpu.VMEM((PTS, 2 * F), jnp.float32)],
        compiler_params=PARAMS,
        name="sort_leaves",
        cost_estimate=pl.CostEstimate(flops=0, bytes_accessed=25 * 10**6, transcendentals=0),
    )(order, points_t, weights_t)


def left_factor(rows, with_ones):
    lane = lax.broadcasted_iota(jnp.int32, rows.shape, 1)
    is_point = lane < F
    scaled = jnp.where(is_point, rows * (2 * RATE), 0.0)
    high = scaled.astype(jnp.bfloat16)
    low = scaled - high.astype(jnp.float32)
    norm = -RATE * jnp.sum(jnp.where(is_point, rows * rows, 0.0), axis=1, keepdims=True)
    one, two, three = split3(norm)
    tail = jnp.where(lane == F, one, 0.0)
    tail = jnp.where(lane == F + 1, two, tail)
    tail = jnp.where(lane == F + 2, three, tail)
    if with_ones:
        tail = jnp.where((lane > F + 2) & (lane < F + 6), 1.0, tail)
    second = jnp.where(is_point, low, tail).astype(jnp.bfloat16)
    return jnp.concatenate([high, second], axis=1)


def fill_right(right, block):
    size = block.shape[1]
    points = block[:F]
    wide = points.astype(jnp.float32)
    norm = -RATE * jnp.sum(wide * wide, axis=0, keepdims=True)
    one, two, three = split3(norm)
    row = lax.broadcasted_iota(jnp.int32, (16, size), 0)
    tail = jnp.where(row < 3, 1.0, 0.0)
    tail = jnp.where(row == 3, one, tail)
    tail = jnp.where(row == 4, two, tail)
    tail = jnp.where(row == 5, three, tail)
    right[pl.ds(0, 2 * F), :] = block
    right[pl.ds(2 * F, F), :] = points
    right[pl.ds(3 * F, 16), :] = tail.astype(jnp.bfloat16)
    right[pl.ds(3 * F + 16, F - 16), :] = jnp.zeros((F - 16, size), jnp.bfloat16)


def targets_kernel(leaves_ref, out_ref):
    for leaf in range(LEAF_DEV):
        for half in range(2):
            rows = leaves_ref[leaf, :, pl.ds(half * 512, 512)].astype(jnp.float32).T
            out_ref[pl.ds(leaf * LEAF_PTS + half * 512, 512), :] = left_factor(rows, True)


def target_factors(leaves):
    return pl.pallas_call(
        targets_kernel,
        out_shape=jax.ShapeDtypeStruct((PTS, 4 * F), jnp.bfloat16),
        in_specs=[VMEM],
        out_specs=VMEM,
        compiler_params=PARAMS,
        name="target_factors",
        cost_estimate=pl.CostEstimate(flops=0, bytes_accessed=8 * 10**6, transcendentals=0),
    )(leaves)


def skeleton(index_ref, rows, blocks, chosen, zero, right, total):
    gather_rows(rows, index_ref, chosen, SKEL)
    blank = jnp.zeros((1, 2 * F), jnp.float32)

    def wipe(i, _):
        for k in range(16):
            rows[pl.ds(index_ref[i * 16 + k], 1), :] = blank
        return 0

    lax.fori_loop(0, SKEL // 16, wipe, 0)
    left = left_factor(chosen[...], False)
    total[...] = chosen[...]
    lane = lax.broadcasted_iota(jnp.int32, (SKEL, 2 * F), 1)
    at = 0
    for block in blocks:
        block = block()
        size = block.shape[1]
        fill_right(right, block)
        exponent = jnp.dot(left, right[...], preferred_element_type=jnp.float32)
        dense = jnp.exp2(exponent)
        spread = (dense * (1.0 / jnp.sum(dense, axis=0, keepdims=True))).astype(jnp.bfloat16)
        rest = rows[pl.ds(at, size), :].astype(jnp.bfloat16)
        part = jnp.dot(spread, rest, preferred_element_type=jnp.float32)
        total[...] += jnp.where(lane < F, 0.0, part)
        at += size


def node_kernel(index_ref, leaves_ref, out_ref, rows, chosen, right, total):
    for leaf in range(LEAF_DEV):
        for half in range(2):
            part = leaves_ref[leaf, :, pl.ds(half * 512, 512)].astype(jnp.float32).T
            rows[pl.ds(leaf * LEAF_PTS + half * 512, 512), :] = part
    blocks = [
        functools.partial(lambda leaf, half: leaves_ref[leaf, :, pl.ds(half * 512, 512)], leaf, half)
        for leaf in range(LEAF_DEV)
        for half in range(2)
    ]
    skeleton(index_ref, rows, blocks, chosen, None, right, total)
    out_ref[...] = total[...].T.astype(jnp.bfloat16)


def first_node(index, leaves):
    return pl.pallas_call(
        node_kernel,
        out_shape=jax.ShapeDtypeStruct((2 * F, SKEL), jnp.bfloat16),
        in_specs=[SMEM, VMEM],
        out_specs=VMEM,
        scratch_shapes=[
            pltpu.VMEM((PTS, 2 * F), jnp.float32),
            pltpu.VMEM((SKEL, 2 * F), jnp.float32),
            pltpu.VMEM((4 * F, 512), jnp.bfloat16),
            pltpu.VMEM((SKEL, 2 * F), jnp.float32),
        ],
        compiler_params=PARAMS,
        name="first_node",
        cost_estimate=pl.CostEstimate(flops=0, bytes_accessed=20 * 10**6, transcendentals=0),
    )(index, leaves)


def merge_kernel(upper_ref, index_ref, node_ref, other_ref, out_ref, rows, chosen, right, total):
    upper = upper_ref[0]
    mine = pl.multiple_of(upper * SKEL, SKEL)
    others = pl.multiple_of((1 - upper) * SKEL, SKEL)
    rows[pl.ds(mine, SKEL), :] = node_ref[...].astype(jnp.float32).T
    rows[pl.ds(others, SKEL), :] = other_ref[...].astype(jnp.float32).T
    first = lambda: jnp.where(upper == 1, other_ref[...].astype(jnp.float32), node_ref[...].astype(jnp.float32)).astype(jnp.bfloat16)
    second = lambda: jnp.where(upper == 1, node_ref[...].astype(jnp.float32), other_ref[...].astype(jnp.float32)).astype(jnp.bfloat16)
    skeleton(index_ref, rows, [first, second], chosen, None, right, total)
    out_ref[...] = total[...].T.astype(jnp.bfloat16)


def merge_nodes(upper, index, node, other):
    return pl.pallas_call(
        merge_kernel,
        out_shape=jax.ShapeDtypeStruct((2 * F, SKEL), jnp.bfloat16),
        in_specs=[SMEM, SMEM, VMEM, VMEM],
        out_specs=VMEM,
        scratch_shapes=[
            pltpu.VMEM((2 * SKEL, 2 * F), jnp.float32),
            pltpu.VMEM((SKEL, 2 * F), jnp.float32),
            pltpu.VMEM((4 * F, 512), jnp.bfloat16),
            pltpu.VMEM((SKEL, 2 * F), jnp.float32),
        ],
        compiler_params=PARAMS,
        name="merge_nodes",
        cost_estimate=pl.CostEstimate(flops=0, bytes_accessed=8 * 10**6, transcendentals=0),
    )(upper, index, node, other)


def add_terms(target, block, left_ref, total, right):
    fill_right(right, block)
    weights = block
    base = pl.multiple_of(target * LEAF_PTS, LEAF_PTS)
    for step in range(LEAF_PTS // 256):
        rows = pl.ds(base + step * 256, 256)
        exponent = jnp.dot(left_ref[rows, :], right[...], preferred_element_type=jnp.float32)
        dense = jnp.exp2(exponent).astype(jnp.bfloat16)
        total[rows, :] += lax.dot_general(
            dense, weights, (((1,), (1,)), ((), ())), preferred_element_type=jnp.float32
        )


def near_kernel(target_ref, left_ref, before_ref, block_ref, out_ref, total, right):
    slot = pl.program_id(0)

    @pl.when(slot == 0)
    def _():
        total[...] = before_ref[...]

    target = target_ref[slot]

    @pl.when(target >= 0)
    def _():
        add_terms(target, block_ref[0], left_ref, total, right)

    @pl.when(slot == pl.num_programs(0) - 1)
    def _():
        out_ref[...] = total[...]


def near_terms(target, left, before, blocks):
    count = blocks.shape[0]
    return pl.pallas_call(
        near_kernel,
        out_shape=jax.ShapeDtypeStruct((PTS, 2 * F), jnp.float32),
        grid=(count,),
        in_specs=[SMEM, VMEM, VMEM, pl.BlockSpec((1, 2 * F, LEAF_PTS), lambda i: (i, 0, 0))],
        out_specs=VMEM,
        scratch_shapes=[pltpu.VMEM((PTS, 2 * F), jnp.float32), pltpu.VMEM((4 * F, LEAF_PTS), jnp.bfloat16)],
        compiler_params=PARAMS,
        name="near_terms",
        cost_estimate=pl.CostEstimate(flops=count * 10**9, bytes_accessed=8 * 10**6, transcendentals=0),
    )(target, left, before, blocks)


def far_kernel(flags_ref, left_ref, *refs):
    *siblings, out_ref, right = refs
    out_ref[...] = jnp.zeros_like(out_ref)
    for level, sibling in enumerate(siblings):
        block = sibling[...]
        fill_right(right, block)

        def leaf_step(leaf, _):
            @pl.when(flags_ref[leaf * LEVELS + level] != 0)
            def _():
                base = pl.multiple_of(leaf * LEAF_PTS, LEAF_PTS)
                for step in range(2):
                    rows = pl.ds(base + step * 512, 512)
                    exponent = jnp.dot(left_ref[rows, :], right[...], preferred_element_type=jnp.float32)
                    dense = jnp.exp2(exponent).astype(jnp.bfloat16)
                    out_ref[rows, :] += lax.dot_general(
                        dense, block, (((1,), (1,)), ((), ())), preferred_element_type=jnp.float32
                    )
            return 0

        lax.fori_loop(0, LEAF_DEV, leaf_step, 0)


def far_terms(flags, left, siblings):
    return pl.pallas_call(
        far_kernel,
        out_shape=jax.ShapeDtypeStruct((PTS, 2 * F), jnp.float32),
        in_specs=[SMEM, VMEM] + [VMEM] * LEVELS,
        out_specs=VMEM,
        scratch_shapes=[pltpu.VMEM((4 * F, SKEL), jnp.bfloat16)],
        compiler_params=PARAMS,
        name="far_terms",
        cost_estimate=pl.CostEstimate(flops=6 * 10**9, bytes_accessed=8 * 10**6, transcendentals=0),
    )(flags, left, *siblings)


def pick_kernel(pick_ref, leaf_ref, out_ref):
    out_ref[...] = leaf_ref[...]


def pick_leaves(pick, leaves):
    return pl.pallas_call(
        pick_kernel,
        out_shape=jax.ShapeDtypeStruct((pick.shape[0],) + leaves.shape[1:], leaves.dtype),
        grid_spec=pltpu.PrefetchScalarGridSpec(
            num_scalar_prefetch=1,
            grid=(pick.shape[0],),
            in_specs=[pl.BlockSpec((1, 2 * F, LEAF_PTS), lambda i, pick: (pick[i], 0, 0))],
            out_specs=pl.BlockSpec((1, 2 * F, LEAF_PTS), lambda i, pick: (i, 0, 0)),
        ),
        name="pick_leaves",
    )(pick, leaves)


def partner(value, axis, stride):
    pairs = [(source, source ^ 2**stride) for source in range(lax.axis_size(axis))]
    return lax.ppermute(value, axis, pairs)


def body(points, weights, point_order, node_order, merge_order, far_list, task_target, task_source):
    leaves = sort_leaves(point_order.reshape(-1), points.T, weights.T)
    requested = lax.all_to_all(task_source[0, 0], "task", split_axis=0, concat_axis=0, tiled=True)
    picked = pick_leaves(requested.reshape(-1), leaves)
    arrived = lax.all_to_all(picked, "task", split_axis=0, concat_axis=0, tiled=True)
    position = lax.axis_index("leaf")
    node = first_node(node_order.reshape(-1)[:SKEL], leaves)
    left = target_factors(leaves)
    siblings = []
    for level in range(LEVELS):
        other = partner(node, "leaf", level)
        siblings.append(other)
        if level < LEVELS - 1:
            upper = ((position >> level) & 1).astype(jnp.int32).reshape(1)
            node = merge_nodes(upper, merge_order[0, 0, level], node, other)
    far = far_terms(far_list.reshape(-1), left, siblings)
    total = near_terms(task_target.reshape(-1), left, far, arrived)
    return total[:, F:]


def solution(mesh):
    return jax.shard_map(
        body,
        mesh=mesh,
        in_specs=(
            P(("leaf", "task"), None),
            P(("leaf", "task"), None),
            P("leaf", "task", None),
            P("leaf", "task", None),
            P("leaf", "task", None, None),
            P("leaf", "task", None, None),
            P("leaf", "task", None, None),
            P("leaf", "task", None, None),
        ),
        out_specs=P(("leaf", "task"), None),
        check_vma=False,
    )
```

time: 216 us -> 159 us (0.74)
  matrix products: 59.3 us -> 0 us
  local copies, waits for them, and re-layouts: 67.1 us -> 11.1 us
  Pallas kernels: 0 us -> 53.8 us
  waiting for transfers between devices: 38.7 us -> 56.6 us
  other arithmetic: 14.7 us -> 0.95 us
    dot_general x26 -> x0, matrix products: 59.3 us -> none  [the longest x16 36.8 us: pair_terms(): jnp.einsum('ktu,kue->kte', dense, source_w, preferred_element_type=jnp.fl...]
    pallas_call x0 -> x8, Pallas kernels: none -> 53.8 us  [the longest x1 18.4 us: near_terms(): pl.pallas_call(near_kernel, out_shape=jax.ShapeDtypeStruct((PTS, 2 * F),...]
    gather x6 -> x0, local copies, waits for them, and re-layouts: 37.3 us -> none  [the longest x1 12.1 us: body(): node = merge_joined(tree[node_order[0, 0]], features)]
    squeeze x16 -> x0, local copies, waits for them, and re-layouts: 17 us -> none  [body(): slot_terms = lax.map(local_peer, (leaves[slot_leaf], arrived))]
    all_to_all x2, waiting for transfers between devices: 35.2 us -> 45.2 us  [the longest x1 45.2 us: body(): lax.all_to_all(picked, 'task', split_axis=0, concat_axis=0, tiled=True)]
    reduce_sum x42 -> x0, other arithmetic: 9.19 us -> none  [the longest x22 5.13 us: kernel(): right_norm = jnp.sum(jnp.square(right_pts.astype(jnp.float32)), axis=-1)]
    ppermute x3, waiting for transfers between devices: 3.48 us -> 11.3 us  [partner(): return lax.ppermute(value, axis, pairs)]
    reshape x3 -> x1, local copies, waits for them, and re-layouts: 5.57 us -> 0.09 us  [body(): far = far_terms(far_list.reshape(-1), left, siblings)]
  transfers between devices with their start and end apart: 5 -> 5, of which waited for: 3 -> 4; matrix products, arithmetic and copies ran while one was open for 31% -> 1% of each run, Pallas kernels for 0% -> 16%
where the time goes in v1:
time: 159 us; the launch traced here: 156 us
  waiting for transfers between devices  56.6 us (36%)
  Pallas kernels  53.8 us (34%)
  starting transfers between devices  33.6 us (21%)
  local copies, waits for them, and re-layouts  11.1 us (7%)
    all_to_all x1, waiting for transfers between devices, body(): lax.all_to_all(picked, 'task', split_axis=0, concat_axis=0, tiled=True)  45.2 us
    pallas_call x1, Pallas kernels, near_terms(): pl.pallas_call(near_kernel, out_shape=jax.ShapeDtypeStruct((PTS, 2 * F),...  18.4 us
    ppermute x3, starting transfers between devices, partner(): return lax.ppermute(value, axis, pairs)  15.6 us
    ppermute x3, waiting for transfers between devices, partner(): return lax.ppermute(value, axis, pairs)  11.3 us
    pallas_call x1, Pallas kernels, pick_leaves(): pl.pallas_call(pick_kernel, out_shape=jax.ShapeDtypeStruct((pick.shape[0]...  10.6 us
    all_to_all x1, starting transfers between devices, body(): lax.all_to_all(task_source[0, 0], 'task', split_axis=0, concat_axis=0, ti...  10.1 us
    all_to_all x1, starting transfers between devices, body(): lax.all_to_all(picked, 'task', split_axis=0, concat_axis=0, tiled=True)  7.85 us
    pallas_call x1, Pallas kernels, far_terms(): pl.pallas_call(far_kernel, out_shape=jax.ShapeDtypeStruct((PTS, 2 * F), j...  6.9 us
  transfers between devices with their start and end apart: 5, of which 4 were waited for; matrix products, arithmetic and copies ran while one was open for 1% of the time, Pallas kernels for 16%

profile of v1, /device:TPU:1, one launch (start us, length us, event | category | flops | bytes accessed | tf_op | source)
XLA Modules:
  0.0 156.1 jit_solution(1821413710671563521)
XLA Ops:
  0.0 1.3 copy.17
  1.3 10.1 %all-to-all-start = ((s32[16,1,1]{2,1,0:T(1,128)}), s32[16,1,1]{2,1,0:T(1,128)S(1)}, u32[]{:S(2)}, u32[]{:S(2)}) async-start(s32[16,1,1]{2,1,0:T(1,128)} %copy.17), calls=%async_computation | async-start | bytes 16384 | tf_op jit(solution)/shard_map/all_to_all | solution.py:313
  11.5 1.0 copy-done.2
  12.5 1.0 copy-done.3
  13.6 0.7 copy-done.4
  14.3 5.8 %sort_leaves.1.leaves_ref.leaf_ref = bf16[4,128,1024]{2,1,0:T(8,128)(2,1)S(1)} custom-call(s32[4096]{0:T(1024)S(1)} %bitcast.12, bf16[64,4096]{1,0:T(8,128)(2,1)S(1)} %bitcast.10, bf16[64,4096]{1,0:T(8,128)(2,1)S(1)} %bitcast.11), custom_call_target="tpu_custom_call" | custom-call | bytes 25000000 | tf_op jit(solution)/shard_map/sort_leaves/pallas_call | solution.py:52
  20.1 0.0 copy-start
  20.1 1.0 copy-done
  21.0 1.0 reduce.pick_ref
  22.0 10.6 %pick_leaves.1 = bf16[16,128,1024]{2,1,0:T(8,128)(2,1)} custom-call(s32[16]{0:T(128)} %reduce.pick_ref, bf16[4,128,1024]{2,1,0:T(8,128)(2,1)} %copy-done), custom_call_target="tpu_custom_call" | custom-call | tf_op jit(solution)/shard_map/pick_leaves/pallas_call | solution.py:293
  32.6 7.9 %all-to-all-start.1 = ((bf16[16,128,1024]{2,1,0:T(8,128)(2,1)}), bf16[16,128,1024]{2,1,0:T(8,128)(2,1)}, u32[]{:S(2)}, u32[]{:S(2)}) async-start(bf16[16,128,1024]{2,1,0:T(8,128)(2,1)} %pick_leaves.1), calls=%async_computation.1 | async-start | bytes 8388608 | tf_op jit(solution)/shard_map/all_to_all | solution.py:315
  40.4 0.7 slice.15
  41.1 4.7 %first_node.1.node_ref = bf16[128,512]{1,0:T(8,128)(2,1)S(1)} custom-call(s32[512]{0:T(512)S(1)} %bitcast.15, bf16[4,128,1024]{2,1,0:T(8,128)(2,1)S(1)} %copy-done.1), custom_call_target="tpu_custom_call" | custom-call | bytes 20000000 | tf_op jit(solution)/shard_map/first_node/pallas_call | solution.py:159
  45.8 0.0 copy-start.9
  45.8 2.5 %collective-permute-start = (bf16[128,512]{1,0:T(8,128)(2,1)S(1)}, bf16[128,512]{1,0:T(8,128)(2,1)S(1)}, u32[]{:S(2)}, u32[]{:S(2)}) collective-permute-start(bf16[128,512]{1,0:T(8,128)(2,1)S(1)} %first_node.1.node_ref), channel_id=1, source_target_pairs={{0,16},{16,0},{32,48},{48,32},{64,80},{80,64},{96,112},{112,96},{1... | collective-permute-start | bytes 393224 | tf_op jit(solution)/shard_map/ppermute | solution.py:308
  48.4 4.4 %collective-permute-done.other_ref.refs_0_ = bf16[128,512]{1,0:T(8,128)(2,1)S(1)} collective-permute-done((bf16[128,512]{1,0:T(8,128)(2,1)S(1)}, bf16[128,512]{1,0:T(8,128)(2,1)S(1)}, u32[]{:S(2)}, u32[]{:S(2)}) %collective-permute-start) | collective-permute-done | bytes 131104 | tf_op jit(solution)/shard_map/ppermute | solution.py:308
  52.8 2.9 %merge_nodes.2.node_ref = bf16[128,512]{1,0:T(8,128)(2,1)S(1)} custom-call(s32[1]{0:T(128)} %bitcast.5.upper_ref, s32[1024]{0:T(1024)S(1)} %bitcast.14, bf16[128,512]{1,0:T(8,128)(2,1)S(1)} %first_node.1.node_ref, bf16[128,512]{1,0:T(8,128)(2,1)S(1)} %collective-permute-done.other_ref.refs_0_), custom_call_target="tpu_custom_call" | custom-call | bytes 8000000 | tf_op jit(solution)/shard_map/merge_nodes/pallas_call | solution.py:189
  55.7 4.9 %collective-permute-start.1 = (bf16[128,512]{1,0:T(8,128)(2,1)S(1)}, bf16[128,512]{1,0:T(8,128)(2,1)S(1)}, u32[]{:S(2)}, u32[]{:S(2)}) collective-permute-start(bf16[128,512]{1,0:T(8,128)(2,1)S(1)} %merge_nodes.2.node_ref), channel_id=1, source_target_pairs={{0,32},{16,48},{32,0},{48,16},{64,96},{80,112},{96,64},{112,80},{1... | collective-permute-start | bytes 393224 | tf_op jit(solution)/shard_map/ppermute | solution.py:308
  60.6 6.2 %collective-permute-done.1.other_ref.refs_1_ = bf16[128,512]{1,0:T(8,128)(2,1)S(1)} collective-permute-done((bf16[128,512]{1,0:T(8,128)(2,1)S(1)}, bf16[128,512]{1,0:T(8,128)(2,1)S(1)}, u32[]{:S(2)}, u32[]{:S(2)}) %collective-permute-start.1) | collective-permute-done | bytes 131104 | tf_op jit(solution)/shard_map/ppermute | solution.py:308
  66.8 2.9 %merge_nodes.3 = bf16[128,512]{1,0:T(8,128)(2,1)S(1)} custom-call(s32[1]{0:T(128)} %bitcast.7.upper_ref, s32[1024]{0:T(1024)S(1)} %bitcast.13, bf16[128,512]{1,0:T(8,128)(2,1)S(1)} %merge_nodes.2.node_ref, bf16[128,512]{1,0:T(8,128)(2,1)S(1)} %collective-permute-done.1.other_ref.refs_1_), custom_call_target="tpu_custom_call" | custom-call | bytes 8000000 | tf_op jit(solution)/shard_map/merge_nodes/pallas_call | solution.py:189
  69.7 8.2 %collective-permute-start.2 = (bf16[128,512]{1,0:T(8,128)(2,1)S(1)}, bf16[128,512]{1,0:T(8,128)(2,1)}, u32[]{:S(2)}, u32[]{:S(2)}) collective-permute-start(bf16[128,512]{1,0:T(8,128)(2,1)S(1)} %merge_nodes.3), channel_id=1, source_target_pairs={{0,64},{16,80},{32,96},{48,112},{64,0},{80,16},{96,32},{112,48},{1... | collective-permute-start | bytes 393224 | tf_op jit(solution)/shard_map/ppermute | solution.py:308
  77.9 1.6 %target_factors.1.left_ref = bf16[4096,256]{1,0:T(8,128)(2,1)S(1)} custom-call(bf16[4,128,1024]{2,1,0:T(8,128)(2,1)S(1)} %copy-done.1), custom_call_target="tpu_custom_call" | custom-call | bytes 8000000 | tf_op jit(solution)/shard_map/target_factors/pallas_call | solution.py:106
  79.5 0.1 copy.16
  79.6 0.1 reshape.26.flags_ref
  79.7 0.8 collective-permute-done.2.refs_2_
  80.5 6.9 %far_terms.1.before_ref = f32[4096,128]{1,0:T(8,128)S(1)} custom-call(s32[12]{0:T(128)S(1)} %reshape.26.flags_ref, bf16[4096,256]{1,0:T(8,128)(2,1)S(1)} %target_factors.1.left_ref, bf16[128,512]{1,0:T(8,128)(2,1)S(1)} %collective-permute-done.other_ref.refs_0_, bf16[128,512]{1,0:T(8,128)(2,1)S(1)} %collective-permute-done.1.other_ref.refs_1_, ...), custom_call_target="tpu_custom_call" | custom-call | flops 6000000000 | bytes 8000000 | tf_op jit(solution)/shard_map/far_terms/pallas_call | solution.py:276
  87.4 1.4 copy-done.6
  88.8 45.2 %all-to-all-done.1.block_ref = bf16[16,128,1024]{2,1,0:T(8,128)(2,1)} async-done(((bf16[16,128,1024]{2,1,0:T(8,128)(2,1)}), bf16[16,128,1024]{2,1,0:T(8,128)(2,1)}, u32[]{:S(2)}, u32[]{:S(2)}) %all-to-all-start.1) | async-done | bytes 4194336 | tf_op jit(solution)/shard_map/all_to_all | solution.py:315
  134.0 1.6 %copy-done.7 = f32[4096,128]{1,0:T(8,128)S(1)} copy-done((f32[4096,128]{1,0:T(8,128)S(1)}, f32[4096,128]{1,0:T(8,128)}, u32[]{:S(2)}) %copy-start.7) | copy-done | bytes 2097176
  135.6 18.4 %near_terms.1 = f32[4096,128]{1,0:T(8,128)S(1)} custom-call(s32[16]{0:T(128)S(1)} %bitcast.16, bf16[4096,256]{1,0:T(8,128)(2,1)S(1)} %target_factors.1.left_ref, f32[4096,128]{1,0:T(8,128)S(1)} %copy-done.7, bf16[16,128,1024]{2,1,0:T(8,128)(2,1)} %all-to-all-done.1.block_ref), custom_call_target="tpu_custom_call" | custom-call | flops 16000000000 | bytes 8000000 | tf_op jit(solution)/shard_map/near_terms/pallas_call | solution.py:239
  154.0 0.6 slice.20
  154.6 1.6 %copy.18 = f32[4096,64]{0,1:T(8,128)} copy(f32[4096,64]{1,0:T(8,128)S(1)} %slice.20) | data formatting | bytes 2097152 | tf_op jit(solution)/shard_map/slice | solution.py:328
  (14 shorter events, 0.0 us)
Async XLA Ops:
  1.3 19.7 %all-to-all-start = ((s32[16,1,1]{2,1,0:T(1,128)}), s32[16,1,1]{2,1,0:T(1,128)S(1)}, u32[]{:S(2)}, u32[]{:S(2)}) async-start(s32[16,1,1]{2,1,0:T(1,128)} %copy.17), calls=%async_computation | async-start | bytes 16384 | tf_op jit(solution)/shard_map/all_to_all | solution.py:313
  11.5 1.0 copy-start.2
  12.5 1.0 copy-start.3
  13.6 0.7 copy-start.4
  20.1 1.0 copy-start
  32.6 8.5 %copy-start.1 = (bf16[4,128,1024]{2,1,0:T(8,128)(2,1)S(1)}, bf16[4,128,1024]{2,1,0:T(8,128)(2,1)}, u32[]{:S(2)}) copy-start(bf16[4,128,1024]{2,1,0:T(8,128)(2,1)} %copy-done) | copy-start | bytes 3145732
  32.6 15.8 %copy-start.8 = (s32[1,1,2,1024]{3,2,1,0:T(2,128)S(1)}, s32[1,1,2,1024]{3,2,1,0:T(2,128)}, u32[]{:S(2)}) copy-start(s32[1,1,2,1024]{3,2,1,0:T(2,128)} %param.12) | copy-start | bytes 24580
  32.6 101.4 %all-to-all-start.1 = ((bf16[16,128,1024]{2,1,0:T(8,128)(2,1)}), bf16[16,128,1024]{2,1,0:T(8,128)(2,1)}, u32[]{:S(2)}, u32[]{:S(2)}) async-start(bf16[16,128,1024]{2,1,0:T(8,128)(2,1)} %pick_leaves.1), calls=%async_computation.1 | async-start | bytes 8388608 | tf_op jit(solution)/shard_map/all_to_all | solution.py:315
  45.8 33.7 %copy-start.9 = (s32[1,1,4,3]{2,1,3,0:T(1,128)S(1)}, s32[1,1,4,3]{2,1,3,0:T(1,128)}, u32[]{:S(2)}) copy-start(s32[1,1,4,3]{2,1,3,0:T(1,128)} %param.13) | copy-start | bytes 148
  45.8 6.9 %collective-permute-start = (bf16[128,512]{1,0:T(8,128)(2,1)S(1)}, bf16[128,512]{1,0:T(8,128)(2,1)S(1)}, u32[]{:S(2)}, u32[]{:S(2)}) collective-permute-start(bf16[128,512]{1,0:T(8,128)(2,1)S(1)} %first_node.1.node_ref), channel_id=1, source_target_pairs={{0,16},{16,0},{32,48},{48,32},{64,80},{80,64},{96,112},{112,96},{1... | collective-permute-start | bytes 393224 | tf_op jit(solution)/shard_map/ppermute | solution.py:308
  55.7 11.0 %collective-permute-start.1 = (bf16[128,512]{1,0:T(8,128)(2,1)S(1)}, bf16[128,512]{1,0:T(8,128)(2,1)S(1)}, u32[]{:S(2)}, u32[]{:S(2)}) collective-permute-start(bf16[128,512]{1,0:T(8,128)(2,1)S(1)} %merge_nodes.2.node_ref), channel_id=1, source_target_pairs={{0,32},{16,48},{32,0},{48,16},{64,96},{80,112},{96,64},{112,80},{1... | collective-permute-start | bytes 393224 | tf_op jit(solution)/shard_map/ppermute | solution.py:308
  69.7 10.8 %collective-permute-start.2 = (bf16[128,512]{1,0:T(8,128)(2,1)S(1)}, bf16[128,512]{1,0:T(8,128)(2,1)}, u32[]{:S(2)}, u32[]{:S(2)}) collective-permute-start(bf16[128,512]{1,0:T(8,128)(2,1)S(1)} %merge_nodes.3), channel_id=1, source_target_pairs={{0,64},{16,80},{32,96},{48,112},{64,0},{80,16},{96,32},{112,48},{1... | collective-permute-start | bytes 393224 | tf_op jit(solution)/shard_map/ppermute | solution.py:308
  79.7 54.3 %copy-start.5 = (s32[1,1,16,1]{2,3,1,0:T(1,128)S(1)}, s32[1,1,16,1]{2,3,1,0:T(1,128)}, u32[]{:S(2)}) copy-start(s32[1,1,16,1]{2,3,1,0:T(1,128)} %param.14) | copy-start | bytes 196
  87.4 1.4 copy-start.6
  134.0 1.6 %copy-start.7 = (f32[4096,128]{1,0:T(8,128)S(1)}, f32[4096,128]{1,0:T(8,128)}, u32[]{:S(2)}) copy-start(f32[4096,128]{1,0:T(8,128)} %copy-done.6) | copy-start | bytes 6291460

commit v2 on v1

--- a/solution.py
+++ b/solution.py
@@ -216,42 +216,9 @@
         )
 
 
-def near_kernel(target_ref, left_ref, before_ref, block_ref, out_ref, total, right):
-    slot = pl.program_id(0)
-
-    @pl.when(slot == 0)
-    def _():
-        total[...] = before_ref[...]
-
-    target = target_ref[slot]
-
-    @pl.when(target >= 0)
-    def _():
-        add_terms(target, block_ref[0], left_ref, total, right)
-
-    @pl.when(slot == pl.num_programs(0) - 1)
-    def _():
-        out_ref[...] = total[...]
-
-
-def near_terms(target, left, before, blocks):
-    count = blocks.shape[0]
-    return pl.pallas_call(
-        near_kernel,
-        out_shape=jax.ShapeDtypeStruct((PTS, 2 * F), jnp.float32),
-        grid=(count,),
-        in_specs=[SMEM, VMEM, VMEM, pl.BlockSpec((1, 2 * F, LEAF_PTS), lambda i: (i, 0, 0))],
-        out_specs=VMEM,
-        scratch_shapes=[pltpu.VMEM((PTS, 2 * F), jnp.float32), pltpu.VMEM((4 * F, LEAF_PTS), jnp.bfloat16)],
-        compiler_params=PARAMS,
-        name="near_terms",
-        cost_estimate=pl.CostEstimate(flops=count * 10**9, bytes_accessed=8 * 10**6, transcendentals=0),
-    )(target, left, before, blocks)
-
-
-def far_kernel(flags_ref, left_ref, *refs):
+def far_kernel(flags_ref, left_ref, before_ref, *refs):
     *siblings, out_ref, right = refs
-    out_ref[...] = jnp.zeros_like(out_ref)
+    out_ref[...] = before_ref[...]
     for level, sibling in enumerate(siblings):
         block = sibling[...]
         fill_right(right, block)
@@ -272,35 +239,112 @@
         lax.fori_loop(0, LEAF_DEV, leaf_step, 0)
 
 
-def far_terms(flags, left, siblings):
+def far_terms(flags, left, before, siblings):
     return pl.pallas_call(
         far_kernel,
         out_shape=jax.ShapeDtypeStruct((PTS, 2 * F), jnp.float32),
-        in_specs=[SMEM, VMEM] + [VMEM] * LEVELS,
+        in_specs=[SMEM, VMEM, VMEM] + [VMEM] * LEVELS,
         out_specs=VMEM,
         scratch_shapes=[pltpu.VMEM((4 * F, SKEL), jnp.bfloat16)],
         compiler_params=PARAMS,
         name="far_terms",
         cost_estimate=pl.CostEstimate(flops=6 * 10**9, bytes_accessed=8 * 10**6, transcendentals=0),
-    )(flags, left, *siblings)
-
-
-def pick_kernel(pick_ref, leaf_ref, out_ref):
-    out_ref[...] = leaf_ref[...]
-
-
-def pick_leaves(pick, leaves):
-    return pl.pallas_call(
-        pick_kernel,
-        out_shape=jax.ShapeDtypeStruct((pick.shape[0],) + leaves.shape[1:], leaves.dtype),
+    )(flags, left, before, *siblings)
+
+
+def source_of(me, distance, other):
+    core = me % 2
+    chip = (me // 2 - (1 - 2 * core) * distance + 8) % 8
+    return 2 * chip + (core + other) % 2
+
+
+def copy_kernel(picks, me_ref, table_ref, *refs):
+    n_inputs = 1 + max(source for out in picks for source, _ in out)
+    inputs, outputs, sems = refs[:n_inputs], refs[n_inputs:-1], refs[-1]
+    me = me_ref[0]
+    copies = []
+    for out_ref, out in zip(outputs, picks):
+        for k, (source, leaf_of) in enumerate(out):
+            copies.append(
+                pltpu.make_async_copy(inputs[source].at[leaf_of(me, table_ref)], out_ref.at[k], sems.at[len(copies)])
+            )
+    for copy in copies:
+        copy.start()
+    for copy in copies:
+        copy.wait()
+
+
+def copy_leaves(me, table, inputs, picks):
+    size = (2 * F, LEAF_PTS)
+    return pl.pallas_call(
+        functools.partial(copy_kernel, picks),
+        out_shape=[jax.ShapeDtypeStruct((len(out),) + size, jnp.bfloat16) for out in picks],
+        in_specs=[SMEM, SMEM] + [pl.BlockSpec(memory_space=pl.ANY)] * len(inputs),
+        out_specs=[pl.BlockSpec(memory_space=pl.ANY)] * len(picks),
+        scratch_shapes=[pltpu.SemaphoreType.DMA((sum(len(out) for out in picks),))],
+        name="copy_leaves",
+        cost_estimate=pl.CostEstimate(flops=0, bytes_accessed=3 * 10**6, transcendentals=0),
+    )(me, table, *inputs)
+
+
+def asked(distance, other, to_chip, to_other):
+    def leaf_of(me, table_ref):
+        core = me % 2
+        chip = (me // 2 + (1 - 2 * core) * to_chip + 8) % 8
+        return table_ref[(2 * chip + (core + to_other) % 2) * 16 + source_of(me, distance, other)]
+
+    return leaf_of
+
+
+def at_slot(slot):
+    return lambda me, table_ref: slot
+
+
+def near_kernel(items, first, last, me_ref, source_ref, target_ref, left_ref, *refs):
+    refs = list(refs)
+    before_ref = None if first else refs.pop(0)
+    blocks, out_ref, right = refs[: len(items)], refs[len(items)], refs[-1]
+    total = refs[-2] if last else out_ref
+    total[...] = jnp.zeros_like(total) if first else before_ref[...]
+    for (distance, other, _), block_ref in zip(items, blocks):
+        target = target_ref[source_of(me_ref[0], distance, other)]
+
+        @pl.when(target >= 0)
+        def _():
+            add_terms(target, block_ref[0], left_ref, total, right)
+
+    if last:
+        for part in range(8):
+            rows = pl.ds(part * 512, 512)
+            out_ref[:, rows] = total[rows, :].T[F:]
+
+
+def near_terms(me, source, target, left, before, items, last=False):
+    def index_of(distance, other, slot):
+        if slot is not None:
+            return lambda i, me_ref, source_ref, target_ref: (slot, 0, 0)
+        return lambda i, me_ref, source_ref, target_ref: (source_ref[source_of(me_ref[0], distance, other)], 0, 0)
+
+    first = before is None
+    plan = [item[1:] for item in items]
+    scratch = [pltpu.VMEM((4 * F, LEAF_PTS), jnp.bfloat16)]
+    if last:
+        scratch = [pltpu.VMEM((PTS, 2 * F), jnp.float32)] + scratch
+    return pl.pallas_call(
+        functools.partial(near_kernel, plan, first, last),
+        out_shape=jax.ShapeDtypeStruct((F, PTS) if last else (PTS, 2 * F), jnp.float32),
         grid_spec=pltpu.PrefetchScalarGridSpec(
-            num_scalar_prefetch=1,
-            grid=(pick.shape[0],),
-            in_specs=[pl.BlockSpec((1, 2 * F, LEAF_PTS), lambda i, pick: (pick[i], 0, 0))],
-            out_specs=pl.BlockSpec((1, 2 * F, LEAF_PTS), lambda i, pick: (i, 0, 0)),
+            num_scalar_prefetch=3,
+            grid=(1,),
+            in_specs=[VMEM] * (1 if first else 2)
+            + [pl.BlockSpec((1, 2 * F, LEAF_PTS), index_of(*item)) for item in plan],
+            out_specs=VMEM,
+            scratch_shapes=scratch,
         ),
-        name="pick_leaves",
-    )(pick, leaves)
+        compiler_params=PARAMS,
+        name="near_terms",
+        cost_estimate=pl.CostEstimate(flops=len(items) * 10**9, bytes_accessed=4 * 10**6, transcendentals=0),
+    )(me, source, target, left, *([] if first else [before]), *[item[0] for item in items])
 
 
 def partner(value, axis, stride):
@@ -308,24 +352,86 @@
     return lax.ppermute(value, axis, pairs)
 
 
+def hop(value):
+    pairs = [(j, (j + 2 - 4 * (j % 2)) % 16) for j in range(16)]
+    return lax.ppermute(value, "task", pairs)
+
+
+def after(value, *others):
+    return lax.optimization_barrier((value, *others))[0]
+
+
 def body(points, weights, point_order, node_order, merge_order, far_list, task_target, task_source):
+    me = lax.axis_index("task").astype(jnp.int32).reshape(1)
+    source = task_source.reshape(-1)
+    target = task_target.reshape(-1)
+    near = functools.partial(near_terms, me, source, target)
+    position = lax.axis_index("leaf")
+
+    def merged(level, node, other):
+        upper = ((position >> level) & 1).astype(jnp.int32).reshape(1)
+        return merge_nodes(upper, merge_order[0, 0, level], node, other)
+
     leaves = sort_leaves(point_order.reshape(-1), points.T, weights.T)
-    requested = lax.all_to_all(task_source[0, 0], "task", split_axis=0, concat_axis=0, tiled=True)
-    picked = pick_leaves(requested.reshape(-1), leaves)
-    arrived = lax.all_to_all(picked, "task", split_axis=0, concat_axis=0, tiled=True)
-    position = lax.axis_index("leaf")
+    one_a = hop(leaves)
+    beside = partner(leaves, "task", 0)
     node = first_node(node_order.reshape(-1)[:SKEL], leaves)
+    beside = after(beside, node)
+    one_b = hop(beside)
+
+    sibling_0 = partner(node, "leaf", 0)
     left = target_factors(leaves)
-    siblings = []
-    for level in range(LEVELS):
-        other = partner(node, "leaf", level)
-        siblings.append(other)
-        if level < LEVELS - 1:
-            upper = ((position >> level) & 1).astype(jnp.int32).reshape(1)
-            node = merge_nodes(upper, merge_order[0, 0, level], node, other)
-    far = far_terms(far_list.reshape(-1), left, siblings)
-    total = near_terms(task_target.reshape(-1), left, far, arrived)
-    return total[:, F:]
+    row = after(jnp.broadcast_to(source, (16, 16)), node)
+    table = lax.all_to_all(row, "task", split_axis=0, concat_axis=0, tiled=True).reshape(-1)
+    sibling_0 = after(sibling_0, left)
+    node = merged(0, node, sibling_0)
+    sibling_1 = partner(node, "leaf", 1)
+    total = near(left, None, [(leaves, 0, 0, None), (after(beside, node), 0, 1, None)])
+    sibling_1 = after(sibling_1, total)
+    node = merged(1, node, sibling_1)
+    one_a = after(one_a, total)
+    two_a = hop(one_a)
+    sibling_2 = partner(node, "leaf", 2)
+    total = near(left, total, [(one_a, 1, 0, None)])
+
+    one_b = after(one_b, total)
+    two_b = hop(one_b)
+    [side_one] = copy_leaves(me, table, [one_a, one_b], [[(0, asked(1, 0, 0, 1)), (1, asked(1, 1, 0, 1))]])
+    side_one = partner(side_one, "task", 0)
+    total = near(left, total, [(one_b, 1, 1, None)])
+    total = far_terms(far_list.reshape(-1), left, total, [sibling_0, sibling_1, sibling_2])
+
+    two_a = after(two_a, total)
+    [send_a] = copy_leaves(me, table, [two_a], [[(0, asked(2, 0, 1, 0)), (0, asked(2, 0, 1, 1)), (0, asked(2, 0, 2, 0))]])
+    three_a = hop(send_a)
+    total = near(left, total, [(side_one, -1, 1, 0), (side_one, -1, 0, 1), (two_a, 2, 0, None)])
+    two_b = after(two_b, total)
+    side_two, send_b = copy_leaves(
+        me,
+        table,
+        [two_a, two_b],
+        [
+            [(0, asked(2, 0, 0, 1)), (1, asked(2, 1, 0, 1))],
+            [(1, asked(2, 1, 1, 0)), (1, asked(2, 1, 1, 1)), (1, asked(2, 1, 2, 0))],
+        ],
+    )
+    three_b = hop(send_b)
+    side_two = partner(side_two, "task", 0)
+    total = near(left, total, [(two_b, 2, 1, None)])
+    three_a = after(three_a, total)
+    total = near(left, total, [(three_a, 3, 0, 0)])
+    three_b = after(three_b, total)
+    send_c, side_three = copy_leaves(
+        me, table, [three_a, three_b], [[(0, at_slot(2)), (1, at_slot(2))], [(0, at_slot(1)), (1, at_slot(1))]]
+    )
+    four = hop(send_c)
+    side_three = partner(side_three, "task", 0)
+    total = near(left, total, [(side_two, -2, 1, 0), (side_two, -2, 0, 1), (three_b, 3, 1, 0)])
+    side_three = after(side_three, total)
+    total = near(left, total, [(side_three, -3, 1, 0), (side_three, -3, 0, 1)])
+    four = after(four, total)
+    total = near(left, total, [(four, 4, 0, 0), (four, 4, 1, 1)], last=True)
+    return total.T
 
 
 def solution(mesh):

time: 159 us -> 268 us (1.69)
  the two profiles are of different devices: /device:TPU:1 before, /device:TPU:3 now
where the time goes in v2:
time: 268 us; the launch traced here: 266 us
  Pallas kernels  177 us (66%)
  starting transfers between devices  56.8 us (21%)
  local copies, waits for them, and re-layouts  20.8 us (8%)
  waiting for transfers between devices  9.24 us (3%)
    pallas_call x4, Pallas kernels, copy_leaves(): pl.pallas_call(functools.partial(copy_kernel, picks), out_shape=[jax.Shap...  119 us
    pallas_call x9, Pallas kernels, near_terms(): pl.pallas_call(functools.partial(near_kernel, plan, first, last), out_sha...  32.9 us
    ppermute x7, starting transfers between devices, partner(): return lax.ppermute(value, axis, pairs)  28.7 us
    ppermute x7, starting transfers between devices, hop(): return lax.ppermute(value, 'task', pairs)  22.3 us
    unnamed x35, local copies, waits for them, and re-layouts  17.5 us
    pallas_call x1, Pallas kernels, far_terms(): pl.pallas_call(far_kernel, out_shape=jax.ShapeDtypeStruct((PTS, 2 * F), j...  7.23 us
    pallas_call x2, Pallas kernels, merge_nodes(): pl.pallas_call(merge_kernel, out_shape=jax.ShapeDtypeStruct((2 * F, SKEL)...  6.51 us
    all_to_all x1, waiting for transfers between devices, body(): lax.all_to_all(row, 'task', split_axis=0, concat_axis=0, tiled=True)  6.16 us
  transfers between devices with their start and end apart: 15, of which 3 were waited for; matrix products, arithmetic and copies ran while one was open for 2% of the time, Pallas kernels for 63%

profile of v2, /device:TPU:3, one launch (start us, length us, event | category | flops | bytes accessed | tf_op | source)
XLA Modules:
  0.0 266.5 jit_solution(7705218578726281382)
XLA Ops:
  2.8 5.8 %sort_leaves.1.leaves_ref.refs_0_ = bf16[4,128,1024]{2,1,0:T(8,128)(2,1)S(1)} custom-call(s32[4096]{0:T(1024)S(1)} %bitcast.15, bf16[64,4096]{1,0:T(8,128)(2,1)S(1)} %bitcast.13, bf16[64,4096]{1,0:T(8,128)(2,1)S(1)} %bitcast.14), custom_call_target="tpu_custom_call" | custom-call | bytes 25000000 | tf_op jit(solution)/shard_map/sort_leaves/pallas_call | solution.py:52
  8.6 2.6 collective-permute-start
  11.2 5.1 %collective-permute-start.2 = (bf16[4,128,1024]{2,1,0:T(8,128)(2,1)S(1)}, bf16[4,128,1024]{2,1,0:T(8,128)(2,1)}, u32[]{:S(2)}, u32[]{:S(2)}) collective-permute-start(bf16[4,128,1024]{2,1,0:T(8,128)(2,1)S(1)} %sort_leaves.1.leaves_ref.refs_0_), channel_id=1, source_target_pairs={{0,2},{1,15},{2,4},{3,1},{4,6},{5,3},{6,8},{7,5},{8,10},{9,7},{10,... | collective-permute-start | bytes 3145736 | tf_op jit(solution)/shard_map/ppermute | solution.py:357
  17.0 4.7 %first_node.1.node_ref = bf16[128,512]{1,0:T(8,128)(2,1)S(1)} custom-call(s32[512]{0:T(512)S(1)} %bitcast.37, bf16[4,128,1024]{2,1,0:T(8,128)(2,1)S(1)} %sort_leaves.1.leaves_ref.refs_0_), custom_call_target="tpu_custom_call" | custom-call | bytes 20000000 | tf_op jit(solution)/shard_map/first_node/pallas_call | solution.py:159
  21.7 3.0 %collective-permute-start.3 = (bf16[4,128,1024]{2,1,0:T(8,128)(2,1)}, bf16[4,128,1024]{2,1,0:T(8,128)(2,1)}, u32[]{:S(2)}, u32[]{:S(2)}) collective-permute-start(bf16[4,128,1024]{2,1,0:T(8,128)(2,1)} %collective-permute-done.refs_1_), channel_id=1, source_target_pairs={{0,2},{1,15},{2,4},{3,1},{4,6},{5,3},{6,8},{7,5},{8,10},{9,7},{10,... | collective-permute-start | bytes 3145736 | tf_op jit(solution)/shard_map/ppermute | solution.py:357
  24.7 4.0 %collective-permute-start.1 = (bf16[128,512]{1,0:T(8,128)(2,1)S(1)}, bf16[128,512]{1,0:T(8,128)(2,1)S(1)}, u32[]{:S(2)}, u32[]{:S(2)}) collective-permute-start(bf16[128,512]{1,0:T(8,128)(2,1)S(1)} %first_node.1.node_ref), channel_id=1, source_target_pairs={{0,16},{16,0},{32,48},{48,32},{64,80},{80,64},{96,112},{112,96},{1... | collective-permute-start | bytes 393224 | tf_op jit(solution)/shard_map/ppermute | solution.py:352
  32.0 2.9 %merge_nodes.2.node_ref = bf16[128,512]{1,0:T(8,128)(2,1)S(1)} custom-call(s32[1]{0:T(128)} %bitcast.7.upper_ref, s32[1024]{0:T(1024)S(1)} %bitcast.17, bf16[128,512]{1,0:T(8,128)(2,1)S(1)} %first_node.1.node_ref, bf16[128,512]{1,0:T(8,128)(2,1)S(1)} %collective-permute-done.1.other_ref.refs_0_), custom_call_target="tpu_custom_call" | custom-call | bytes 8000000 | tf_op jit(solution)/shard_map/merge_nodes/pallas_call | solution.py:189
  34.9 4.2 %near_terms.9.refs_0_ = f32[4096,128]{1,0:T(8,128)S(1)} custom-call(s32[1]{0:T(128)} %bitcast.me_ref, s32[16]{0:T(128)S(1)} %bitcast.18, s32[16]{0:T(128)S(1)} %bitcast.28, bf16[4096,256]{1,0:T(8,128)(2,1)S(1)} %target_factors.1.left_ref, bf16[4,128,1024]{2,1,0:T(8,128)(2,1)S(1)} %sort_leaves.1.leaves_ref.refs_0_, ...), custom_call_target="tpu_custom_call" | custom-call | flops 2000000000 | bytes 4000000 | tf_op jit(solution)/shard_map/near_terms/pallas_call | solution.py:333
  39.1 2.0 collective-permute-start.7
  41.2 4.5 %collective-permute-start.4 = (bf16[128,512]{1,0:T(8,128)(2,1)S(1)}, bf16[128,512]{1,0:T(8,128)(2,1)S(1)}, u32[]{:S(2)}, u32[]{:S(2)}) collective-permute-start(bf16[128,512]{1,0:T(8,128)(2,1)S(1)} %merge_nodes.2.node_ref), channel_id=1, source_target_pairs={{0,32},{16,48},{32,0},{48,16},{64,96},{80,112},{96,64},{112,80},{1... | collective-permute-start | bytes 393224 | tf_op jit(solution)/shard_map/ppermute | solution.py:352
  45.7 2.9 %near_terms.10.refs_0_ = f32[4096,128]{1,0:T(8,128)S(1)} custom-call(s32[1]{0:T(128)} %bitcast.me_ref, s32[16]{0:T(128)S(1)} %bitcast.19, s32[16]{0:T(128)S(1)} %bitcast.29, bf16[4096,256]{1,0:T(8,128)(2,1)S(1)} %target_factors.1.left_ref, f32[4096,128]{1,0:T(8,128)S(1)} %near_terms.9.refs_0_, bf16[4,128,1024]{2,1,0:T(8,128)(2,1)} %collective-permute-done.2.refs_1_.refs_0_), custom_call_target="tpu_custom_call" | custom-call | flops 1000000000 | bytes 4000000 | tf_op jit(solution)/shard_map/near_terms/pallas_call | solution.py:333
  50.0 3.8 %collective-permute-start.8 = (bf16[4,128,1024]{2,1,0:T(8,128)(2,1)}, bf16[4,128,1024]{2,1,0:T(8,128)(2,1)}, u32[]{:S(2)}, u32[]{:S(2)}) collective-permute-start(bf16[4,128,1024]{2,1,0:T(8,128)(2,1)} %collective-permute-done.3.refs_1_), channel_id=1, source_target_pairs={{0,2},{1,15},{2,4},{3,1},{4,6},{5,3},{6,8},{7,5},{8,10},{9,7},{10,... | collective-permute-start | bytes 3145736 | tf_op jit(solution)/shard_map/ppermute | solution.py:357
  53.8 3.6 %merge_nodes.3 = bf16[128,512]{1,0:T(8,128)(2,1)} custom-call(s32[1]{0:T(128)} %bitcast.9.upper_ref, s32[1024]{0:T(1024)S(1)} %bitcast.16, bf16[128,512]{1,0:T(8,128)(2,1)S(1)} %merge_nodes.2.node_ref, bf16[128,512]{1,0:T(8,128)(2,1)S(1)} %collective-permute-done.4.other_ref.refs_1_), custom_call_target="tpu_custom_call" | custom-call | bytes 8000000 | tf_op jit(solution)/shard_map/merge_nodes/pallas_call | solution.py:189
  57.4 9.7 %collective-permute-start.5 = (bf16[128,512]{1,0:T(8,128)(2,1)}, bf16[128,512]{1,0:T(8,128)(2,1)S(1)}, u32[]{:S(2)}, u32[]{:S(2)}) collective-permute-start(bf16[128,512]{1,0:T(8,128)(2,1)} %merge_nodes.3), channel_id=1, source_target_pairs={{0,64},{16,80},{32,96},{48,112},{64,0},{80,16},{96,32},{112,48},{1... | collective-permute-start | bytes 393224 | tf_op jit(solution)/shard_map/ppermute | solution.py:352
  67.7 5.8 %all-to-all-start = ((s32[16,1,16]{2,1,0:T(1,128)}), s32[16,1,16]{2,1,0:T(1,128)}, u32[]{:S(2)}, u32[]{:S(2)}) async-start(s32[16,1,16]{2,1,0:T(1,128)} %bitcast.11), calls=%async_computation | async-start | bytes 16384 | tf_op jit(solution)/shard_map/all_to_all | solution.py:385
  74.3 6.2 %all-to-all-done = s32[16,1,16]{2,1,0:T(1,128)} async-done(((s32[16,1,16]{2,1,0:T(1,128)}), s32[16,1,16]{2,1,0:T(1,128)}, u32[]{:S(2)}, u32[]{:S(2)}) %all-to-all-start) | async-done | bytes 1056 | tf_op jit(solution)/shard_map/all_to_all | solution.py:385
  84.4 17.7 %copy_leaves.4 = bf16[2,128,1024]{2,1,0:T(8,128)(2,1)} custom-call(s32[1]{0:T(128)} %bitcast.me_ref, s32[256]{0:T(256)} %reshape.36.table_ref, bf16[4,128,1024]{2,1,0:T(8,128)(2,1)} %collective-permute-done.2.refs_1_.refs_0_, bf16[4,128,1024]{2,1,0:T(8,128)(2,1)} %collective-permute-done.3.refs_1_), custom_call_target="tpu_custom_call" | custom-call | bytes 3000000 | tf_op jit(solution)/shard_map/copy_leaves/pallas_call | solution.py:279
  102.1 2.7 %collective-permute-start.6 = (bf16[2,128,1024]{2,1,0:T(8,128)(2,1)}, bf16[2,128,1024]{2,1,0:T(8,128)(2,1)}, u32[]{:S(2)}, u32[]{:S(2)}) collective-permute-start(bf16[2,128,1024]{2,1,0:T(8,128)(2,1)} %copy_leaves.4), channel_id=1, source_target_pairs={{0,1},{1,0},{2,3},{3,2},{4,5},{5,4},{6,7},{7,6},{8,9},{9,8},{10,11... | collective-permute-start | bytes 1572872 | tf_op jit(solution)/shard_map/ppermute | solution.py:352
  106.4 2.9 %near_terms.11.before_ref = f32[4096,128]{1,0:T(8,128)S(1)} custom-call(s32[1]{0:T(128)} %bitcast.me_ref, s32[16]{0:T(128)S(1)} %bitcast.21, s32[16]{0:T(128)S(1)} %bitcast.30, bf16[4096,256]{1,0:T(8,128)(2,1)S(1)} %target_factors.1.left_ref, f32[4096,128]{1,0:T(8,128)S(1)} %copy-done.1, bf16[4,128,1024]{2,1,0:T(8,128)(2,1)} %collective-permute-done.3.refs_1_), custom_call_target="tpu_custom_call" | custom-call | flops 1000000000 | bytes 4000000 | tf_op jit(solution)/shard_map/near_terms/pallas_call | solution.py:333
  109.3 7.2 %far_terms.1.refs_0_ = f32[4096,128]{1,0:T(8,128)S(1)} custom-call(s32[12]{0:T(128)S(1)} %reshape.33.flags_ref, bf16[4096,256]{1,0:T(8,128)(2,1)S(1)} %target_factors.1.left_ref, f32[4096,128]{1,0:T(8,128)S(1)} %near_terms.11.before_ref, bf16[128,512]{1,0:T(8,128)(2,1)S(1)} %collective-permute-done.1.other_ref.refs_0_, ...), custom_call_target="tpu_custom_call" | custom-call | flops 6000000000 | bytes 8000000 | tf_op jit(solution)/shard_map/far_terms/pallas_call | solution.py:243
  118.9 25.7 %copy_leaves.5 = bf16[3,128,1024]{2,1,0:T(8,128)(2,1)} custom-call(s32[1]{0:T(128)} %bitcast.me_ref, s32[256]{0:T(256)} %reshape.36.table_ref, bf16[4,128,1024]{2,1,0:T(8,128)(2,1)} %copy-done.2), custom_call_target="tpu_custom_call" | custom-call | bytes 3000000 | tf_op jit(solution)/shard_map/copy_leaves/pallas_call | solution.py:279
  144.6 2.9 %collective-permute-start.9 = (bf16[3,128,1024]{2,1,0:T(8,128)(2,1)}, bf16[3,128,1024]{2,1,0:T(8,128)(2,1)S(1)}, u32[]{:S(2)}, u32[]{:S(2)}) collective-permute-start(bf16[3,128,1024]{2,1,0:T(8,128)(2,1)} %copy_leaves.5), channel_id=1, source_target_pairs={{0,2},{1,15},{2,4},{3,1},{4,6},{5,3},{6,8},{7,5},{8,10},{9,7},{10,... | collective-permute-start | bytes 2359304 | tf_op jit(solution)/shard_map/ppermute | solution.py:357
  150.3 5.6 %near_terms.12.refs_0_ = f32[4096,128]{1,0:T(8,128)S(1)} custom-call(s32[1]{0:T(128)} %bitcast.me_ref, s32[16]{0:T(128)S(1)} %bitcast.22, s32[16]{0:T(128)S(1)} %bitcast.31, bf16[4096,256]{1,0:T(8,128)(2,1)S(1)} %target_factors.1.left_ref, f32[4096,128]{1,0:T(8,128)S(1)} %copy-done.15, bf16[2,128,1024]{2,1,0:T(8,128)(2,1)} %collective-permute-done.6.refs_1_.refs_2_, ...), custom_call_target="tpu_custom_call" | custom-call | flops 3000000000 | bytes 4000000 | tf_op jit(solution)/shard_map/near_terms/pallas_call | solution.py:333
  157.2 41.6 %copy_leaves.6 = (bf16[2,128,1024]{2,1,0:T(8,128)(2,1)}, bf16[3,128,1024]{2,1,0:T(8,128)(2,1)}) custom-call(s32[1]{0:T(128)} %bitcast.me_ref, s32[256]{0:T(256)} %reshape.36.table_ref, bf16[4,128,1024]{2,1,0:T(8,128)(2,1)} %copy-done.2, bf16[4,128,1024]{2,1,0:T(8,128)(2,1)} %collective-permute-done.8.refs_1_), custom_call_target="tpu_custom_call" | custom-call | bytes 3000000 | tf_op jit(solution)/shard_map/copy_leaves/pallas_call | solution.py:279
  204.2 2.9 %near_terms.13.refs_0_ = f32[4096,128]{1,0:T(8,128)S(1)} custom-call(s32[1]{0:T(128)} %bitcast.me_ref, s32[16]{0:T(128)S(1)} %bitcast.23, s32[16]{0:T(128)S(1)} %bitcast.32, bf16[4096,256]{1,0:T(8,128)(2,1)S(1)} %target_factors.1.left_ref, f32[4096,128]{1,0:T(8,128)S(1)} %copy-done.8, bf16[4,128,1024]{2,1,0:T(8,128)(2,1)} %collective-permute-done.8.refs_1_), custom_call_target="tpu_custom_call" | custom-call | flops 1000000000 | bytes 4000000 | tf_op jit(solution)/shard_map/near_terms/pallas_call | solution.py:333
  207.2 2.2 near_terms.14.refs_0_
  212.1 33.6 %copy_leaves.7 = (bf16[2,128,1024]{2,1,0:T(8,128)(2,1)}, bf16[2,128,1024]{2,1,0:T(8,128)(2,1)}) custom-call(s32[1]{0:T(128)} %bitcast.me_ref, s32[256]{0:T(256)} %reshape.36.table_ref, bf16[3,128,1024]{2,1,0:T(8,128)(2,1)} %copy-done.4, bf16[3,128,1024]{2,1,0:T(8,128)(2,1)} %collective-permute-done.11.refs_3_.refs_1_), custom_call_target="tpu_custom_call" | custom-call | bytes 3000000 | tf_op jit(solution)/shard_map/copy_leaves/pallas_call | solution.py:279
  245.7 3.2 %collective-permute-start.12 = (bf16[2,128,1024]{2,1,0:T(8,128)(2,1)}, bf16[2,128,1024]{2,1,0:T(8,128)(2,1)S(1)}, u32[]{:S(2)}, u32[]{:S(2)}) collective-permute-start(bf16[2,128,1024]{2,1,0:T(8,128)(2,1)} %get-tuple-element.35), channel_id=1, source_target_pairs={{0,1},{1,0},{2,3},{3,2},{4,5},{5,4},{6,7},{7,6},{8,9},{9,8},{10,11... | collective-permute-start | bytes 1572872 | tf_op jit(solution)/shard_map/ppermute | solution.py:352
  248.9 3.6 %collective-permute-start.13 = (bf16[2,128,1024]{2,1,0:T(8,128)(2,1)}, bf16[2,128,1024]{2,1,0:T(8,128)(2,1)S(1)}, u32[]{:S(2)}, u32[]{:S(2)}) collective-permute-start(bf16[2,128,1024]{2,1,0:T(8,128)(2,1)} %get-tuple-element.37), channel_id=1, source_target_pairs={{0,2},{1,15},{2,4},{3,1},{4,6},{5,3},{6,8},{7,5},{8,10},{9,7},{10,... | collective-permute-start | bytes 1572872 | tf_op jit(solution)/shard_map/ppermute | solution.py:357
  254.2 5.5 %near_terms.15.refs_0_ = f32[4096,128]{1,0:T(8,128)S(1)} custom-call(s32[1]{0:T(128)} %bitcast.me_ref, s32[16]{0:T(128)S(1)} %bitcast.25, s32[16]{0:T(128)S(1)} %bitcast.34, bf16[4096,256]{1,0:T(8,128)(2,1)S(1)} %target_factors.1.left_ref, f32[4096,128]{1,0:T(8,128)S(1)} %copy-done.6, bf16[2,128,1024]{2,1,0:T(8,128)(2,1)S(1)} %collective-permute-done.10.refs_1_.refs_2_, ...), custom_call_target="tpu_custom_call" | custom-call | flops 3000000000 | bytes 4000000 | tf_op jit(solution)/shard_map/near_terms/pallas_call | solution.py:333
  259.7 3.2 %near_terms.16.refs_0_ = f32[4096,128]{1,0:T(8,128)S(1)} custom-call(s32[1]{0:T(128)} %bitcast.me_ref, s32[16]{0:T(128)S(1)} %bitcast.26, s32[16]{0:T(128)S(1)} %bitcast.35, bf16[4096,256]{1,0:T(8,128)(2,1)S(1)} %target_factors.1.left_ref, f32[4096,128]{1,0:T(8,128)S(1)} %near_terms.15.refs_0_, ...), custom_call_target="tpu_custom_call" | custom-call | flops 2000000000 | bytes 4000000 | tf_op jit(solution)/shard_map/near_terms/pallas_call | solution.py:333
  262.9 3.6 %near_terms.17 = f32[64,4096]{1,0:T(8,128)} custom-call(s32[1]{0:T(128)} %bitcast.me_ref, s32[16]{0:T(128)S(1)} %bitcast.27, s32[16]{0:T(128)S(1)} %bitcast.36, bf16[4096,256]{1,0:T(8,128)(2,1)S(1)} %target_factors.1.left_ref, f32[4096,128]{1,0:T(8,128)S(1)} %near_terms.16.refs_0_, bf16[2,128,1024]{2,1,0:T(8,128)(2,1)S(1)} %collective-permute-done.13.refs_1_.refs_2_, ...), custom_call_target="tpu_custom_call" | custom-call | flops 2000000000 | bytes 4000000 | tf_op jit(solution)/shard_map/near_terms/pallas_call | solution.py:333
  (59 shorter events, 31.2 us)
Async XLA Ops:
  0.0 1.0 copy-start.9
  1.0 1.0 copy-start.10
  2.1 0.7 copy-start.11
  8.6 13.1 %collective-permute-start = (bf16[4,128,1024]{2,1,0:T(8,128)(2,1)S(1)}, bf16[4,128,1024]{2,1,0:T(8,128)(2,1)}, u32[]{:S(2)}, u32[]{:S(2)}) collective-permute-start(bf16[4,128,1024]{2,1,0:T(8,128)(2,1)S(1)} %sort_leaves.1.leaves_ref.refs_0_), channel_id=1, source_target_pairs={{0,1},{1,0},{2,3},{3,2},{4,5},{5,4},{6,7},{7,6},{8,9},{9,8},{10,11... | collective-permute-start | bytes 3145736 | tf_op jit(solution)/shard_map/ppermute | solution.py:352
  11.2 27.9 %collective-permute-start.2 = (bf16[4,128,1024]{2,1,0:T(8,128)(2,1)S(1)}, bf16[4,128,1024]{2,1,0:T(8,128)(2,1)}, u32[]{:S(2)}, u32[]{:S(2)}) collective-permute-start(bf16[4,128,1024]{2,1,0:T(8,128)(2,1)S(1)} %sort_leaves.1.leaves_ref.refs_0_), channel_id=1, source_target_pairs={{0,2},{1,15},{2,4},{3,1},{4,6},{5,3},{6,8},{7,5},{8,10},{9,7},{10,... | collective-permute-start | bytes 3145736 | tf_op jit(solution)/shard_map/ppermute | solution.py:357
  17.0 13.3 %copy-start.16 = (s32[1,1,2,1024]{3,2,1,0:T(2,128)S(1)}, s32[1,1,2,1024]{3,2,1,0:T(2,128)}, u32[]{:S(2)}) copy-start(s32[1,1,2,1024]{3,2,1,0:T(2,128)} %param.12) | copy-start | bytes 24580
  17.0 17.9 %copy-start.12 = (s32[1,1,16,1]{2,3,1,0:T(1,128)S(1)}, s32[1,1,16,1]{2,3,1,0:T(1,128)}, u32[]{:S(2)}) copy-start(s32[1,1,16,1]{2,3,1,0:T(1,128)} %param.15) | copy-start | bytes 196
  17.0 17.9 %copy-start.13 = (s32[1,1,16,1]{2,3,1,0:T(1,128)S(1)}, s32[1,1,16,1]{2,3,1,0:T(1,128)}, u32[]{:S(2)}) copy-start(s32[1,1,16,1]{2,3,1,0:T(1,128)} %param.14) | copy-start | bytes 196
  21.7 28.3 %collective-permute-start.3 = (bf16[4,128,1024]{2,1,0:T(8,128)(2,1)}, bf16[4,128,1024]{2,1,0:T(8,128)(2,1)}, u32[]{:S(2)}, u32[]{:S(2)}) collective-permute-start(bf16[4,128,1024]{2,1,0:T(8,128)(2,1)} %collective-permute-done.refs_1_), channel_id=1, source_target_pairs={{0,2},{1,15},{2,4},{3,1},{4,6},{5,3},{6,8},{7,5},{8,10},{9,7},{10,... | collective-permute-start | bytes 3145736 | tf_op jit(solution)/shard_map/ppermute | solution.py:357
  24.7 7.2 %collective-permute-start.1 = (bf16[128,512]{1,0:T(8,128)(2,1)S(1)}, bf16[128,512]{1,0:T(8,128)(2,1)S(1)}, u32[]{:S(2)}, u32[]{:S(2)}) collective-permute-start(bf16[128,512]{1,0:T(8,128)(2,1)S(1)} %first_node.1.node_ref), channel_id=1, source_target_pairs={{0,16},{16,0},{32,48},{48,32},{64,80},{80,64},{96,112},{112,96},{1... | collective-permute-start | bytes 393224 | tf_op jit(solution)/shard_map/ppermute | solution.py:352
  39.1 78.8 %collective-permute-start.7 = (bf16[4,128,1024]{2,1,0:T(8,128)(2,1)}, bf16[4,128,1024]{2,1,0:T(8,128)(2,1)S(1)}, u32[]{:S(2)}, u32[]{:S(2)}) collective-permute-start(bf16[4,128,1024]{2,1,0:T(8,128)(2,1)} %collective-permute-done.2.refs_1_.refs_0_), channel_id=1, source_target_pairs={{0,2},{1,15},{2,4},{3,1},{4,6},{5,3},{6,8},{7,5},{8,10},{9,7},{10,... | collective-permute-start | bytes 3145736 | tf_op jit(solution)/shard_map/ppermute | solution.py:357
  41.2 12.6 %collective-permute-start.4 = (bf16[128,512]{1,0:T(8,128)(2,1)S(1)}, bf16[128,512]{1,0:T(8,128)(2,1)S(1)}, u32[]{:S(2)}, u32[]{:S(2)}) collective-permute-start(bf16[128,512]{1,0:T(8,128)(2,1)S(1)} %merge_nodes.2.node_ref), channel_id=1, source_target_pairs={{0,32},{16,48},{32,0},{48,16},{64,96},{80,112},{96,64},{112,80},{1... | collective-permute-start | bytes 393224 | tf_op jit(solution)/shard_map/ppermute | solution.py:352
  48.6 1.4 copy-start
  50.0 107.2 %collective-permute-start.8 = (bf16[4,128,1024]{2,1,0:T(8,128)(2,1)}, bf16[4,128,1024]{2,1,0:T(8,128)(2,1)}, u32[]{:S(2)}, u32[]{:S(2)}) collective-permute-start(bf16[4,128,1024]{2,1,0:T(8,128)(2,1)} %collective-permute-done.3.refs_1_), channel_id=1, source_target_pairs={{0,2},{1,15},{2,4},{3,1},{4,6},{5,3},{6,8},{7,5},{8,10},{9,7},{10,... | collective-permute-start | bytes 3145736 | tf_op jit(solution)/shard_map/ppermute | solution.py:357
  57.4 52.0 %collective-permute-start.5 = (bf16[128,512]{1,0:T(8,128)(2,1)}, bf16[128,512]{1,0:T(8,128)(2,1)S(1)}, u32[]{:S(2)}, u32[]{:S(2)}) collective-permute-start(bf16[128,512]{1,0:T(8,128)(2,1)} %merge_nodes.3), channel_id=1, source_target_pairs={{0,64},{16,80},{32,96},{48,112},{64,0},{80,16},{96,32},{112,48},{1... | collective-permute-start | bytes 393224 | tf_op jit(solution)/shard_map/ppermute | solution.py:352
  67.7 12.8 %all-to-all-start = ((s32[16,1,16]{2,1,0:T(1,128)}), s32[16,1,16]{2,1,0:T(1,128)}, u32[]{:S(2)}, u32[]{:S(2)}) async-start(s32[16,1,16]{2,1,0:T(1,128)} %bitcast.11), calls=%async_computation | async-start | bytes 16384 | tf_op jit(solution)/shard_map/all_to_all | solution.py:385
  102.1 45.4 %collective-permute-start.6 = (bf16[2,128,1024]{2,1,0:T(8,128)(2,1)}, bf16[2,128,1024]{2,1,0:T(8,128)(2,1)}, u32[]{:S(2)}, u32[]{:S(2)}) collective-permute-start(bf16[2,128,1024]{2,1,0:T(8,128)(2,1)} %copy_leaves.4), channel_id=1, source_target_pairs={{0,1},{1,0},{2,3},{3,2},{4,5},{5,4},{6,7},{7,6},{8,9},{9,8},{10,11... | collective-permute-start | bytes 1572872 | tf_op jit(solution)/shard_map/ppermute | solution.py:352
  104.8 1.6 copy-start.1
  116.6 1.4 copy-start.14
  117.9 1.0 copy-start.2
  144.6 62.6 %collective-permute-start.9 = (bf16[3,128,1024]{2,1,0:T(8,128)(2,1)}, bf16[3,128,1024]{2,1,0:T(8,128)(2,1)S(1)}, u32[]{:S(2)}, u32[]{:S(2)}) collective-permute-start(bf16[3,128,1024]{2,1,0:T(8,128)(2,1)} %copy_leaves.5), channel_id=1, source_target_pairs={{0,2},{1,15},{2,4},{3,1},{4,6},{5,3},{6,8},{7,5},{8,10},{9,7},{10,... | collective-permute-start | bytes 2359304 | tf_op jit(solution)/shard_map/ppermute | solution.py:357
  147.5 1.2 copy-start.3
  148.7 1.6 copy-start.15
  155.9 1.4 copy-start.7
  198.8 13.3 %collective-permute-start.11 = (bf16[3,128,1024]{2,1,0:T(8,128)(2,1)}, bf16[3,128,1024]{2,1,0:T(8,128)(2,1)}, u32[]{:S(2)}, u32[]{:S(2)}) collective-permute-start(bf16[3,128,1024]{2,1,0:T(8,128)(2,1)} %get-tuple-element.33), channel_id=1, source_target_pairs={{0,2},{1,15},{2,4},{3,1},{4,6},{5,3},{6,8},{7,5},{8,10},{9,7},{10,... | collective-permute-start | bytes 2359304 | tf_op jit(solution)/shard_map/ppermute | solution.py:357
  200.7 51.8 %collective-permute-start.10 = (bf16[2,128,1024]{2,1,0:T(8,128)(2,1)}, bf16[2,128,1024]{2,1,0:T(8,128)(2,1)S(1)}, u32[]{:S(2)}, u32[]{:S(2)}) collective-permute-start(bf16[2,128,1024]{2,1,0:T(8,128)(2,1)} %get-tuple-element.32), channel_id=1, source_target_pairs={{0,1},{1,0},{2,3},{3,2},{4,5},{5,4},{6,7},{7,6},{8,9},{9,8},{10,11... | collective-permute-start | bytes 1572872 | tf_op jit(solution)/shard_map/ppermute | solution.py:352
  202.6 1.6 copy-start.8
  207.2 2.2 copy-start.4
  209.3 1.4 copy-start.5
  245.7 13.9 %collective-permute-start.12 = (bf16[2,128,1024]{2,1,0:T(8,128)(2,1)}, bf16[2,128,1024]{2,1,0:T(8,128)(2,1)S(1)}, u32[]{:S(2)}, u32[]{:S(2)}) collective-permute-start(bf16[2,128,1024]{2,1,0:T(8,128)(2,1)} %get-tuple-element.35), channel_id=1, source_target_pairs={{0,1},{1,0},{2,3},{3,2},{4,5},{5,4},{6,7},{7,6},{8,9},{9,8},{10,11... | collective-permute-start | bytes 1572872 | tf_op jit(solution)/shard_map/ppermute | solution.py:352
  248.9 14.0 %collective-permute-start.13 = (bf16[2,128,1024]{2,1,0:T(8,128)(2,1)}, bf16[2,128,1024]{2,1,0:T(8,128)(2,1)S(1)}, u32[]{:S(2)}, u32[]{:S(2)}) collective-permute-start(bf16[2,128,1024]{2,1,0:T(8,128)(2,1)} %get-tuple-element.37), channel_id=1, source_target_pairs={{0,2},{1,15},{2,4},{3,1},{4,6},{5,3},{6,8},{7,5},{8,10},{9,7},{10,... | collective-permute-start | bytes 1572872 | tf_op jit(solution)/shard_map/ppermute | solution.py:357
  252.6 1.6 copy-start.6

commit v3 on v2

v3 whole, which is shorter than its diff:
```python
import functools
import math

import jax
import jax.numpy as jnp
from jax import lax
from jax.experimental import pallas as pl
from jax.experimental.pallas import tpu as pltpu
from jax.sharding import PartitionSpec as P

LEAF_PTS = 1024
SKEL = 512
LEVELS = 3
LEAF_DEV = 4
F = 64
PTS = LEAF_PTS * LEAF_DEV
RATE = 1.5 / 64 * math.log2(math.e)
VMEM = pl.BlockSpec(memory_space=pltpu.VMEM)
SMEM = pl.BlockSpec(memory_space=pltpu.SMEM)
HBM = pl.BlockSpec(memory_space=pltpu.HBM)
COST = pl.CostEstimate(flops=0, bytes_accessed=1000, transcendentals=0)
PARAMS = pltpu.CompilerParams(vmem_limit_bytes=40 * 2**20)


def split3(value):
    one = value.astype(jnp.bfloat16).astype(jnp.float32)
    rest = value - one
    two = rest.astype(jnp.bfloat16).astype(jnp.float32)
    return one, two, rest - two


def gather_rows(src_ref, index_ref, dst_ref, count, unroll=16):
    def step(i, _):
        for k in range(unroll):
            at = i * unroll + k
            dst_ref[pl.ds(at, 1), :] = src_ref[pl.ds(index_ref[at], 1), :]
        return 0

    lax.fori_loop(0, count // unroll, step, 0)


def sort_kernel(order_ref, points_ref, weights_ref, out_ref, raw, tree):
    for c in range(8):
        cols = pl.ds(c * 512, 512)
        block = jnp.concatenate([points_ref[:, cols], weights_ref[:, cols]], axis=0)
        raw[pl.ds(c * 512, 512), :] = block.astype(jnp.float32).T
    gather_rows(raw, order_ref, tree, PTS)
    for leaf in range(LEAF_DEV):
        rows = tree[pl.ds(leaf * LEAF_PTS, LEAF_PTS), :]
        out_ref[leaf] = rows.T.astype(jnp.bfloat16)


def sort_leaves(order, points_t, weights_t):
    return pl.pallas_call(
        sort_kernel,
        out_shape=jax.ShapeDtypeStruct((LEAF_DEV, 2 * F, LEAF_PTS), jnp.bfloat16),
        in_specs=[SMEM, VMEM, VMEM],
        out_specs=VMEM,
        scratch_shapes=[pltpu.VMEM((PTS, 2 * F), jnp.float32), pltpu.VMEM((PTS, 2 * F), jnp.float32)],
        compiler_params=PARAMS,
        name="sort_leaves",
        cost_estimate=COST,
    )(order, points_t, weights_t)


def left_factor(rows, with_ones):
    lane = lax.broadcasted_iota(jnp.int32, rows.shape, 1)
    is_point = lane < F
    scaled = jnp.where(is_point, rows * (2 * RATE), 0.0)
    high = scaled.astype(jnp.bfloat16)
    low = scaled - high.astype(jnp.float32)
    norm = -RATE * jnp.sum(jnp.where(is_point, rows * rows, 0.0), axis=1, keepdims=True)
    one, two, three = split3(norm)
    tail = jnp.where(lane == F, one, 0.0)
    tail = jnp.where(lane == F + 1, two, tail)
    tail = jnp.where(lane == F + 2, three, tail)
    if with_ones:
        tail = jnp.where((lane > F + 2) & (lane < F + 6), 1.0, tail)
    second = jnp.where(is_point, low, tail).astype(jnp.bfloat16)
    return jnp.concatenate([high, second], axis=1)


def fill_right(right, block):
    size = block.shape[1]
    points = block[:F]
    wide = points.astype(jnp.float32)
    norm = -RATE * jnp.sum(wide * wide, axis=0, keepdims=True)
    one, two, three = split3(norm)
    row = lax.broadcasted_iota(jnp.int32, (16, size), 0)
    tail = jnp.where(row < 3, 1.0, 0.0)
    tail = jnp.where(row == 3, one, tail)
    tail = jnp.where(row == 4, two, tail)
    tail = jnp.where(row == 5, three, tail)
    right[pl.ds(0, 2 * F), :] = block
    right[pl.ds(2 * F, F), :] = points
    right[pl.ds(3 * F, 16), :] = tail.astype(jnp.bfloat16)
    right[pl.ds(3 * F + 16, F - 16), :] = jnp.zeros((F - 16, size), jnp.bfloat16)


def targets_kernel(leaves_ref, out_ref):
    for leaf in range(LEAF_DEV):
        for half in range(2):
            rows = leaves_ref[leaf, :, pl.ds(half * 512, 512)].astype(jnp.float32).T
            out_ref[pl.ds(leaf * LEAF_PTS + half * 512, 512), :] = left_factor(rows, True)


def target_factors(leaves):
    return pl.pallas_call(
        targets_kernel,
        out_shape=jax.ShapeDtypeStruct((PTS, 4 * F), jnp.bfloat16),
        in_specs=[VMEM],
        out_specs=VMEM,
        compiler_params=PARAMS,
        name="target_factors",
        cost_estimate=COST,
    )(leaves)


def skeleton(index, blocks, right, chosen, total):
    spots = lax.broadcasted_iota(jnp.int32, (SKEL, SKEL), 0).astype(jnp.float32)

    def picks(k):
        return jnp.where(spots == index - k * SKEL, 1.0, 0.0).astype(jnp.bfloat16)

    for k, block in enumerate(blocks):
        part = jnp.dot(block(), picks(k), preferred_element_type=jnp.float32)
        chosen[...] = part if k == 0 else chosen[...] + part
    left = left_factor(chosen[...].T, False)
    ones = jnp.ones((16, SKEL), jnp.bfloat16)
    nt = (((1,), (1,)), ((), ()))
    for k, block in enumerate(blocks):
        taken = lax.dot_general(ones, picks(k), nt, preferred_element_type=jnp.float32)[:1]
        rows = block()
        fill_right(right, rows)
        dense = jnp.exp2(jnp.dot(left, right[...], preferred_element_type=jnp.float32))
        factor = jnp.where(taken > 0.5, 0.0, 1.0 / jnp.sum(dense, axis=0, keepdims=True))
        spread = (dense * factor).astype(jnp.bfloat16)
        part = lax.dot_general(rows, spread, nt, preferred_element_type=jnp.float32)
        total[...] = part if k == 0 else total[...] + part
    row = lax.broadcasted_iota(jnp.int32, (2 * F, SKEL), 0)
    return (chosen[...] + jnp.where(row < F, 0.0, total[...])).astype(jnp.bfloat16)


SKELETON_SCRATCH = [
    pltpu.VMEM((4 * F, SKEL), jnp.bfloat16),
    pltpu.VMEM((2 * F, SKEL), jnp.float32),
    pltpu.VMEM((2 * F, SKEL), jnp.float32),
]


def node_kernel(index_ref, merge_ref, leaves_ref, out_ref, right, chosen, total):
    def block_at(k):
        return lambda: leaves_ref[k // 2, :, pl.ds(k % 2 * SKEL, SKEL)]

    index = index_ref[...].astype(jnp.float32)
    out_ref[pl.ds(0, 2 * F), :] = skeleton(index, [block_at(k) for k in range(2 * LEAF_DEV)], right, chosen, total)
    entry = merge_ref[...]
    high = entry // 32
    row = lax.broadcasted_iota(jnp.int32, (16, SKEL), 0)
    packed = jnp.zeros((16, SKEL), jnp.float32)
    for k, line in enumerate((high[:1], entry[:1] - 32 * high[:1], high[1:2], entry[1:2] - 32 * high[1:2])):
        packed = jnp.where(row == k, line.astype(jnp.float32), packed)
    out_ref[pl.ds(2 * F, 16), :] = packed.astype(jnp.bfloat16)


def first_node(index, merge_index, leaves):
    return pl.pallas_call(
        node_kernel,
        out_shape=jax.ShapeDtypeStruct((2 * F + 16, SKEL), jnp.bfloat16),
        in_specs=[VMEM, VMEM, VMEM],
        out_specs=VMEM,
        scratch_shapes=SKELETON_SCRATCH,
        compiler_params=PARAMS,
        name="first_node",
        cost_estimate=COST,
    )(index, merge_index, leaves)


def siblings_kernel(place_ref, nodes_ref, out_ref, pairs, right, chosen, total):
    place = place_ref[0]
    pair = place // 2
    quad = place // 4
    other_pair = pair + 1 - 2 * (pair % 2)
    other_quad = quad + 1 - 2 * (quad % 2)
    out_ref[0] = nodes_ref[place + 1 - 2 * (place % 2), pl.ds(0, 2 * F), :]

    def entries(base, level):
        lines = nodes_ref[base, pl.ds(2 * F, 16), :].astype(jnp.float32)
        return lines[2 * level : 2 * level + 1] * 32.0 + lines[2 * level + 1 : 2 * level + 2]

    def merge_pair(k, _):
        base = 2 * jnp.where(k == 0, other_pair, 2 * other_quad + k - 1)
        blocks = [lambda: nodes_ref[base, pl.ds(0, 2 * F), :], lambda: nodes_ref[base + 1, pl.ds(0, 2 * F), :]]
        pairs[k] = skeleton(entries(base, 0), blocks, right, chosen, total)
        return 0

    lax.fori_loop(0, 3, merge_pair, 0)
    out_ref[1] = pairs[0]
    out_ref[2] = skeleton(entries(4 * other_quad, 1), [lambda: pairs[1], lambda: pairs[2]], right, chosen, total)


def sibling_nodes(place, nodes):
    return pl.pallas_call(
        siblings_kernel,
        out_shape=jax.ShapeDtypeStruct((LEVELS, 2 * F, SKEL), jnp.bfloat16),
        in_specs=[SMEM, VMEM],
        out_specs=VMEM,
        scratch_shapes=[pltpu.VMEM((3, 2 * F, SKEL), jnp.bfloat16)] + SKELETON_SCRATCH,
        compiler_params=PARAMS,
        name="sibling_nodes",
        cost_estimate=COST,
    )(place, nodes)


def add_terms(target, block, left_ref, total, right):
    fill_right(right, block)
    weights = block
    base = pl.multiple_of(target * LEAF_PTS, LEAF_PTS)
    for step in range(LEAF_PTS // 256):
        rows = pl.ds(base + step * 256, 256)
        exponent = jnp.dot(left_ref[rows, :], right[...], preferred_element_type=jnp.float32)
        dense = jnp.exp2(exponent).astype(jnp.bfloat16)
        total[rows, :] += lax.dot_general(
            dense, weights, (((1,), (1,)), ((), ())), preferred_element_type=jnp.float32
        )


def far_kernel(flags_ref, left_ref, before_ref, siblings_ref, out_ref, right):
    out_ref[...] = before_ref[...]
    for level in range(LEVELS):
        block = siblings_ref[level]
        fill_right(right, block)

        def leaf_step(leaf, _):
            @pl.when(flags_ref[leaf * LEVELS + level] != 0)
            def _():
                base = pl.multiple_of(leaf * LEAF_PTS, LEAF_PTS)
                for step in range(2):
                    rows = pl.ds(base + step * 512, 512)
                    exponent = jnp.dot(left_ref[rows, :], right[...], preferred_element_type=jnp.float32)
                    dense = jnp.exp2(exponent).astype(jnp.bfloat16)
                    out_ref[rows, :] += lax.dot_general(
                        dense, block, (((1,), (1,)), ((), ())), preferred_element_type=jnp.float32
                    )
            return 0

        lax.fori_loop(0, LEAF_DEV, leaf_step, 0)


def far_terms(flags, left, before, siblings):
    return pl.pallas_call(
        far_kernel,
        out_shape=jax.ShapeDtypeStruct((PTS, 2 * F), jnp.float32),
        in_specs=[SMEM, VMEM, VMEM, VMEM],
        out_specs=VMEM,
        scratch_shapes=[pltpu.VMEM((4 * F, SKEL), jnp.bfloat16)],
        compiler_params=PARAMS,
        name="far_terms",
        cost_estimate=COST,
    )(flags, left, before, siblings)


def source_of(me, distance, other):
    core = me % 2
    chip = (me // 2 - (1 - 2 * core) * distance + 8) % 8
    return 2 * chip + (core + other) % 2


def copy_kernel(picks, me_ref, table_ref, *refs):
    inputs, out_ref, held, arrive, leave = refs[:-4], refs[-4], refs[-3], refs[-2], refs[-1]
    me = me_ref[0]
    incoming = [
        pltpu.make_async_copy(inputs[source].at[leaf_of(me, table_ref)], held.at[k], arrive.at[k])
        for k, (source, leaf_of) in enumerate(picks)
    ]
    outgoing = [pltpu.make_async_copy(held.at[k], out_ref.at[k], leave.at[k]) for k in range(len(picks))]
    for copy in incoming:
        copy.start()
    for one, two in zip(incoming, outgoing):
        one.wait()
        two.start()
    for copy in outgoing:
        copy.wait()


def copy_leaves(me, table, inputs, picks):
    size = (len(picks), 2 * F, LEAF_PTS)
    return pl.pallas_call(
        functools.partial(copy_kernel, picks),
        out_shape=jax.ShapeDtypeStruct(size, jnp.bfloat16),
        in_specs=[SMEM, SMEM] + [HBM] * len(inputs),
        out_specs=HBM,
        scratch_shapes=[
            pltpu.VMEM(size, jnp.bfloat16),
            pltpu.SemaphoreType.DMA((len(picks),)),
            pltpu.SemaphoreType.DMA((len(picks),)),
        ],
        compiler_params=PARAMS,
        name="copy_leaves",
        cost_estimate=COST,
    )(me, table, *inputs)


def asked(distance, other, to_chip, to_other):
    def leaf_of(me, table_ref):
        core = me % 2
        chip = (me // 2 + (1 - 2 * core) * to_chip + 8) % 8
        return table_ref[2 * chip + (core + to_other) % 2, 0, source_of(me, distance, other)]

    return leaf_of


def at_slot(slot):
    return lambda me, table_ref: slot


def near_kernel(items, first, last, me_ref, source_ref, target_ref, left_ref, *refs):
    refs = list(refs)
    before_ref = None if first else refs.pop(0)
    count = len(items)
    arrays, out_ref, held, arrive, right = refs[:count], refs[count], refs[count + 1], refs[count + 2], refs[count + 3]
    total = refs[count + 4] if last else out_ref
    plan = []
    for k, ((distance, other, slot), array_ref) in enumerate(zip(items, arrays)):
        peer = source_of(me_ref[0], distance, other)
        leaf = source_ref[peer] if slot is None else slot
        plan.append((target_ref[peer], pltpu.make_async_copy(array_ref.at[leaf], held.at[k], arrive.at[k])))
    for target, copy in plan:
        pl.when(target >= 0)(copy.start)
    total[...] = jnp.zeros_like(total) if first else before_ref[...]
    for k, (target, copy) in enumerate(plan):

        @pl.when(target >= 0)
        def _():
            copy.wait()
            add_terms(target, held[k], left_ref, total, right)

    if last:
        for part in range(8):
            rows = pl.ds(part * 512, 512)
            out_ref[:, rows] = total[rows, :].T[F:]


def near_terms(me, source, target, left, before, items, last=False):
    first = before is None
    plan = [item[1:] for item in items]
    count = len(items)
    scratch = [
        pltpu.VMEM((count, 2 * F, LEAF_PTS), jnp.bfloat16),
        pltpu.SemaphoreType.DMA((count,)),
        pltpu.VMEM((4 * F, LEAF_PTS), jnp.bfloat16),
    ]
    if last:
        scratch.append(pltpu.VMEM((PTS, 2 * F), jnp.float32))
    return pl.pallas_call(
        functools.partial(near_kernel, plan, first, last),
        out_shape=jax.ShapeDtypeStruct((F, PTS) if last else (PTS, 2 * F), jnp.float32),
        in_specs=[SMEM] * 3 + [VMEM] * (1 if first else 2) + [HBM] * count,
        out_specs=VMEM,
        scratch_shapes=scratch,
        compiler_params=PARAMS,
        name="near_terms",
        cost_estimate=COST,
    )(me, source, target, left, *([] if first else [before]), *[item[0] for item in items])


def partner(value, axis, stride):
    pairs = [(source, source ^ 2**stride) for source in range(lax.axis_size(axis))]
    return lax.ppermute(value, axis, pairs)


def hop(value):
    pairs = [(j, (j + 2 - 4 * (j % 2)) % 16) for j in range(16)]
    return lax.ppermute(value, "task", pairs)


def after(value, *others):
    return lax.optimization_barrier((value, *others))[0]


def body(points, weights, point_order, node_order, merge_order, far_list, task_target, task_source):
    me = lax.axis_index("task").astype(jnp.int32).reshape(1)
    source = task_source.reshape(-1)
    target = task_target.reshape(-1)
    near = functools.partial(near_terms, me, source, target)
    place = (lax.axis_index("leaf") % 8).astype(jnp.int32).reshape(1)

    leaves = sort_leaves(point_order.reshape(-1), points.T, weights.T)
    one_a = hop(leaves)
    beside = partner(leaves, "task", 0)
    row = after(jnp.broadcast_to(source, (16, 1, 16)), leaves)
    table = lax.all_to_all(row, "task", split_axis=0, concat_axis=0, tiled=True)
    left = target_factors(leaves)
    beside = after(beside, left)
    one_b = hop(beside)
    node = first_node(node_order.reshape(1, -1)[:, :SKEL], merge_order[0, 0, :, :SKEL], after(leaves, beside))
    groups = [list(range(8 * x, 8 * x + 8)) for x in range(lax.axis_size("leaf") // 8)]
    nodes = lax.all_gather(node, "leaf", axis_index_groups=groups)
    beside = after(beside, node)
    total = near(left, None, [(leaves, 0, 0, None), (beside, 0, 1, None)])

    one_a = after(one_a, total)
    two_a = hop(one_a)
    total = near(left, total, [(one_a, 1, 0, None)])
    one_b = after(one_b, total)
    two_b = hop(one_b)
    total = near(left, total, [(one_b, 1, 1, None)])
    nodes = after(nodes, total)
    siblings = sibling_nodes(place, nodes)
    total = far_terms(far_list.reshape(-1), left, total, siblings)

    two_a = after(two_a, total)
    two_b = after(two_b, two_a)
    send = copy_leaves(
        me,
        table,
        [two_a, two_b],
        [(0, asked(2, 0, 2, 0)), (1, asked(2, 1, 2, 0)), (0, asked(2, 0, 1, 0)), (1, asked(2, 1, 1, 0))],
    )
    three = hop(send)
    send = copy_leaves(me, table, [after(two_a, send), two_b], [(0, asked(2, 0, 1, 1)), (1, asked(2, 1, 1, 1))])
    three_side = hop(send)
    send = copy_leaves(
        me,
        table,
        [after(one_a, send), one_b, two_a, two_b],
        [(0, asked(1, 0, 0, 1)), (1, asked(1, 1, 0, 1)), (2, asked(2, 0, 0, 1)), (3, asked(2, 1, 0, 1))],
    )
    side = partner(send, "task", 0)
    total = near(left, total, [(after(two_a, send), 2, 0, None), (two_b, 2, 1, None)])
    side = after(side, total)
    total = near(left, total, [(side, -1, 1, 0), (side, -1, 0, 1), (side, -2, 1, 2), (side, -2, 0, 3)])
    three = after(three, total)
    send = copy_leaves(me, table, [three], [(0, at_slot(0)), (0, at_slot(1))])
    four = hop(send)
    total = near(left, total, [(after(three, send), 3, 0, 2), (three, 3, 1, 3)])
    three_side = partner(after(three_side, total), "task", 0)
    four = after(four, total)
    total = near(left, total, [(four, 4, 0, 0), (four, 4, 1, 1)])
    three_side = after(three_side, total)
    total = near(left, total, [(three_side, -3, 1, 0), (three_side, -3, 0, 1)], last=True)
    return total.T


def solution(mesh):
    return jax.shard_map(
        body,
        mesh=mesh,
        in_specs=(
            P(("leaf", "task"), None),
            P(("leaf", "task"), None),
            P("leaf", "task", None),
            P("leaf", "task", None),
            P("leaf", "task", None, None),
            P("leaf", "task", None, None),
            P("leaf", "task", None, None),
            P("leaf", "task", None, None),
        ),
        out_specs=P(("leaf", "task"), None),
        check_vma=False,
    )
```

time: 268 us -> 152 us (0.57)
  the two profiles are of different devices: /device:TPU:3 before, /device:TPU:38 now
where the time goes in v3:
time: 152 us; the launch traced here: 151 us
  Pallas kernels  61.1 us (40%)
  waiting for transfers between devices  34.7 us (23%)
  starting transfers between devices  29 us (19%)
  between operations  13.8 us (9%)
  local copies, waits for them, and re-layouts  12.8 us (8%)
    pallas_call x8, Pallas kernels, near_terms(): pl.pallas_call(functools.partial(near_kernel, plan, first, last), out_sha...  24 us
    ppermute x7, waiting for transfers between devices, hop(): return lax.ppermute(value, 'task', pairs)  19.1 us
    all_gather x1, waiting for transfers between devices, body(): nodes = lax.all_gather(node, 'leaf', axis_index_groups=groups)  15.5 us
    ppermute x7, starting transfers between devices, hop(): return lax.ppermute(value, 'task', pairs)  15.4 us
    unnamed x29, local copies, waits for them, and re-layouts  11.4 us
    pallas_call x1, Pallas kernels, far_terms(): pl.pallas_call(far_kernel, out_shape=jax.ShapeDtypeStruct((PTS, 2 * F), j...  9.34 us
    all_to_all x1, starting transfers between devices, body(): table = lax.all_to_all(row, 'task', split_axis=0, concat_axis=0, tiled=True)  7.78 us
    pallas_call x1, Pallas kernels, sibling_nodes(): pl.pallas_call(siblings_kernel, out_shape=jax.ShapeDtypeStruct((LEVELS, 2...  7.41 us
  transfers between devices with their start and end apart: 12, of which 5 were waited for; matrix products, arithmetic and copies ran while one was open for 1% of the time, Pallas kernels for 30%

profile of v3, /device:TPU:38, one launch (start us, length us, event | category | flops | bytes accessed | tf_op | source)
XLA Modules:
  0.0 151.4 jit_solution(927784366221104557)
XLA Ops:
  9.3 5.8 %sort_leaves.1.leaves_ref.refs_0_ = bf16[4,128,1024]{2,1,0:T(8,128)(2,1)S(1)} custom-call(s32[4096]{0:T(1024)S(1)} %bitcast.32, bf16[64,4096]{1,0:T(8,128)(2,1)S(1)} %bitcast.13, bf16[64,4096]{1,0:T(8,128)(2,1)S(1)} %bitcast.14), custom_call_target="tpu_custom_call" | custom-call | bytes 1000 | tf_op jit(solution)/shard_map/sort_leaves/pallas_call | solution.py:54
  15.2 2.1 %collective-permute-start = (bf16[4,128,1024]{2,1,0:T(8,128)(2,1)S(1)}, bf16[4,128,1024]{2,1,0:T(8,128)(2,1)}, u32[]{:S(2)}, u32[]{:S(2)}) collective-permute-start(bf16[4,128,1024]{2,1,0:T(8,128)(2,1)S(1)} %sort_leaves.1.leaves_ref.refs_0_), channel_id=1, source_target_pairs={{0,1},{1,0},{2,3},{3,2},{4,5},{5,4},{6,7},{7,6},{8,9},{9,8},{10,11... | collective-permute-start | bytes 3145736 | tf_op jit(solution)/shard_map/ppermute | solution.py:369
  17.2 2.6 %collective-permute-start.1 = (bf16[4,128,1024]{2,1,0:T(8,128)(2,1)S(1)}, bf16[4,128,1024]{2,1,0:T(8,128)(2,1)}, u32[]{:S(2)}, u32[]{:S(2)}) collective-permute-start(bf16[4,128,1024]{2,1,0:T(8,128)(2,1)S(1)} %sort_leaves.1.leaves_ref.refs_0_), channel_id=1, source_target_pairs={{0,2},{1,15},{2,4},{3,1},{4,6},{5,3},{6,8},{7,5},{8,10},{9,7},{10,... | collective-permute-start | bytes 3145736 | tf_op jit(solution)/shard_map/ppermute | solution.py:374
  21.4 2.6 %collective-permute-start.2 = (bf16[4,128,1024]{2,1,0:T(8,128)(2,1)}, bf16[4,128,1024]{2,1,0:T(8,128)(2,1)}, u32[]{:S(2)}, u32[]{:S(2)}) collective-permute-start(bf16[4,128,1024]{2,1,0:T(8,128)(2,1)} %collective-permute-done.refs_1_), channel_id=1, source_target_pairs={{0,2},{1,15},{2,4},{3,1},{4,6},{5,3},{6,8},{7,5},{8,10},{9,7},{10,... | collective-permute-start | bytes 3145736 | tf_op jit(solution)/shard_map/ppermute | solution.py:374
  24.7 6.7 %first_node.1 = bf16[144,512]{1,0:T(8,128)(2,1)} custom-call(s32[1,512]{1,0:T(1,128)S(1)} %slice.8.index_ref, s32[2,512]{1,0:T(2,128)S(1)} %slice_bitcast_fusion.merge_ref, bf16[4,128,1024]{2,1,0:T(8,128)(2,1)S(1)} %sort_leaves.1.leaves_ref.refs_0_), custom_call_target="tpu_custom_call" | custom-call | bytes 1000 | tf_op jit(solution)/shard_map/first_node/pallas_call | solution.py:167
  31.5 3.3 %near_terms.8.refs_0_ = f32[4096,128]{1,0:T(8,128)S(1)} custom-call(s32[1]{0:T(128)} %bitcast.me_ref, s32[16]{0:T(128)S(1)} %bitcast.15, s32[16]{0:T(128)S(1)} %bitcast.24, bf16[4096,256]{1,0:T(8,128)(2,1)S(1)} %target_factors.1.left_ref, bf16[4,128,1024]{2,1,0:T(8,128)(2,1)S(1)} %sort_leaves.1.leaves_ref.refs_0_, ...), custom_call_target="tpu_custom_call" | custom-call | bytes 1000 | tf_op jit(solution)/shard_map/near_terms/pallas_call | solution.py:355
  35.2 2.8 %near_terms.9.refs_0_ = f32[4096,128]{1,0:T(8,128)S(1)} custom-call(s32[1]{0:T(128)} %bitcast.me_ref, s32[16]{0:T(128)S(1)} %bitcast.16, s32[16]{0:T(128)S(1)} %bitcast.25, bf16[4096,256]{1,0:T(8,128)(2,1)S(1)} %target_factors.1.left_ref, f32[4096,128]{1,0:T(8,128)S(1)} %near_terms.8.refs_0_, bf16[4,128,1024]{2,1,0:T(8,128)(2,1)} %collective-permute-done.1.refs_1_.refs_0_), custom_call_target="tpu_custom_call" | custom-call | bytes 1000 | tf_op jit(solution)/shard_map/near_terms/pallas_call | solution.py:355
  39.4 1.9 %collective-permute-start.3 = (bf16[4,128,1024]{2,1,0:T(8,128)(2,1)}, bf16[4,128,1024]{2,1,0:T(8,128)(2,1)S(1)}, u32[]{:S(2)}, u32[]{:S(2)}) collective-permute-start(bf16[4,128,1024]{2,1,0:T(8,128)(2,1)} %collective-permute-done.1.refs_1_.refs_0_), channel_id=1, source_target_pairs={{0,2},{1,15},{2,4},{3,1},{4,6},{5,3},{6,8},{7,5},{8,10},{9,7},{10,... | collective-permute-start | bytes 3145736 | tf_op jit(solution)/shard_map/ppermute | solution.py:374
  41.3 5.2 %collective-permute-done.2.refs_1_ = bf16[4,128,1024]{2,1,0:T(8,128)(2,1)} collective-permute-done((bf16[4,128,1024]{2,1,0:T(8,128)(2,1)}, bf16[4,128,1024]{2,1,0:T(8,128)(2,1)}, u32[]{:S(2)}, u32[]{:S(2)}) %collective-permute-start.2) | collective-permute-done | bytes 1048608 | tf_op jit(solution)/shard_map/ppermute | solution.py:374
  46.5 1.9 %collective-permute-start.4 = (bf16[4,128,1024]{2,1,0:T(8,128)(2,1)}, bf16[4,128,1024]{2,1,0:T(8,128)(2,1)}, u32[]{:S(2)}, u32[]{:S(2)}) collective-permute-start(bf16[4,128,1024]{2,1,0:T(8,128)(2,1)} %collective-permute-done.2.refs_1_), channel_id=1, source_target_pairs={{0,2},{1,15},{2,4},{3,1},{4,6},{5,3},{6,8},{7,5},{8,10},{9,7},{10,... | collective-permute-start | bytes 3145736 | tf_op jit(solution)/shard_map/ppermute | solution.py:374
  49.0 7.8 %all-to-all-start = ((s32[16,1,16]{2,1,0:T(1,128)}), s32[16,1,16]{2,1,0:T(1,128)S(1)}, u32[]{:S(2)}, u32[]{:S(2)}) async-start(s32[16,1,16]{2,1,0:T(1,128)} %broadcast_in_dim.3), calls=%async_computation | async-start | bytes 16384 | tf_op jit(solution)/shard_map/all_to_all | solution.py:392
  57.0 1.6 %copy-done.5 = f32[4096,128]{1,0:T(8,128)S(1)} copy-done((f32[4096,128]{1,0:T(8,128)S(1)}, f32[4096,128]{1,0:T(8,128)}, u32[]{:S(2)}) %copy-start.5) | copy-done | bytes 2097176
  58.6 2.8 %near_terms.10.before_ref = f32[4096,128]{1,0:T(8,128)S(1)} custom-call(s32[1]{0:T(128)} %bitcast.me_ref, s32[16]{0:T(128)S(1)} %bitcast.18, s32[16]{0:T(128)S(1)} %bitcast.26, bf16[4096,256]{1,0:T(8,128)(2,1)S(1)} %target_factors.1.left_ref, f32[4096,128]{1,0:T(8,128)S(1)} %copy-done.5, bf16[4,128,1024]{2,1,0:T(8,128)(2,1)} %collective-permute-done.2.refs_1_), custom_call_target="tpu_custom_call" | custom-call | bytes 1000 | tf_op jit(solution)/shard_map/near_terms/pallas_call | solution.py:355
  62.7 15.5 %all-gather.3.cloned.1.call-done = bf16[1152,512]{1,0:T(8,128)(2,1)} async-done(((bf16[144,512]{1,0:T(8,128)(2,1)}), bf16[1152,512]{1,0:T(8,128)(2,1)}) %all-gather.3.cloned.1.call-update) | async-done | bytes 1179664 | tf_op jit(solution)/shard_map/all_gather | solution.py:398
  79.5 7.4 %sibling_nodes.1.siblings_ref = bf16[3,128,512]{2,1,0:T(8,128)(2,1)S(1)} custom-call(s32[1]{0:T(128)} %bitcast.8.place_ref, bf16[8,144,512]{2,1,0:T(8,128)(2,1)S(1)} %bitcast.12), custom_call_target="tpu_custom_call" | custom-call | bytes 1000 | tf_op jit(solution)/shard_map/sibling_nodes/pallas_call | solution.py:203
  86.9 1.6 %copy-done.3 = f32[4096,128]{1,0:T(8,128)S(1)} copy-done((f32[4096,128]{1,0:T(8,128)S(1)}, f32[4096,128]{1,0:T(8,128)}, u32[]{:S(2)}) %copy-start.3) | copy-done | bytes 2097176
  88.5 9.3 %far_terms.1.refs_0_ = f32[4096,128]{1,0:T(8,128)S(1)} custom-call(s32[12]{0:T(128)S(1)} %reshape.25.flags_ref, bf16[4096,256]{1,0:T(8,128)(2,1)S(1)} %target_factors.1.left_ref, f32[4096,128]{1,0:T(8,128)S(1)} %copy-done.3, bf16[3,128,512]{2,1,0:T(8,128)(2,1)S(1)} %sibling_nodes.1.siblings_ref), custom_call_target="tpu_custom_call" | custom-call | bytes 1000 | tf_op jit(solution)/shard_map/far_terms/pallas_call | solution.py:251
  99.2 1.8 %copy_leaves.4 = bf16[4,128,1024]{2,1,0:T(8,128)(2,1)S(1)} custom-call(s32[1]{0:T(128)} %bitcast.me_ref, s32[16,1,16]{2,1,0:T(1,128)S(1)} %all-to-all-done.table_ref, bf16[4,128,1024]{2,1,0:T(8,128)(2,1)S(1)} %collective-permute-done.3.refs_0_.refs_2_.refs_1_, bf16[4,128,1024]{2,1,0:T(8,128)(2,1)} %collective-permute-done.4.refs_1_.refs_3_.refs_2_), custom_call_target="tpu_custom_call" | custom-call | bytes 1000 | tf_op jit(solution)/shard_map/copy_leaves/pallas_call | solution.py:288
  101.1 1.7 %copy_leaves.5 = bf16[2,128,1024]{2,1,0:T(8,128)(2,1)S(1)} custom-call(s32[1]{0:T(128)} %bitcast.me_ref, s32[16,1,16]{2,1,0:T(1,128)S(1)} %all-to-all-done.table_ref, bf16[4,128,1024]{2,1,0:T(8,128)(2,1)S(1)} %collective-permute-done.3.refs_0_.refs_2_.refs_1_, bf16[4,128,1024]{2,1,0:T(8,128)(2,1)} %collective-permute-done.4.refs_1_.refs_3_.refs_2_), custom_call_target="tpu_custom_call" | custom-call | bytes 1000 | tf_op jit(solution)/shard_map/copy_leaves/pallas_call | solution.py:288
  102.8 1.9 %copy_leaves.6 = bf16[4,128,1024]{2,1,0:T(8,128)(2,1)S(1)} custom-call(s32[1]{0:T(128)} %bitcast.me_ref, s32[16,1,16]{2,1,0:T(1,128)S(1)} %all-to-all-done.table_ref, bf16[4,128,1024]{2,1,0:T(8,128)(2,1)} %collective-permute-done.1.refs_1_.refs_0_, bf16[4,128,1024]{2,1,0:T(8,128)(2,1)} %collective-permute-done.2.refs_1_, ...), custom_call_target="tpu_custom_call" | custom-call | bytes 1000 | tf_op jit(solution)/shard_map/copy_leaves/pallas_call | solution.py:288
  104.7 1.9 %collective-permute-start.5 = (bf16[4,128,1024]{2,1,0:T(8,128)(2,1)S(1)}, bf16[4,128,1024]{2,1,0:T(8,128)(2,1)S(1)}, u32[]{:S(2)}, u32[]{:S(2)}) collective-permute-start(bf16[4,128,1024]{2,1,0:T(8,128)(2,1)S(1)} %copy_leaves.6), channel_id=1, source_target_pairs={{0,1},{1,0},{2,3},{3,2},{4,5},{5,4},{6,7},{7,6},{8,9},{9,8},{10,11... | collective-permute-start | bytes 3145736 | tf_op jit(solution)/shard_map/ppermute | solution.py:369
  106.6 2.5 %collective-permute-start.6 = (bf16[4,128,1024]{2,1,0:T(8,128)(2,1)S(1)}, bf16[4,128,1024]{2,1,0:T(8,128)(2,1)S(1)}, u32[]{:S(2)}, u32[]{:S(2)}) collective-permute-start(bf16[4,128,1024]{2,1,0:T(8,128)(2,1)S(1)} %copy_leaves.4), channel_id=1, source_target_pairs={{0,2},{1,15},{2,4},{3,1},{4,6},{5,3},{6,8},{7,5},{8,10},{9,7},{10,... | collective-permute-start | bytes 3145736 | tf_op jit(solution)/shard_map/ppermute | solution.py:374
  109.2 1.9 %collective-permute-start.8 = (bf16[2,128,1024]{2,1,0:T(8,128)(2,1)S(1)}, bf16[2,128,1024]{2,1,0:T(8,128)(2,1)S(1)}, u32[]{:S(2)}, u32[]{:S(2)}) collective-permute-start(bf16[2,128,1024]{2,1,0:T(8,128)(2,1)S(1)} %copy_leaves.5), channel_id=1, source_target_pairs={{0,2},{1,15},{2,4},{3,1},{4,6},{5,3},{6,8},{7,5},{8,10},{9,7},{10,... | collective-permute-start | bytes 1572872 | tf_op jit(solution)/shard_map/ppermute | solution.py:374
  111.1 2.8 %near_terms.11.refs_0_ = f32[4096,128]{1,0:T(8,128)S(1)} custom-call(s32[1]{0:T(128)} %bitcast.me_ref, s32[16]{0:T(128)S(1)} %bitcast.19, s32[16]{0:T(128)S(1)} %bitcast.27, bf16[4096,256]{1,0:T(8,128)(2,1)S(1)} %target_factors.1.left_ref, f32[4096,128]{1,0:T(8,128)S(1)} %copy-done.1, ...), custom_call_target="tpu_custom_call" | custom-call | bytes 1000 | tf_op jit(solution)/shard_map/near_terms/pallas_call | solution.py:355
  113.9 2.3 %near_terms.12.refs_0_ = f32[4096,128]{1,0:T(8,128)S(1)} custom-call(s32[1]{0:T(128)} %bitcast.me_ref, s32[16]{0:T(128)S(1)} %bitcast.20, s32[16]{0:T(128)S(1)} %bitcast.28, bf16[4096,256]{1,0:T(8,128)(2,1)S(1)} %target_factors.1.left_ref, f32[4096,128]{1,0:T(8,128)S(1)} %near_terms.11.refs_0_, ...), custom_call_target="tpu_custom_call" | custom-call | bytes 1000 | tf_op jit(solution)/shard_map/near_terms/pallas_call | solution.py:355
  116.2 8.3 %collective-permute-done.6.refs_0_.refs_1_.refs_2_ = bf16[4,128,1024]{2,1,0:T(8,128)(2,1)S(1)} collective-permute-done((bf16[4,128,1024]{2,1,0:T(8,128)(2,1)S(1)}, bf16[4,128,1024]{2,1,0:T(8,128)(2,1)S(1)}, u32[]{:S(2)}, u32[]{:S(2)}) %collective-permute-start.6) | collective-permute-done | bytes 1048608 | tf_op jit(solution)/shard_map/ppermute | solution.py:374
  125.3 1.9 %collective-permute-start.7 = (bf16[2,128,1024]{2,1,0:T(8,128)(2,1)S(1)}, bf16[2,128,1024]{2,1,0:T(8,128)(2,1)S(1)}, u32[]{:S(2)}, u32[]{:S(2)}) collective-permute-start(bf16[2,128,1024]{2,1,0:T(8,128)(2,1)S(1)} %copy_leaves.7), channel_id=1, source_target_pairs={{0,2},{1,15},{2,4},{3,1},{4,6},{5,3},{6,8},{7,5},{8,10},{9,7},{10,... | collective-permute-start | bytes 1572872 | tf_op jit(solution)/shard_map/ppermute | solution.py:374
  127.3 3.3 %near_terms.13.refs_0_ = f32[4096,128]{1,0:T(8,128)S(1)} custom-call(s32[1]{0:T(128)} %bitcast.me_ref, s32[16]{0:T(128)S(1)} %bitcast.21, s32[16]{0:T(128)S(1)} %bitcast.29, bf16[4096,256]{1,0:T(8,128)(2,1)S(1)} %target_factors.1.left_ref, f32[4096,128]{1,0:T(8,128)S(1)} %near_terms.12.refs_0_, ...), custom_call_target="tpu_custom_call" | custom-call | bytes 1000 | tf_op jit(solution)/shard_map/near_terms/pallas_call | solution.py:355
  130.6 1.9 %collective-permute-start.9 = (bf16[2,128,1024]{2,1,0:T(8,128)(2,1)S(1)}, bf16[2,128,1024]{2,1,0:T(8,128)(2,1)S(1)}, u32[]{:S(2)}, u32[]{:S(2)}) collective-permute-start(bf16[2,128,1024]{2,1,0:T(8,128)(2,1)S(1)} %collective-permute-done.8), channel_id=1, source_target_pairs={{0,1},{1,0},{2,3},{3,2},{4,5},{5,4},{6,7},{7,6},{8,9},{9,8},{10,11... | collective-permute-start | bytes 1572872 | tf_op jit(solution)/shard_map/ppermute | solution.py:369
  132.5 5.1 %collective-permute-done.7.refs_1_.refs_2_ = bf16[2,128,1024]{2,1,0:T(8,128)(2,1)S(1)} collective-permute-done((bf16[2,128,1024]{2,1,0:T(8,128)(2,1)S(1)}, bf16[2,128,1024]{2,1,0:T(8,128)(2,1)S(1)}, u32[]{:S(2)}, u32[]{:S(2)}) %collective-permute-start.7) | collective-permute-done | bytes 524320 | tf_op jit(solution)/shard_map/ppermute | solution.py:374
  137.6 2.0 %near_terms.14.refs_0_ = f32[4096,128]{1,0:T(8,128)S(1)} custom-call(s32[1]{0:T(128)} %bitcast.me_ref, s32[16]{0:T(128)S(1)} %bitcast.22, s32[16]{0:T(128)S(1)} %bitcast.30, bf16[4096,256]{1,0:T(8,128)(2,1)S(1)} %target_factors.1.left_ref, f32[4096,128]{1,0:T(8,128)S(1)} %near_terms.13.refs_0_, ...), custom_call_target="tpu_custom_call" | custom-call | bytes 1000 | tf_op jit(solution)/shard_map/near_terms/pallas_call | solution.py:355
  139.6 4.9 %near_terms.15 = f32[64,4096]{1,0:T(8,128)} custom-call(s32[1]{0:T(128)} %bitcast.me_ref, s32[16]{0:T(128)S(1)} %bitcast.23, s32[16]{0:T(128)S(1)} %bitcast.31, bf16[4096,256]{1,0:T(8,128)(2,1)S(1)} %target_factors.1.left_ref, f32[4096,128]{1,0:T(8,128)S(1)} %near_terms.14.refs_0_, bf16[2,128,1024]{2,1,0:T(8,128)(2,1)S(1)} %collective-permute-done.9.refs_1_.refs_2_, ...), custom_call_target="tpu_custom_call" | custom-call | bytes 1000 | tf_op jit(solution)/shard_map/near_terms/pallas_call | solution.py:355
  (43 shorter events, 12.4 us)
Async XLA Ops:
  6.5 71.7 %all-gather.3.cloned.1.call-start = ((), (), s32[]{:S(2)}) async-start(), calls=%async_computation.1 | async-start | bytes 1327104 | tf_op jit(solution)/shard_map/all_gather | solution.py:398
  6.5 1.0 copy-start.7
  7.6 1.0 copy-start.8
  8.6 0.7 copy-start.11
  15.1 8.9 %copy-start.12 = (s32[1,1,2,1024]{3,2,1,0:T(2,128)S(1)}, s32[1,1,2,1024]{3,2,1,0:T(2,128)}, u32[]{:S(2)}) copy-start(s32[1,1,2,1024]{3,2,1,0:T(2,128)} %param.12) | copy-start | bytes 24580
  15.1 16.3 %copy-start.9 = (s32[1,1,16,1]{2,3,1,0:T(1,128)S(1)}, s32[1,1,16,1]{2,3,1,0:T(1,128)}, u32[]{:S(2)}) copy-start(s32[1,1,16,1]{2,3,1,0:T(1,128)} %param.15) | copy-start | bytes 196
  15.2 16.3 %copy-start.10 = (s32[1,1,16,1]{2,3,1,0:T(1,128)S(1)}, s32[1,1,16,1]{2,3,1,0:T(1,128)}, u32[]{:S(2)}) copy-start(s32[1,1,16,1]{2,3,1,0:T(1,128)} %param.14) | copy-start | bytes 196
  15.2 6.2 %collective-permute-start = (bf16[4,128,1024]{2,1,0:T(8,128)(2,1)S(1)}, bf16[4,128,1024]{2,1,0:T(8,128)(2,1)}, u32[]{:S(2)}, u32[]{:S(2)}) collective-permute-start(bf16[4,128,1024]{2,1,0:T(8,128)(2,1)S(1)} %sort_leaves.1.leaves_ref.refs_0_), channel_id=1, source_target_pairs={{0,1},{1,0},{2,3},{3,2},{4,5},{5,4},{6,7},{7,6},{8,9},{9,8},{10,11... | collective-permute-start | bytes 3145736 | tf_op jit(solution)/shard_map/ppermute | solution.py:369
  17.2 18.0 %collective-permute-start.1 = (bf16[4,128,1024]{2,1,0:T(8,128)(2,1)S(1)}, bf16[4,128,1024]{2,1,0:T(8,128)(2,1)}, u32[]{:S(2)}, u32[]{:S(2)}) collective-permute-start(bf16[4,128,1024]{2,1,0:T(8,128)(2,1)S(1)} %sort_leaves.1.leaves_ref.refs_0_), channel_id=1, source_target_pairs={{0,2},{1,15},{2,4},{3,1},{4,6},{5,3},{6,8},{7,5},{8,10},{9,7},{10,... | collective-permute-start | bytes 3145736 | tf_op jit(solution)/shard_map/ppermute | solution.py:374
  21.4 25.1 %collective-permute-start.2 = (bf16[4,128,1024]{2,1,0:T(8,128)(2,1)}, bf16[4,128,1024]{2,1,0:T(8,128)(2,1)}, u32[]{:S(2)}, u32[]{:S(2)}) collective-permute-start(bf16[4,128,1024]{2,1,0:T(8,128)(2,1)} %collective-permute-done.refs_1_), channel_id=1, source_target_pairs={{0,2},{1,15},{2,4},{3,1},{4,6},{5,3},{6,8},{7,5},{8,10},{9,7},{10,... | collective-permute-start | bytes 3145736 | tf_op jit(solution)/shard_map/ppermute | solution.py:374
  34.8 22.0 %copy-start.13 = (s32[1,1,4,3]{2,1,3,0:T(1,128)S(1)}, s32[1,1,4,3]{2,1,3,0:T(1,128)}, u32[]{:S(2)}) copy-start(s32[1,1,4,3]{2,1,3,0:T(1,128)} %param.13) | copy-start | bytes 148
  38.0 1.3 copy-start.4
  39.4 59.8 %collective-permute-start.3 = (bf16[4,128,1024]{2,1,0:T(8,128)(2,1)}, bf16[4,128,1024]{2,1,0:T(8,128)(2,1)S(1)}, u32[]{:S(2)}, u32[]{:S(2)}) collective-permute-start(bf16[4,128,1024]{2,1,0:T(8,128)(2,1)} %collective-permute-done.1.refs_1_.refs_0_), channel_id=1, source_target_pairs={{0,2},{1,15},{2,4},{3,1},{4,6},{5,3},{6,8},{7,5},{8,10},{9,7},{10,... | collective-permute-start | bytes 3145736 | tf_op jit(solution)/shard_map/ppermute | solution.py:374
  46.5 52.7 %collective-permute-start.4 = (bf16[4,128,1024]{2,1,0:T(8,128)(2,1)}, bf16[4,128,1024]{2,1,0:T(8,128)(2,1)}, u32[]{:S(2)}, u32[]{:S(2)}) collective-permute-start(bf16[4,128,1024]{2,1,0:T(8,128)(2,1)} %collective-permute-done.2.refs_1_), channel_id=1, source_target_pairs={{0,2},{1,15},{2,4},{3,1},{4,6},{5,3},{6,8},{7,5},{8,10},{9,7},{10,... | collective-permute-start | bytes 3145736 | tf_op jit(solution)/shard_map/ppermute | solution.py:374
  49.0 50.2 %all-to-all-start = ((s32[16,1,16]{2,1,0:T(1,128)}), s32[16,1,16]{2,1,0:T(1,128)S(1)}, u32[]{:S(2)}, u32[]{:S(2)}) async-start(s32[16,1,16]{2,1,0:T(1,128)} %broadcast_in_dim.3), calls=%async_computation | async-start | bytes 16384 | tf_op jit(solution)/shard_map/all_to_all | solution.py:392
  57.0 1.6 %copy-start.5 = (f32[4096,128]{1,0:T(8,128)S(1)}, f32[4096,128]{1,0:T(8,128)}, u32[]{:S(2)}) copy-start(f32[4096,128]{1,0:T(8,128)} %copy-done.4) | copy-start | bytes 6291460
  61.3 1.3 copy-start.2
  78.2 1.3 copy-start.6
  86.9 1.6 %copy-start.3 = (f32[4096,128]{1,0:T(8,128)S(1)}, f32[4096,128]{1,0:T(8,128)}, u32[]{:S(2)}) copy-start(f32[4096,128]{1,0:T(8,128)} %copy-done.2) | copy-start | bytes 6291460
  97.9 1.3 copy-start
  102.8 8.3 %copy-start.1 = (f32[4096,128]{1,0:T(8,128)S(1)}, f32[4096,128]{1,0:T(8,128)}, u32[]{:S(2)}) copy-start(f32[4096,128]{1,0:T(8,128)} %copy-done) | copy-start | bytes 6291460
  104.7 9.2 %collective-permute-start.5 = (bf16[4,128,1024]{2,1,0:T(8,128)(2,1)S(1)}, bf16[4,128,1024]{2,1,0:T(8,128)(2,1)S(1)}, u32[]{:S(2)}, u32[]{:S(2)}) collective-permute-start(bf16[4,128,1024]{2,1,0:T(8,128)(2,1)S(1)} %copy_leaves.6), channel_id=1, source_target_pairs={{0,1},{1,0},{2,3},{3,2},{4,5},{5,4},{6,7},{7,6},{8,9},{9,8},{10,11... | collective-permute-start | bytes 3145736 | tf_op jit(solution)/shard_map/ppermute | solution.py:369
  106.6 17.9 %collective-permute-start.6 = (bf16[4,128,1024]{2,1,0:T(8,128)(2,1)S(1)}, bf16[4,128,1024]{2,1,0:T(8,128)(2,1)S(1)}, u32[]{:S(2)}, u32[]{:S(2)}) collective-permute-start(bf16[4,128,1024]{2,1,0:T(8,128)(2,1)S(1)} %copy_leaves.4), channel_id=1, source_target_pairs={{0,2},{1,15},{2,4},{3,1},{4,6},{5,3},{6,8},{7,5},{8,10},{9,7},{10,... | collective-permute-start | bytes 3145736 | tf_op jit(solution)/shard_map/ppermute | solution.py:374
  109.2 21.4 %collective-permute-start.8 = (bf16[2,128,1024]{2,1,0:T(8,128)(2,1)S(1)}, bf16[2,128,1024]{2,1,0:T(8,128)(2,1)S(1)}, u32[]{:S(2)}, u32[]{:S(2)}) collective-permute-start(bf16[2,128,1024]{2,1,0:T(8,128)(2,1)S(1)} %copy_leaves.5), channel_id=1, source_target_pairs={{0,2},{1,15},{2,4},{3,1},{4,6},{5,3},{6,8},{7,5},{8,10},{9,7},{10,... | collective-permute-start | bytes 1572872 | tf_op jit(solution)/shard_map/ppermute | solution.py:374
  125.3 12.3 %collective-permute-start.7 = (bf16[2,128,1024]{2,1,0:T(8,128)(2,1)S(1)}, bf16[2,128,1024]{2,1,0:T(8,128)(2,1)S(1)}, u32[]{:S(2)}, u32[]{:S(2)}) collective-permute-start(bf16[2,128,1024]{2,1,0:T(8,128)(2,1)S(1)} %copy_leaves.7), channel_id=1, source_target_pairs={{0,2},{1,15},{2,4},{3,1},{4,6},{5,3},{6,8},{7,5},{8,10},{9,7},{10,... | collective-permute-start | bytes 1572872 | tf_op jit(solution)/shard_map/ppermute | solution.py:374
  130.6 9.1 %collective-permute-start.9 = (bf16[2,128,1024]{2,1,0:T(8,128)(2,1)S(1)}, bf16[2,128,1024]{2,1,0:T(8,128)(2,1)S(1)}, u32[]{:S(2)}, u32[]{:S(2)}) collective-permute-start(bf16[2,128,1024]{2,1,0:T(8,128)(2,1)S(1)} %collective-permute-done.8), channel_id=1, source_target_pairs={{0,1},{1,0},{2,3},{3,2},{4,5},{5,4},{6,7},{7,6},{8,9},{9,8},{10,11... | collective-permute-start | bytes 1572872 | tf_op jit(solution)/shard_map/ppermute | solution.py:369
Sparse Core Ops, SparseCore 0:
  31.6 46.6 all-gather.2

commit v4 on v3

--- a/solution.py
+++ b/solution.py
@@ -19,7 +19,7 @@
 SMEM = pl.BlockSpec(memory_space=pltpu.SMEM)
 HBM = pl.BlockSpec(memory_space=pltpu.HBM)
 COST = pl.CostEstimate(flops=0, bytes_accessed=1000, transcendentals=0)
-PARAMS = pltpu.CompilerParams(vmem_limit_bytes=40 * 2**20)
+PARAMS = pltpu.CompilerParams(vmem_limit_bytes=20 * 2**20)
 
 
 def split3(value):
@@ -267,13 +267,14 @@
 
 
 def copy_kernel(picks, me_ref, table_ref, *refs):
-    inputs, out_ref, held, arrive, leave = refs[:-4], refs[-4], refs[-3], refs[-2], refs[-1]
+    inputs, outputs = refs[: -3 - len(picks)], refs[-3 - len(picks) : -3]
+    held, arrive, leave = refs[-3:]
     me = me_ref[0]
-    incoming = [
-        pltpu.make_async_copy(inputs[source].at[leaf_of(me, table_ref)], held.at[k], arrive.at[k])
-        for k, (source, leaf_of) in enumerate(picks)
-    ]
-    outgoing = [pltpu.make_async_copy(held.at[k], out_ref.at[k], leave.at[k]) for k in range(len(picks))]
+    rows = [(out_ref, k, *pick) for out_ref, out in zip(outputs, picks) for k, pick in enumerate(out)]
+    incoming, outgoing = [], []
+    for at, (out_ref, k, source, leaf_of) in enumerate(rows):
+        incoming.append(pltpu.make_async_copy(inputs[source].at[leaf_of(me, table_ref)], held.at[at], arrive.at[at]))
+        outgoing.append(pltpu.make_async_copy(held.at[at], out_ref.at[k], leave.at[at]))
     for copy in incoming:
         copy.start()
     for one, two in zip(incoming, outgoing):
@@ -284,16 +285,17 @@
 
 
 def copy_leaves(me, table, inputs, picks):
-    size = (len(picks), 2 * F, LEAF_PTS)
+    size = (2 * F, LEAF_PTS)
+    count = sum(len(rows) for rows in picks)
     return pl.pallas_call(
         functools.partial(copy_kernel, picks),
-        out_shape=jax.ShapeDtypeStruct(size, jnp.bfloat16),
+        out_shape=[jax.ShapeDtypeStruct((len(rows),) + size, jnp.bfloat16) for rows in picks],
         in_specs=[SMEM, SMEM] + [HBM] * len(inputs),
-        out_specs=HBM,
+        out_specs=[HBM] * len(picks),
         scratch_shapes=[
-            pltpu.VMEM(size, jnp.bfloat16),
-            pltpu.SemaphoreType.DMA((len(picks),)),
-            pltpu.SemaphoreType.DMA((len(picks),)),
+            pltpu.VMEM((count,) + size, jnp.bfloat16),
+            pltpu.SemaphoreType.DMA((count,)),
+            pltpu.SemaphoreType.DMA((count,)),
         ],
         compiler_params=PARAMS,
         name="copy_leaves",
@@ -401,44 +403,57 @@
 
     one_a = after(one_a, total)
     two_a = hop(one_a)
-    total = near(left, total, [(one_a, 1, 0, None)])
-    one_b = after(one_b, total)
+    one_b = after(one_b, one_a)
     two_b = hop(one_b)
-    total = near(left, total, [(one_b, 1, 1, None)])
+    total = near(left, total, [(one_a, 1, 0, None), (one_b, 1, 1, None)])
+    two_a = after(two_a, total)
+    send, send_side = copy_leaves(
+        me,
+        table,
+        [one_a, one_b, two_a],
+        [
+            [(2, asked(2, 0, 1, 0)), (2, asked(2, 0, 1, 1)), (2, asked(2, 0, 2, 0))],
+            [(0, asked(1, 0, 0, 1)), (1, asked(1, 1, 0, 1)), (2, asked(2, 0, 0, 1))],
+        ],
+    )
+    three_a = hop(send)
+    side = partner(send_side, "task", 0)
+    two_b = after(two_b, send)
+    [send] = copy_leaves(
+        me, table, [two_b], [[(0, asked(2, 1, 1, 0)), (0, asked(2, 1, 1, 1)), (0, asked(2, 1, 2, 0))]]
+    )
+    three_b = hop(send)
+    total = near(left, total, [(two_a, 2, 0, None), (after(two_b, send), 2, 1, None)])
     nodes = after(nodes, total)
     siblings = sibling_nodes(place, nodes)
-    total = far_terms(far_list.reshape(-1), left, total, siblings)
-
-    two_a = after(two_a, total)
-    two_b = after(two_b, two_a)
-    send = copy_leaves(
+    total = after(total, siblings)
+    side = after(side, siblings)
+    total = near(left, total, [(side, -1, 1, 0), (side, -1, 0, 1), (side, -2, 1, 2)])
+    three_a = after(three_a, total)
+    send, send_side = copy_leaves(
         me,
         table,
-        [two_a, two_b],
-        [(0, asked(2, 0, 2, 0)), (1, asked(2, 1, 2, 0)), (0, asked(2, 0, 1, 0)), (1, asked(2, 1, 1, 0))],
+        [two_b, three_a, three_b],
+        [[(1, at_slot(2)), (2, at_slot(2))], [(0, asked(2, 1, 0, 1)), (1, at_slot(1)), (2, at_slot(1))]],
     )
-    three = hop(send)
-    send = copy_leaves(me, table, [after(two_a, send), two_b], [(0, asked(2, 0, 1, 1)), (1, asked(2, 1, 1, 1))])
-    three_side = hop(send)
-    send = copy_leaves(
-        me,
-        table,
-        [after(one_a, send), one_b, two_a, two_b],
-        [(0, asked(1, 0, 0, 1)), (1, asked(1, 1, 0, 1)), (2, asked(2, 0, 0, 1)), (3, asked(2, 1, 0, 1))],
+    four = hop(send)
+    side = partner(send_side, "task", 0)
+    total = far_terms(far_list.reshape(-1), left, after(total, send), siblings)
+    side = after(side, total)
+    total = near(
+        left,
+        total,
+        [
+            (three_a, 3, 0, 0),
+            (three_b, 3, 1, 0),
+            (side, -2, 0, 0),
+            (side, -3, 1, 1),
+            (side, -3, 0, 2),
+            (after(four, side), 4, 0, 0),
+            (four, 4, 1, 1),
+        ],
+        last=True,
     )
-    side = partner(send, "task", 0)
-    total = near(left, total, [(after(two_a, send), 2, 0, None), (two_b, 2, 1, None)])
-    side = after(side, total)
-    total = near(left, total, [(side, -1, 1, 0), (side, -1, 0, 1), (side, -2, 1, 2), (side, -2, 0, 3)])
-    three = after(three, total)
-    send = copy_leaves(me, table, [three], [(0, at_slot(0)), (0, at_slot(1))])
-    four = hop(send)
-    total = near(left, total, [(after(three, send), 3, 0, 2), (three, 3, 1, 3)])
-    three_side = partner(after(three_side, total), "task", 0)
-    four = after(four, total)
-    total = near(left, total, [(four, 4, 0, 0), (four, 4, 1, 1)])
-    three_side = after(three_side, total)
-    total = near(left, total, [(three_side, -3, 1, 0), (three_side, -3, 0, 1)], last=True)
     return total.T
 
 

time: 152 us -> 149 us (0.980)
  the two profiles are of different devices: /device:TPU:38 before, /device:TPU:387 now
where the time goes in v4:
time: 149 us; the launch traced here: 148 us
  Pallas kernels  62.6 us (42%)
  starting transfers between devices  40.1 us (27%)
  local copies, waits for them, and re-layouts  19 us (13%)
  between operations  13.7 us (9%)
  waiting for transfers between devices  12.5 us (8%)
    ppermute x7, starting transfers between devices, hop(): return lax.ppermute(value, 'task', pairs)  27.1 us
    pallas_call x5, Pallas kernels, near_terms(): pl.pallas_call(functools.partial(near_kernel, plan, first, last), out_sha...  24.9 us
    unnamed x37, local copies, waits for them, and re-layouts  17.7 us
    all_to_all x1, waiting for transfers between devices, body(): table = lax.all_to_all(row, 'task', split_axis=0, concat_axis=0, tiled=True)  9.04 us
    pallas_call x1, Pallas kernels, far_terms(): pl.pallas_call(far_kernel, out_shape=jax.ShapeDtypeStruct((PTS, 2 * F), j...  8.63 us
    pallas_call x3, Pallas kernels, copy_leaves(): pl.pallas_call(functools.partial(copy_kernel, picks), out_shape=[jax.Shap...  7.57 us
    ppermute x3, starting transfers between devices, partner(): return lax.ppermute(value, axis, pairs)  7.38 us
    pallas_call x1, Pallas kernels, sibling_nodes(): pl.pallas_call(siblings_kernel, out_shape=jax.ShapeDtypeStruct((LEVELS, 2...  7.37 us
  transfers between devices with their start and end apart: 12, of which 2 were waited for; matrix products, arithmetic and copies ran while one was open for 1% of the time, Pallas kernels for 28%

profile of v4, /device:TPU:387, one launch (start us, length us, event | category | flops | bytes accessed | tf_op | source)
XLA Modules:
  0.0 147.9 jit_solution(7428281903970052892)
XLA Ops:
  9.3 5.8 %sort_leaves.1.leaves_ref.refs_0_ = bf16[4,128,1024]{2,1,0:T(8,128)(2,1)S(1)} custom-call(s32[4096]{0:T(1024)S(1)} %bitcast.21, bf16[64,4096]{1,0:T(8,128)(2,1)S(1)} %bitcast.13, bf16[64,4096]{1,0:T(8,128)(2,1)S(1)} %bitcast.14), custom_call_target="tpu_custom_call" | custom-call | bytes 1000 | tf_op jit(solution)/shard_map/sort_leaves/pallas_call | solution.py:54
  15.2 2.7 %collective-permute-start = (bf16[4,128,1024]{2,1,0:T(8,128)(2,1)S(1)}, bf16[4,128,1024]{2,1,0:T(8,128)(2,1)}, u32[]{:S(2)}, u32[]{:S(2)}) collective-permute-start(bf16[4,128,1024]{2,1,0:T(8,128)(2,1)S(1)} %sort_leaves.1.leaves_ref.refs_0_), channel_id=1, source_target_pairs={{0,1},{1,0},{2,3},{3,2},{4,5},{5,4},{6,7},{7,6},{8,9},{9,8},{10,11... | collective-permute-start | bytes 3145736 | tf_op jit(solution)/shard_map/ppermute | solution.py:371
  17.9 5.1 %collective-permute-start.1 = (bf16[4,128,1024]{2,1,0:T(8,128)(2,1)S(1)}, bf16[4,128,1024]{2,1,0:T(8,128)(2,1)}, u32[]{:S(2)}, u32[]{:S(2)}) collective-permute-start(bf16[4,128,1024]{2,1,0:T(8,128)(2,1)S(1)} %sort_leaves.1.leaves_ref.refs_0_), channel_id=1, source_target_pairs={{0,2},{1,15},{2,4},{3,1},{4,6},{5,3},{6,8},{7,5},{8,10},{9,7},{10,... | collective-permute-start | bytes 3145736 | tf_op jit(solution)/shard_map/ppermute | solution.py:376
  23.0 1.6 %target_factors.1.left_ref = bf16[4096,256]{1,0:T(8,128)(2,1)S(1)} custom-call(bf16[4,128,1024]{2,1,0:T(8,128)(2,1)S(1)} %sort_leaves.1.leaves_ref.refs_0_), custom_call_target="tpu_custom_call" | custom-call | bytes 1000 | tf_op jit(solution)/shard_map/target_factors/pallas_call | solution.py:108
  24.6 3.0 %collective-permute-start.2 = (bf16[4,128,1024]{2,1,0:T(8,128)(2,1)}, bf16[4,128,1024]{2,1,0:T(8,128)(2,1)}, u32[]{:S(2)}, u32[]{:S(2)}) collective-permute-start(bf16[4,128,1024]{2,1,0:T(8,128)(2,1)} %collective-permute-done.refs_1_), channel_id=1, source_target_pairs={{0,2},{1,15},{2,4},{3,1},{4,6},{5,3},{6,8},{7,5},{8,10},{9,7},{10,... | collective-permute-start | bytes 3145736 | tf_op jit(solution)/shard_map/ppermute | solution.py:376
  28.3 6.7 %first_node.1 = bf16[144,512]{1,0:T(8,128)(2,1)} custom-call(s32[1,512]{1,0:T(1,128)S(1)} %slice.8.index_ref, s32[2,512]{1,0:T(2,128)S(1)} %slice_bitcast_fusion.merge_ref, bf16[4,128,1024]{2,1,0:T(8,128)(2,1)S(1)} %sort_leaves.1.leaves_ref.refs_0_), custom_call_target="tpu_custom_call" | custom-call | bytes 1000 | tf_op jit(solution)/shard_map/first_node/pallas_call | solution.py:167
  35.0 2.0 %near_terms.5.refs_0_ = f32[4096,128]{1,0:T(8,128)S(1)} custom-call(s32[1]{0:T(128)} %bitcast.me_ref, s32[16]{0:T(128)S(1)} %bitcast.15, s32[16]{0:T(128)S(1)} %bitcast.22, bf16[4096,256]{1,0:T(8,128)(2,1)S(1)} %target_factors.1.left_ref, bf16[4,128,1024]{2,1,0:T(8,128)(2,1)S(1)} %sort_leaves.1.leaves_ref.refs_0_, ...), custom_call_target="tpu_custom_call" | custom-call | bytes 1000 | tf_op jit(solution)/shard_map/near_terms/pallas_call | solution.py:357
  37.0 1.4 copy-done.6
  38.4 4.2 %collective-permute-start.3 = (bf16[4,128,1024]{2,1,0:T(8,128)(2,1)}, bf16[4,128,1024]{2,1,0:T(8,128)(2,1)}, u32[]{:S(2)}, u32[]{:S(2)}) collective-permute-start(bf16[4,128,1024]{2,1,0:T(8,128)(2,1)} %collective-permute-done.1.refs_1_.refs_0_), channel_id=1, source_target_pairs={{0,2},{1,15},{2,4},{3,1},{4,6},{5,3},{6,8},{7,5},{8,10},{9,7},{10,... | collective-permute-start | bytes 3145736 | tf_op jit(solution)/shard_map/ppermute | solution.py:376
  42.7 3.4 %collective-permute-done.2.refs_2_.refs_1_ = bf16[4,128,1024]{2,1,0:T(8,128)(2,1)} collective-permute-done((bf16[4,128,1024]{2,1,0:T(8,128)(2,1)}, bf16[4,128,1024]{2,1,0:T(8,128)(2,1)}, u32[]{:S(2)}, u32[]{:S(2)}) %collective-permute-start.2) | collective-permute-done | bytes 1048608 | tf_op jit(solution)/shard_map/ppermute | solution.py:376
  46.1 5.0 %collective-permute-start.4 = (bf16[4,128,1024]{2,1,0:T(8,128)(2,1)}, bf16[4,128,1024]{2,1,0:T(8,128)(2,1)S(1)}, u32[]{:S(2)}, u32[]{:S(2)}) collective-permute-start(bf16[4,128,1024]{2,1,0:T(8,128)(2,1)} %collective-permute-done.2.refs_2_.refs_1_), channel_id=1, source_target_pairs={{0,2},{1,15},{2,4},{3,1},{4,6},{5,3},{6,8},{7,5},{8,10},{9,7},{10,... | collective-permute-start | bytes 3145736 | tf_op jit(solution)/shard_map/ppermute | solution.py:376
  51.7 5.6 %all-to-all-start = ((s32[16,1,16]{2,1,0:T(1,128)}), s32[16,1,16]{2,1,0:T(1,128)S(1)}, u32[]{:S(2)}, u32[]{:S(2)}) async-start(s32[16,1,16]{2,1,0:T(1,128)} %broadcast_in_dim.3), calls=%async_computation | async-start | bytes 16384 | tf_op jit(solution)/shard_map/all_to_all | solution.py:394
  57.3 1.6 %copy-done.7 = f32[4096,128]{1,0:T(8,128)S(1)} copy-done((f32[4096,128]{1,0:T(8,128)S(1)}, f32[4096,128]{1,0:T(8,128)}, u32[]{:S(2)}) %copy-start.7) | copy-done | bytes 2097176
  58.9 2.8 %near_terms.6.refs_0_ = f32[4096,128]{1,0:T(8,128)S(1)} custom-call(s32[1]{0:T(128)} %bitcast.me_ref, s32[16]{0:T(128)S(1)} %bitcast.17, s32[16]{0:T(128)S(1)} %bitcast.23, bf16[4096,256]{1,0:T(8,128)(2,1)S(1)} %target_factors.1.left_ref, f32[4096,128]{1,0:T(8,128)S(1)} %copy-done.7, bf16[4,128,1024]{2,1,0:T(8,128)(2,1)} %collective-permute-done.1.refs_1_.refs_0_, ...), custom_call_target="tpu_custom_call" | custom-call | bytes 1000 | tf_op jit(solution)/shard_map/near_terms/pallas_call | solution.py:357
  61.8 1.4 copy-done
  63.1 9.0 %all-to-all-done.table_ref = s32[16,1,16]{2,1,0:T(1,128)S(1)} async-done(((s32[16,1,16]{2,1,0:T(1,128)}), s32[16,1,16]{2,1,0:T(1,128)S(1)}, u32[]{:S(2)}, u32[]{:S(2)}) %all-to-all-start) | async-done | bytes 1056 | tf_op jit(solution)/shard_map/all_to_all | solution.py:394
  72.2 3.1 %copy_leaves.3 = (bf16[3,128,1024]{2,1,0:T(8,128)(2,1)}, bf16[3,128,1024]{2,1,0:T(8,128)(2,1)}) custom-call(s32[1]{0:T(128)} %bitcast.me_ref, s32[16,1,16]{2,1,0:T(1,128)S(1)} %all-to-all-done.table_ref, bf16[4,128,1024]{2,1,0:T(8,128)(2,1)} %collective-permute-done.1.refs_1_.refs_0_, bf16[4,128,1024]{2,1,0:T(8,128)(2,1)} %collective-permute-done.2.refs_2_.refs_1_, ...), custom_call_target="tpu_custom_call" | custom-call | bytes 1000 | tf_op jit(solution)/shard_map/copy_leaves/pallas_call | solution.py:290
  75.3 2.7 %collective-permute-start.5 = (bf16[3,128,1024]{2,1,0:T(8,128)(2,1)}, bf16[3,128,1024]{2,1,0:T(8,128)(2,1)}, u32[]{:S(2)}, u32[]{:S(2)}) collective-permute-start(bf16[3,128,1024]{2,1,0:T(8,128)(2,1)} %get-tuple-element.37), channel_id=1, source_target_pairs={{0,1},{1,0},{2,3},{3,2},{4,5},{5,4},{6,7},{7,6},{8,9},{9,8},{10,11... | collective-permute-start | bytes 2359304 | tf_op jit(solution)/shard_map/ppermute | solution.py:371
  78.0 2.2 %collective-permute-start.6 = (bf16[3,128,1024]{2,1,0:T(8,128)(2,1)}, bf16[3,128,1024]{2,1,0:T(8,128)(2,1)}, u32[]{:S(2)}, u32[]{:S(2)}) collective-permute-start(bf16[3,128,1024]{2,1,0:T(8,128)(2,1)} %get-tuple-element.32), channel_id=1, source_target_pairs={{0,2},{1,15},{2,4},{3,1},{4,6},{5,3},{6,8},{7,5},{8,10},{9,7},{10,... | collective-permute-start | bytes 2359304 | tf_op jit(solution)/shard_map/ppermute | solution.py:376
  80.3 1.7 %copy_leaves.4 = bf16[3,128,1024]{2,1,0:T(8,128)(2,1)} custom-call(s32[1]{0:T(128)} %bitcast.me_ref, s32[16,1,16]{2,1,0:T(1,128)S(1)} %all-to-all-done.table_ref, bf16[4,128,1024]{2,1,0:T(8,128)(2,1)S(1)} %collective-permute-done.4.refs_0_.refs_2_), custom_call_target="tpu_custom_call" | custom-call | bytes 1000 | tf_op jit(solution)/shard_map/copy_leaves/pallas_call | solution.py:290
  82.0 3.8 %collective-permute-start.7 = (bf16[3,128,1024]{2,1,0:T(8,128)(2,1)}, bf16[3,128,1024]{2,1,0:T(8,128)(2,1)}, u32[]{:S(2)}, u32[]{:S(2)}) collective-permute-start(bf16[3,128,1024]{2,1,0:T(8,128)(2,1)} %copy_leaves.4), channel_id=1, source_target_pairs={{0,2},{1,15},{2,4},{3,1},{4,6},{5,3},{6,8},{7,5},{8,10},{9,7},{10,... | collective-permute-start | bytes 2359304 | tf_op jit(solution)/shard_map/ppermute | solution.py:376
  85.8 1.6 %copy-done.1 = f32[4096,128]{1,0:T(8,128)S(1)} copy-done((f32[4096,128]{1,0:T(8,128)S(1)}, f32[4096,128]{1,0:T(8,128)}, u32[]{:S(2)}) %copy-start.1) | copy-done | bytes 2097176
  87.4 4.1 %near_terms.7.refs_0_ = f32[4096,128]{1,0:T(8,128)S(1)} custom-call(s32[1]{0:T(128)} %bitcast.me_ref, s32[16]{0:T(128)S(1)} %bitcast.18, s32[16]{0:T(128)S(1)} %bitcast.24, bf16[4096,256]{1,0:T(8,128)(2,1)S(1)} %target_factors.1.left_ref, f32[4096,128]{1,0:T(8,128)S(1)} %copy-done.1, bf16[4,128,1024]{2,1,0:T(8,128)(2,1)} %collective-permute-done.3.refs_2_.refs_1_, ...), custom_call_target="tpu_custom_call" | custom-call | bytes 1000 | tf_op jit(solution)/shard_map/near_terms/pallas_call | solution.py:357
  94.1 7.4 %sibling_nodes.1.siblings_ref = bf16[3,128,512]{2,1,0:T(8,128)(2,1)S(1)} custom-call(s32[1]{0:T(128)} %bitcast.8.place_ref, bf16[8,144,512]{2,1,0:T(8,128)(2,1)S(1)} %bitcast.12), custom_call_target="tpu_custom_call" | custom-call | bytes 1000 | tf_op jit(solution)/shard_map/sibling_nodes/pallas_call | solution.py:203
  102.2 1.6 %copy-done.3 = f32[4096,128]{1,0:T(8,128)S(1)} copy-done((f32[4096,128]{1,0:T(8,128)S(1)}, f32[4096,128]{1,0:T(8,128)}, u32[]{:S(2)}) %copy-start.3) | copy-done | bytes 2097176
  103.8 4.1 %near_terms.8.before_ref = f32[4096,128]{1,0:T(8,128)S(1)} custom-call(s32[1]{0:T(128)} %bitcast.me_ref, s32[16]{0:T(128)S(1)} %bitcast.19, s32[16]{0:T(128)S(1)} %bitcast.25, bf16[4096,256]{1,0:T(8,128)(2,1)S(1)} %target_factors.1.left_ref, f32[4096,128]{1,0:T(8,128)S(1)} %copy-done.3, bf16[3,128,1024]{2,1,0:T(8,128)(2,1)} %collective-permute-done.5.refs_1_.refs_2_.refs_3_, ...), custom_call_target="tpu_custom_call" | custom-call | bytes 1000 | tf_op jit(solution)/shard_map/near_terms/pallas_call | solution.py:357
  109.2 2.8 %copy_leaves.5 = (bf16[2,128,1024]{2,1,0:T(8,128)(2,1)}, bf16[3,128,1024]{2,1,0:T(8,128)(2,1)}) custom-call(s32[1]{0:T(128)} %bitcast.me_ref, s32[16,1,16]{2,1,0:T(1,128)S(1)} %all-to-all-done.table_ref, bf16[4,128,1024]{2,1,0:T(8,128)(2,1)S(1)} %collective-permute-done.4.refs_0_.refs_2_, bf16[3,128,1024]{2,1,0:T(8,128)(2,1)} %collective-permute-done.6.refs_1_, ...), custom_call_target="tpu_custom_call" | custom-call | bytes 1000 | tf_op jit(solution)/shard_map/copy_leaves/pallas_call | solution.py:290
  111.9 1.9 %collective-permute-start.8 = (bf16[3,128,1024]{2,1,0:T(8,128)(2,1)}, bf16[3,128,1024]{2,1,0:T(8,128)(2,1)S(1)}, u32[]{:S(2)}, u32[]{:S(2)}) collective-permute-start(bf16[3,128,1024]{2,1,0:T(8,128)(2,1)} %get-tuple-element.42), channel_id=1, source_target_pairs={{0,1},{1,0},{2,3},{3,2},{4,5},{5,4},{6,7},{7,6},{8,9},{9,8},{10,11... | collective-permute-start | bytes 2359304 | tf_op jit(solution)/shard_map/ppermute | solution.py:371
  113.9 3.8 %collective-permute-start.9 = (bf16[2,128,1024]{2,1,0:T(8,128)(2,1)}, bf16[2,128,1024]{2,1,0:T(8,128)(2,1)S(1)}, u32[]{:S(2)}, u32[]{:S(2)}) collective-permute-start(bf16[2,128,1024]{2,1,0:T(8,128)(2,1)} %get-tuple-element.40), channel_id=1, source_target_pairs={{0,2},{1,15},{2,4},{3,1},{4,6},{5,3},{6,8},{7,5},{8,10},{9,7},{10,... | collective-permute-start | bytes 1572872 | tf_op jit(solution)/shard_map/ppermute | solution.py:376
  117.8 1.6 %copy-done.5 = f32[4096,128]{1,0:T(8,128)S(1)} copy-done((f32[4096,128]{1,0:T(8,128)S(1)}, f32[4096,128]{1,0:T(8,128)}, u32[]{:S(2)}) %copy-start.5) | copy-done | bytes 2097176
  120.4 8.6 %far_terms.1.refs_0_ = f32[4096,128]{1,0:T(8,128)S(1)} custom-call(s32[12]{0:T(128)S(1)} %reshape.25.flags_ref, bf16[4096,256]{1,0:T(8,128)(2,1)S(1)} %target_factors.1.left_ref, f32[4096,128]{1,0:T(8,128)S(1)} %copy-done.5, bf16[3,128,512]{2,1,0:T(8,128)(2,1)S(1)} %copy-done.9), custom_call_target="tpu_custom_call" | custom-call | bytes 1000 | tf_op jit(solution)/shard_map/far_terms/pallas_call | solution.py:251
  129.1 12.0 %near_terms.9 = f32[64,4096]{1,0:T(8,128)} custom-call(s32[1]{0:T(128)} %bitcast.me_ref, s32[16]{0:T(128)S(1)} %bitcast.20, s32[16]{0:T(128)S(1)} %bitcast.26, bf16[4096,256]{1,0:T(8,128)(2,1)S(1)} %target_factors.1.left_ref, f32[4096,128]{1,0:T(8,128)S(1)} %far_terms.1.refs_0_, bf16[3,128,1024]{2,1,0:T(8,128)(2,1)} %collective-permute-done.6.refs_1_, ...), custom_call_target="tpu_custom_call" | custom-call | bytes 1000 | tf_op jit(solution)/shard_map/near_terms/pallas_call | solution.py:357
  (47 shorter events, 9.9 us)
Async XLA Ops:
  6.5 86.3 %all-gather.3.cloned.1.call-start = ((), (), s32[]{:S(2)}) async-start(), calls=%async_computation.1 | async-start | bytes 1327104 | tf_op jit(solution)/shard_map/all_gather | solution.py:400
  6.5 1.0 copy-start.11
  7.6 1.0 copy-start.12
  8.6 0.7 copy-start.14
  15.1 13.1 %copy-start.16 = (s32[1,1,2,1024]{3,2,1,0:T(2,128)S(1)}, s32[1,1,2,1024]{3,2,1,0:T(2,128)}, u32[]{:S(2)}) copy-start(s32[1,1,2,1024]{3,2,1,0:T(2,128)} %param.12) | copy-start | bytes 24580
  15.1 19.9 %copy-start.13 = (s32[1,1,16,1]{2,3,1,0:T(1,128)S(1)}, s32[1,1,16,1]{2,3,1,0:T(1,128)}, u32[]{:S(2)}) copy-start(s32[1,1,16,1]{2,3,1,0:T(1,128)} %param.15) | copy-start | bytes 196
  15.2 19.9 %copy-start.15 = (s32[1,1,16,1]{2,3,1,0:T(1,128)S(1)}, s32[1,1,16,1]{2,3,1,0:T(1,128)}, u32[]{:S(2)}) copy-start(s32[1,1,16,1]{2,3,1,0:T(1,128)} %param.14) | copy-start | bytes 196
  15.2 9.4 %collective-permute-start = (bf16[4,128,1024]{2,1,0:T(8,128)(2,1)S(1)}, bf16[4,128,1024]{2,1,0:T(8,128)(2,1)}, u32[]{:S(2)}, u32[]{:S(2)}) collective-permute-start(bf16[4,128,1024]{2,1,0:T(8,128)(2,1)S(1)} %sort_leaves.1.leaves_ref.refs_0_), channel_id=1, source_target_pairs={{0,1},{1,0},{2,3},{3,2},{4,5},{5,4},{6,7},{7,6},{8,9},{9,8},{10,11... | collective-permute-start | bytes 3145736 | tf_op jit(solution)/shard_map/ppermute | solution.py:371
  17.9 20.5 %collective-permute-start.1 = (bf16[4,128,1024]{2,1,0:T(8,128)(2,1)S(1)}, bf16[4,128,1024]{2,1,0:T(8,128)(2,1)}, u32[]{:S(2)}, u32[]{:S(2)}) collective-permute-start(bf16[4,128,1024]{2,1,0:T(8,128)(2,1)S(1)} %sort_leaves.1.leaves_ref.refs_0_), channel_id=1, source_target_pairs={{0,2},{1,15},{2,4},{3,1},{4,6},{5,3},{6,8},{7,5},{8,10},{9,7},{10,... | collective-permute-start | bytes 3145736 | tf_op jit(solution)/shard_map/ppermute | solution.py:376
  24.6 21.5 %collective-permute-start.2 = (bf16[4,128,1024]{2,1,0:T(8,128)(2,1)}, bf16[4,128,1024]{2,1,0:T(8,128)(2,1)}, u32[]{:S(2)}, u32[]{:S(2)}) collective-permute-start(bf16[4,128,1024]{2,1,0:T(8,128)(2,1)} %collective-permute-done.refs_1_), channel_id=1, source_target_pairs={{0,2},{1,15},{2,4},{3,1},{4,6},{5,3},{6,8},{7,5},{8,10},{9,7},{10,... | collective-permute-start | bytes 3145736 | tf_op jit(solution)/shard_map/ppermute | solution.py:376
  37.0 1.4 copy-start.6
  38.4 24.7 %collective-permute-start.3 = (bf16[4,128,1024]{2,1,0:T(8,128)(2,1)}, bf16[4,128,1024]{2,1,0:T(8,128)(2,1)}, u32[]{:S(2)}, u32[]{:S(2)}) collective-permute-start(bf16[4,128,1024]{2,1,0:T(8,128)(2,1)} %collective-permute-done.1.refs_1_.refs_0_), channel_id=1, source_target_pairs={{0,2},{1,15},{2,4},{3,1},{4,6},{5,3},{6,8},{7,5},{8,10},{9,7},{10,... | collective-permute-start | bytes 3145736 | tf_op jit(solution)/shard_map/ppermute | solution.py:376
  46.1 34.2 %collective-permute-start.4 = (bf16[4,128,1024]{2,1,0:T(8,128)(2,1)}, bf16[4,128,1024]{2,1,0:T(8,128)(2,1)S(1)}, u32[]{:S(2)}, u32[]{:S(2)}) collective-permute-start(bf16[4,128,1024]{2,1,0:T(8,128)(2,1)} %collective-permute-done.2.refs_2_.refs_1_), channel_id=1, source_target_pairs={{0,2},{1,15},{2,4},{3,1},{4,6},{5,3},{6,8},{7,5},{8,10},{9,7},{10,... | collective-permute-start | bytes 3145736 | tf_op jit(solution)/shard_map/ppermute | solution.py:376
  51.7 20.5 %all-to-all-start = ((s32[16,1,16]{2,1,0:T(1,128)}), s32[16,1,16]{2,1,0:T(1,128)S(1)}, u32[]{:S(2)}, u32[]{:S(2)}) async-start(s32[16,1,16]{2,1,0:T(1,128)} %broadcast_in_dim.3), calls=%async_computation | async-start | bytes 16384 | tf_op jit(solution)/shard_map/all_to_all | solution.py:394
  57.3 1.6 %copy-start.7 = (f32[4096,128]{1,0:T(8,128)S(1)}, f32[4096,128]{1,0:T(8,128)}, u32[]{:S(2)}) copy-start(f32[4096,128]{1,0:T(8,128)} %copy-done.6) | copy-start | bytes 6291460
  61.7 1.4 copy-start
  75.3 26.9 %collective-permute-start.5 = (bf16[3,128,1024]{2,1,0:T(8,128)(2,1)}, bf16[3,128,1024]{2,1,0:T(8,128)(2,1)}, u32[]{:S(2)}, u32[]{:S(2)}) collective-permute-start(bf16[3,128,1024]{2,1,0:T(8,128)(2,1)} %get-tuple-element.37), channel_id=1, source_target_pairs={{0,1},{1,0},{2,3},{3,2},{4,5},{5,4},{6,7},{7,6},{8,9},{9,8},{10,11... | collective-permute-start | bytes 2359304 | tf_op jit(solution)/shard_map/ppermute | solution.py:371
  78.0 31.1 %collective-permute-start.6 = (bf16[3,128,1024]{2,1,0:T(8,128)(2,1)}, bf16[3,128,1024]{2,1,0:T(8,128)(2,1)}, u32[]{:S(2)}, u32[]{:S(2)}) collective-permute-start(bf16[3,128,1024]{2,1,0:T(8,128)(2,1)} %get-tuple-element.32), channel_id=1, source_target_pairs={{0,2},{1,15},{2,4},{3,1},{4,6},{5,3},{6,8},{7,5},{8,10},{9,7},{10,... | collective-permute-start | bytes 2359304 | tf_op jit(solution)/shard_map/ppermute | solution.py:376
  82.0 27.2 %collective-permute-start.7 = (bf16[3,128,1024]{2,1,0:T(8,128)(2,1)}, bf16[3,128,1024]{2,1,0:T(8,128)(2,1)}, u32[]{:S(2)}, u32[]{:S(2)}) collective-permute-start(bf16[3,128,1024]{2,1,0:T(8,128)(2,1)} %copy_leaves.4), channel_id=1, source_target_pairs={{0,2},{1,15},{2,4},{3,1},{4,6},{5,3},{6,8},{7,5},{8,10},{9,7},{10,... | collective-permute-start | bytes 2359304 | tf_op jit(solution)/shard_map/ppermute | solution.py:376
  85.8 1.6 %copy-start.1 = (f32[4096,128]{1,0:T(8,128)S(1)}, f32[4096,128]{1,0:T(8,128)}, u32[]{:S(2)}) copy-start(f32[4096,128]{1,0:T(8,128)} %copy-done) | copy-start | bytes 6291460
  91.5 1.3 copy-start.2
  92.8 1.3 copy-start.10
  101.5 0.7 copy-start.8
  102.2 1.6 %copy-start.3 = (f32[4096,128]{1,0:T(8,128)S(1)}, f32[4096,128]{1,0:T(8,128)}, u32[]{:S(2)}) copy-start(f32[4096,128]{1,0:T(8,128)} %copy-done.2) | copy-start | bytes 6291460
  107.9 1.3 copy-start.4
  109.2 8.5 %copy-start.17 = (s32[1,1,4,3]{2,1,3,0:T(1,128)S(1)}, s32[1,1,4,3]{2,1,3,0:T(1,128)}, u32[]{:S(2)}) copy-start(s32[1,1,4,3]{2,1,3,0:T(1,128)} %param.13) | copy-start | bytes 148
  111.9 17.1 %collective-permute-start.8 = (bf16[3,128,1024]{2,1,0:T(8,128)(2,1)}, bf16[3,128,1024]{2,1,0:T(8,128)(2,1)S(1)}, u32[]{:S(2)}, u32[]{:S(2)}) collective-permute-start(bf16[3,128,1024]{2,1,0:T(8,128)(2,1)} %get-tuple-element.42), channel_id=1, source_target_pairs={{0,1},{1,0},{2,3},{3,2},{4,5},{5,4},{6,7},{7,6},{8,9},{9,8},{10,11... | collective-permute-start | bytes 2359304 | tf_op jit(solution)/shard_map/ppermute | solution.py:371
  113.9 15.2 %collective-permute-start.9 = (bf16[2,128,1024]{2,1,0:T(8,128)(2,1)}, bf16[2,128,1024]{2,1,0:T(8,128)(2,1)S(1)}, u32[]{:S(2)}, u32[]{:S(2)}) collective-permute-start(bf16[2,128,1024]{2,1,0:T(8,128)(2,1)} %get-tuple-element.40), channel_id=1, source_target_pairs={{0,2},{1,15},{2,4},{3,1},{4,6},{5,3},{6,8},{7,5},{8,10},{9,7},{10,... | collective-permute-start | bytes 1572872 | tf_op jit(solution)/shard_map/ppermute | solution.py:376
  117.8 1.6 %copy-start.5 = (f32[4096,128]{1,0:T(8,128)S(1)}, f32[4096,128]{1,0:T(8,128)}, u32[]{:S(2)}) copy-start(f32[4096,128]{1,0:T(8,128)} %copy-done.4) | copy-start | bytes 6291460
  119.4 1.0 copy-start.9
Sparse Core Ops, SparseCore 0:
  35.1 32.4 all-gather.2

commit v5 on v4

--- a/solution.py
+++ b/solution.py
@@ -387,25 +387,35 @@
     near = functools.partial(near_terms, me, source, target)
     place = (lax.axis_index("leaf") % 8).astype(jnp.int32).reshape(1)
 
+    row = jnp.broadcast_to(source, (16, 1, 16))
+    table = lax.all_to_all(row, "task", split_axis=0, concat_axis=0, tiled=True)
     leaves = sort_leaves(point_order.reshape(-1), points.T, weights.T)
+    leaves = after(leaves, table)
     one_a = hop(leaves)
     beside = partner(leaves, "task", 0)
-    row = after(jnp.broadcast_to(source, (16, 1, 16)), leaves)
-    table = lax.all_to_all(row, "task", split_axis=0, concat_axis=0, tiled=True)
-    left = target_factors(leaves)
-    beside = after(beside, left)
     one_b = hop(beside)
+    left = target_factors(after(leaves, beside))
     node = first_node(node_order.reshape(1, -1)[:, :SKEL], merge_order[0, 0, :, :SKEL], after(leaves, beside))
     groups = [list(range(8 * x, 8 * x + 8)) for x in range(lax.axis_size("leaf") // 8)]
-    nodes = lax.all_gather(node, "leaf", axis_index_groups=groups)
-    beside = after(beside, node)
-    total = near(left, None, [(leaves, 0, 0, None), (beside, 0, 1, None)])
-
-    one_a = after(one_a, total)
+    nodes = lax.all_to_all(
+        jnp.broadcast_to(node, (8,) + node.shape), "leaf", split_axis=0, concat_axis=0, axis_index_groups=groups, tiled=True
+    )
+
+    one_a = after(one_a, node)
     two_a = hop(one_a)
     one_b = after(one_b, one_a)
     two_b = hop(one_b)
-    total = near(left, total, [(one_a, 1, 0, None), (one_b, 1, 1, None)])
+    siblings = sibling_nodes(place, after(nodes, one_b))
+    total = near(
+        left,
+        None,
+        [
+            (leaves, 0, 0, None),
+            (after(beside, siblings), 0, 1, None),
+            (one_a, 1, 0, None),
+            (one_b, 1, 1, None),
+        ],
+    )
     two_a = after(two_a, total)
     send, send_side = copy_leaves(
         me,
@@ -423,12 +433,12 @@
         me, table, [two_b], [[(0, asked(2, 1, 1, 0)), (0, asked(2, 1, 1, 1)), (0, asked(2, 1, 2, 0))]]
     )
     three_b = hop(send)
-    total = near(left, total, [(two_a, 2, 0, None), (after(two_b, send), 2, 1, None)])
-    nodes = after(nodes, total)
-    siblings = sibling_nodes(place, nodes)
-    total = after(total, siblings)
-    side = after(side, siblings)
-    total = near(left, total, [(side, -1, 1, 0), (side, -1, 0, 1), (side, -2, 1, 2)])
+    side = after(side, send)
+    total = near(
+        left,
+        total,
+        [(two_a, 2, 0, None), (two_b, 2, 1, None), (side, -1, 1, 0), (side, -1, 0, 1), (side, -2, 1, 2)],
+    )
     three_a = after(three_a, total)
     send, send_side = copy_leaves(
         me,

time: 149 us -> 149 us (level)
  the two profiles are of different devices: /device:TPU:387 before, /device:TPU:1 now
where the time goes in v5:
time: 149 us; the launch traced here: 147 us
  Pallas kernels  55.9 us (38%)
  starting transfers between devices  51.7 us (35%)
  waiting for transfers between devices  28.4 us (19%)
  local copies, waits for them, and re-layouts  10 us (7%)
    ppermute x7, starting transfers between devices, hop(): return lax.ppermute(value, 'task', pairs)  23.3 us
    all_to_all x1, waiting for transfers between devices, body(): lax.all_to_all(jnp.broadcast_to(node, (8,) + node.shape), 'leaf', split_a...  22 us
    pallas_call x3, Pallas kernels, near_terms(): pl.pallas_call(functools.partial(near_kernel, plan, first, last), out_sha...  19.1 us
    all_to_all x1, starting transfers between devices, body(): table = lax.all_to_all(row, 'task', split_axis=0, concat_axis=0, tiled=True)  10.1 us
    ppermute x3, starting transfers between devices, partner(): return lax.ppermute(value, axis, pairs)  9.87 us
    pallas_call x1, Pallas kernels, sibling_nodes(): pl.pallas_call(siblings_kernel, out_shape=jax.ShapeDtypeStruct((LEVELS, 2...  8.71 us
    all_to_all x1, starting transfers between devices, body(): lax.all_to_all(jnp.broadcast_to(node, (8,) + node.shape), 'leaf', split_a...  8.44 us
    pallas_call x1, Pallas kernels, far_terms(): pl.pallas_call(far_kernel, out_shape=jax.ShapeDtypeStruct((PTS, 2 * F), j...  7.93 us
  transfers between devices with their start and end apart: 12, of which 3 were waited for; matrix products, arithmetic and copies ran while one was open for 1% of the time, Pallas kernels for 31%

profile of v5, /device:TPU:1, one launch (start us, length us, event | category | flops | bytes accessed | tf_op | source)
XLA Modules:
  0.0 146.6 jit_solution(10526377392457037541)
XLA Ops:
  0.0 1.3 broadcast_in_dim.6
  1.3 10.1 %all-to-all-start = ((s32[16,1,16]{2,1,0:T(1,128)}), s32[16,1,16]{2,1,0:T(1,128)S(1)}, u32[]{:S(2)}, u32[]{:S(2)}) async-start(s32[16,1,16]{2,1,0:T(1,128)} %broadcast_in_dim.6), calls=%async_computation | async-start | bytes 16384 | tf_op jit(solution)/shard_map/all_to_all | solution.py:391
  11.4 1.0 copy-done.10
  12.5 1.0 copy-done.11
  14.2 5.8 %sort_leaves.1.leaves_ref.refs_0_ = bf16[4,128,1024]{2,1,0:T(8,128)(2,1)S(1)} custom-call(s32[4096]{0:T(1024)S(1)} %bitcast.13, bf16[64,4096]{1,0:T(8,128)(2,1)S(1)} %bitcast.11, bf16[64,4096]{1,0:T(8,128)(2,1)S(1)} %bitcast.12), custom_call_target="tpu_custom_call" | custom-call | bytes 1000 | tf_op jit(solution)/shard_map/sort_leaves/pallas_call | solution.py:54
  20.0 2.1 %collective-permute-start = (bf16[4,128,1024]{2,1,0:T(8,128)(2,1)S(1)}, bf16[4,128,1024]{2,1,0:T(8,128)(2,1)S(1)}, u32[]{:S(2)}, u32[]{:S(2)}) collective-permute-start(bf16[4,128,1024]{2,1,0:T(8,128)(2,1)S(1)} %sort_leaves.1.leaves_ref.refs_0_), channel_id=1, source_target_pairs={{0,1},{1,0},{2,3},{3,2},{4,5},{5,4},{6,7},{7,6},{8,9},{9,8},{10,11... | collective-permute-start | bytes 3145736 | tf_op jit(solution)/shard_map/ppermute | solution.py:371
  22.2 4.7 %collective-permute-start.2 = (bf16[4,128,1024]{2,1,0:T(8,128)(2,1)S(1)}, bf16[4,128,1024]{2,1,0:T(8,128)(2,1)}, u32[]{:S(2)}, u32[]{:S(2)}) collective-permute-start(bf16[4,128,1024]{2,1,0:T(8,128)(2,1)S(1)} %sort_leaves.1.leaves_ref.refs_0_), channel_id=1, source_target_pairs={{0,2},{1,15},{2,4},{3,1},{4,6},{5,3},{6,8},{7,5},{8,10},{9,7},{10,... | collective-permute-start | bytes 3145736 | tf_op jit(solution)/shard_map/ppermute | solution.py:376
  26.9 3.1 %collective-permute-start.1 = (bf16[4,128,1024]{2,1,0:T(8,128)(2,1)S(1)}, bf16[4,128,1024]{2,1,0:T(8,128)(2,1)}, u32[]{:S(2)}, u32[]{:S(2)}) collective-permute-start(bf16[4,128,1024]{2,1,0:T(8,128)(2,1)S(1)} %collective-permute-done.refs_1_), channel_id=1, source_target_pairs={{0,2},{1,15},{2,4},{3,1},{4,6},{5,3},{6,8},{7,5},{8,10},{9,7},{10,... | collective-permute-start | bytes 3145736 | tf_op jit(solution)/shard_map/ppermute | solution.py:376
  30.7 6.0 %first_node.1 = bf16[144,512]{1,0:T(8,128)(2,1)S(1)} custom-call(s32[1,512]{1,0:T(1,128)S(1)} %slice.8.index_ref, s32[2,512]{1,0:T(2,128)S(1)} %slice_bitcast_fusion.merge_ref, bf16[4,128,1024]{2,1,0:T(8,128)(2,1)S(1)} %sort_leaves.1.leaves_ref.refs_0_), custom_call_target="tpu_custom_call" | custom-call | bytes 1000 | tf_op jit(solution)/shard_map/first_node/pallas_call | solution.py:167
  36.8 1.1 broadcast_in_dim.7
  37.9 8.4 %all-to-all-start.1 = ((bf16[8,144,512]{2,1,0:T(8,128)(2,1)}), bf16[8,144,512]{2,1,0:T(8,128)(2,1)}, u32[]{:S(2)}, u32[]{:S(2)}) async-start(bf16[8,144,512]{2,1,0:T(8,128)(2,1)} %broadcast_in_dim.7), calls=%async_computation.1 | async-start | bytes 2359296 | tf_op jit(solution)/shard_map/all_to_all | solution.py:400
  46.3 3.1 %collective-permute-start.3 = (bf16[4,128,1024]{2,1,0:T(8,128)(2,1)}, bf16[4,128,1024]{2,1,0:T(8,128)(2,1)}, u32[]{:S(2)}, u32[]{:S(2)}) collective-permute-start(bf16[4,128,1024]{2,1,0:T(8,128)(2,1)} %collective-permute-done.2.refs_2_.refs_0_), channel_id=1, source_target_pairs={{0,2},{1,15},{2,4},{3,1},{4,6},{5,3},{6,8},{7,5},{8,10},{9,7},{10,... | collective-permute-start | bytes 3145736 | tf_op jit(solution)/shard_map/ppermute | solution.py:376
  49.9 5.1 %collective-permute-start.4 = (bf16[4,128,1024]{2,1,0:T(8,128)(2,1)}, bf16[4,128,1024]{2,1,0:T(8,128)(2,1)}, u32[]{:S(2)}, u32[]{:S(2)}) collective-permute-start(bf16[4,128,1024]{2,1,0:T(8,128)(2,1)} %collective-permute-done.1.refs_3_.refs_1_), channel_id=1, source_target_pairs={{0,2},{1,15},{2,4},{3,1},{4,6},{5,3},{6,8},{7,5},{8,10},{9,7},{10,... | collective-permute-start | bytes 3145736 | tf_op jit(solution)/shard_map/ppermute | solution.py:376
  55.0 1.6 %target_factors.1.left_ref = bf16[4096,256]{1,0:T(8,128)(2,1)S(1)} custom-call(bf16[4,128,1024]{2,1,0:T(8,128)(2,1)S(1)} %sort_leaves.1.leaves_ref.refs_0_), custom_call_target="tpu_custom_call" | custom-call | bytes 1000 | tf_op jit(solution)/shard_map/target_factors/pallas_call | solution.py:108
  56.6 22.0 %all-to-all-done.1.nodes_ref = bf16[8,144,512]{2,1,0:T(8,128)(2,1)} async-done(((bf16[8,144,512]{2,1,0:T(8,128)(2,1)}), bf16[8,144,512]{2,1,0:T(8,128)(2,1)}, u32[]{:S(2)}, u32[]{:S(2)}) %all-to-all-start.1) | async-done | bytes 1179680 | tf_op jit(solution)/shard_map/all_to_all | solution.py:400
  78.6 8.7 %sibling_nodes.1.siblings_ref = bf16[3,128,512]{2,1,0:T(8,128)(2,1)S(1)} custom-call(s32[1]{0:T(128)} %bitcast.6.place_ref, bf16[8,144,512]{2,1,0:T(8,128)(2,1)} %all-to-all-done.1.nodes_ref), custom_call_target="tpu_custom_call" | custom-call | bytes 1000 | tf_op jit(solution)/shard_map/sibling_nodes/pallas_call | solution.py:203
  87.3 4.8 %near_terms.3.refs_0_ = f32[4096,128]{1,0:T(8,128)S(1)} custom-call(s32[1]{0:T(128)} %bitcast.me_ref, s32[16]{0:T(128)S(1)} %bitcast.15, s32[16]{0:T(128)S(1)} %bitcast.18, bf16[4096,256]{1,0:T(8,128)(2,1)S(1)} %target_factors.1.left_ref, bf16[4,128,1024]{2,1,0:T(8,128)(2,1)S(1)} %sort_leaves.1.leaves_ref.refs_0_, bf16[4,128,1024]{2,1,0:T(8,128)(2,1)S(1)} %copy-done.9, ...), custom_call_target="tpu_custom_call" | custom-call | bytes 1000 | tf_op jit(solution)/shard_map/near_terms/pallas_call | solution.py:357
  92.1 2.2 %copy_leaves.3 = (bf16[3,128,1024]{2,1,0:T(8,128)(2,1)S(1)}, bf16[3,128,1024]{2,1,0:T(8,128)(2,1)S(1)}) custom-call(s32[1]{0:T(128)} %bitcast.me_ref, s32[16,1,16]{2,1,0:T(1,128)S(1)} %all-to-all-done.table_ref, bf16[4,128,1024]{2,1,0:T(8,128)(2,1)} %collective-permute-done.2.refs_2_.refs_0_, bf16[4,128,1024]{2,1,0:T(8,128)(2,1)} %collective-permute-done.1.refs_3_.refs_1_, ...), custom_call_target="tpu_custom_call" | custom-call | bytes 1000 | tf_op jit(solution)/shard_map/copy_leaves/pallas_call | solution.py:290
  94.3 3.8 %collective-permute-start.5 = (bf16[3,128,1024]{2,1,0:T(8,128)(2,1)S(1)}, bf16[3,128,1024]{2,1,0:T(8,128)(2,1)S(1)}, u32[]{:S(2)}, u32[]{:S(2)}) collective-permute-start(bf16[3,128,1024]{2,1,0:T(8,128)(2,1)S(1)} %get-tuple-element.31), channel_id=1, source_target_pairs={{0,1},{1,0},{2,3},{3,2},{4,5},{5,4},{6,7},{7,6},{8,9},{9,8},{10,11... | collective-permute-start | bytes 2359304 | tf_op jit(solution)/shard_map/ppermute | solution.py:371
  98.0 1.9 %collective-permute-start.6 = (bf16[3,128,1024]{2,1,0:T(8,128)(2,1)S(1)}, bf16[3,128,1024]{2,1,0:T(8,128)(2,1)S(1)}, u32[]{:S(2)}, u32[]{:S(2)}) collective-permute-start(bf16[3,128,1024]{2,1,0:T(8,128)(2,1)S(1)} %get-tuple-element.29), channel_id=1, source_target_pairs={{0,2},{1,15},{2,4},{3,1},{4,6},{5,3},{6,8},{7,5},{8,10},{9,7},{10,... | collective-permute-start | bytes 2359304 | tf_op jit(solution)/shard_map/ppermute | solution.py:376
  100.0 1.9 %copy_leaves.4 = bf16[3,128,1024]{2,1,0:T(8,128)(2,1)S(1)} custom-call(s32[1]{0:T(128)} %bitcast.me_ref, s32[16,1,16]{2,1,0:T(1,128)S(1)} %all-to-all-done.table_ref, bf16[4,128,1024]{2,1,0:T(8,128)(2,1)} %collective-permute-done.4.refs_0_.refs_2_), custom_call_target="tpu_custom_call" | custom-call | bytes 1000 | tf_op jit(solution)/shard_map/copy_leaves/pallas_call | solution.py:290
  101.9 3.4 %collective-permute-start.7 = (bf16[3,128,1024]{2,1,0:T(8,128)(2,1)S(1)}, bf16[3,128,1024]{2,1,0:T(8,128)(2,1)S(1)}, u32[]{:S(2)}, u32[]{:S(2)}) collective-permute-start(bf16[3,128,1024]{2,1,0:T(8,128)(2,1)S(1)} %copy_leaves.4), channel_id=1, source_target_pairs={{0,2},{1,15},{2,4},{3,1},{4,6},{5,3},{6,8},{7,5},{8,10},{9,7},{10,... | collective-permute-start | bytes 2359304 | tf_op jit(solution)/shard_map/ppermute | solution.py:376
  105.3 6.8 %near_terms.4.before_ref = f32[4096,128]{1,0:T(8,128)S(1)} custom-call(s32[1]{0:T(128)} %bitcast.me_ref, s32[16]{0:T(128)S(1)} %bitcast.16, s32[16]{0:T(128)S(1)} %bitcast.19, bf16[4096,256]{1,0:T(8,128)(2,1)S(1)} %target_factors.1.left_ref, f32[4096,128]{1,0:T(8,128)S(1)} %near_terms.3.refs_0_, ...), custom_call_target="tpu_custom_call" | custom-call | bytes 1000 | tf_op jit(solution)/shard_map/near_terms/pallas_call | solution.py:357
  112.1 1.3 copy-done
  113.5 6.0 %collective-permute-done.7.refs_2_ = bf16[3,128,1024]{2,1,0:T(8,128)(2,1)S(1)} collective-permute-done((bf16[3,128,1024]{2,1,0:T(8,128)(2,1)S(1)}, bf16[3,128,1024]{2,1,0:T(8,128)(2,1)S(1)}, u32[]{:S(2)}, u32[]{:S(2)}) %collective-permute-start.7) | collective-permute-done | bytes 786464 | tf_op jit(solution)/shard_map/ppermute | solution.py:376
  119.5 2.7 %copy_leaves.5 = (bf16[2,128,1024]{2,1,0:T(8,128)(2,1)}, bf16[3,128,1024]{2,1,0:T(8,128)(2,1)}) custom-call(s32[1]{0:T(128)} %bitcast.me_ref, s32[16,1,16]{2,1,0:T(1,128)S(1)} %all-to-all-done.table_ref, bf16[4,128,1024]{2,1,0:T(8,128)(2,1)} %collective-permute-done.4.refs_0_.refs_2_, bf16[3,128,1024]{2,1,0:T(8,128)(2,1)S(1)} %collective-permute-done.6.refs_1_, ...), custom_call_target="tpu_custom_call" | custom-call | bytes 1000 | tf_op jit(solution)/shard_map/copy_leaves/pallas_call | solution.py:290
  122.2 4.0 %collective-permute-start.8 = (bf16[3,128,1024]{2,1,0:T(8,128)(2,1)}, bf16[3,128,1024]{2,1,0:T(8,128)(2,1)S(1)}, u32[]{:S(2)}, u32[]{:S(2)}) collective-permute-start(bf16[3,128,1024]{2,1,0:T(8,128)(2,1)} %get-tuple-element.36), channel_id=1, source_target_pairs={{0,1},{1,0},{2,3},{3,2},{4,5},{5,4},{6,7},{7,6},{8,9},{9,8},{10,11... | collective-permute-start | bytes 2359304 | tf_op jit(solution)/shard_map/ppermute | solution.py:371
  126.2 1.9 %collective-permute-start.9 = (bf16[2,128,1024]{2,1,0:T(8,128)(2,1)}, bf16[2,128,1024]{2,1,0:T(8,128)(2,1)S(1)}, u32[]{:S(2)}, u32[]{:S(2)}) collective-permute-start(bf16[2,128,1024]{2,1,0:T(8,128)(2,1)} %get-tuple-element.34), channel_id=1, source_target_pairs={{0,2},{1,15},{2,4},{3,1},{4,6},{5,3},{6,8},{7,5},{8,10},{9,7},{10,... | collective-permute-start | bytes 1572872 | tf_op jit(solution)/shard_map/ppermute | solution.py:376
  128.3 1.6 %copy-done.1 = f32[4096,128]{1,0:T(8,128)S(1)} copy-done((f32[4096,128]{1,0:T(8,128)S(1)}, f32[4096,128]{1,0:T(8,128)}, u32[]{:S(2)}) %copy-start.1) | copy-done | bytes 2097176
  129.9 1.0 copy-done.7
  130.9 7.9 %far_terms.1.refs_0_ = f32[4096,128]{1,0:T(8,128)S(1)} custom-call(s32[12]{0:T(128)S(1)} %reshape.25.flags_ref, bf16[4096,256]{1,0:T(8,128)(2,1)S(1)} %target_factors.1.left_ref, f32[4096,128]{1,0:T(8,128)S(1)} %copy-done.1, bf16[3,128,512]{2,1,0:T(8,128)(2,1)S(1)} %copy-done.7), custom_call_target="tpu_custom_call" | custom-call | bytes 1000 | tf_op jit(solution)/shard_map/far_terms/pallas_call | solution.py:251
  138.9 7.5 %near_terms.5 = f32[64,4096]{1,0:T(8,128)} custom-call(s32[1]{0:T(128)} %bitcast.me_ref, s32[16]{0:T(128)S(1)} %bitcast.17, s32[16]{0:T(128)S(1)} %bitcast.20, bf16[4096,256]{1,0:T(8,128)(2,1)S(1)} %target_factors.1.left_ref, f32[4096,128]{1,0:T(8,128)S(1)} %far_terms.1.refs_0_, bf16[3,128,1024]{2,1,0:T(8,128)(2,1)S(1)} %copy-done.3, ...), custom_call_target="tpu_custom_call" | custom-call | bytes 1000 | tf_op jit(solution)/shard_map/near_terms/pallas_call | solution.py:357
  (43 shorter events, 2.1 us)
Async XLA Ops:
  0.0 30.0 %copy-start.15 = (s32[1,1,2,1024]{3,2,1,0:T(2,128)S(1)}, s32[1,1,2,1024]{3,2,1,0:T(2,128)}, u32[]{:S(2)}) copy-start(s32[1,1,2,1024]{3,2,1,0:T(2,128)} %param.12) | copy-start | bytes 24580
  1.3 18.7 %all-to-all-start = ((s32[16,1,16]{2,1,0:T(1,128)}), s32[16,1,16]{2,1,0:T(1,128)S(1)}, u32[]{:S(2)}, u32[]{:S(2)}) async-start(s32[16,1,16]{2,1,0:T(1,128)} %broadcast_in_dim.6), calls=%async_computation | async-start | bytes 16384 | tf_op jit(solution)/shard_map/all_to_all | solution.py:391
  11.4 1.0 copy-start.10
  12.5 1.0 copy-start.11
  13.5 0.7 copy-start.12
  20.0 6.9 %collective-permute-start = (bf16[4,128,1024]{2,1,0:T(8,128)(2,1)S(1)}, bf16[4,128,1024]{2,1,0:T(8,128)(2,1)S(1)}, u32[]{:S(2)}, u32[]{:S(2)}) collective-permute-start(bf16[4,128,1024]{2,1,0:T(8,128)(2,1)S(1)} %sort_leaves.1.leaves_ref.refs_0_), channel_id=1, source_target_pairs={{0,1},{1,0},{2,3},{3,2},{4,5},{5,4},{6,7},{7,6},{8,9},{9,8},{10,11... | collective-permute-start | bytes 3145736 | tf_op jit(solution)/shard_map/ppermute | solution.py:371
  22.2 24.2 %collective-permute-start.2 = (bf16[4,128,1024]{2,1,0:T(8,128)(2,1)S(1)}, bf16[4,128,1024]{2,1,0:T(8,128)(2,1)}, u32[]{:S(2)}, u32[]{:S(2)}) collective-permute-start(bf16[4,128,1024]{2,1,0:T(8,128)(2,1)S(1)} %sort_leaves.1.leaves_ref.refs_0_), channel_id=1, source_target_pairs={{0,2},{1,15},{2,4},{3,1},{4,6},{5,3},{6,8},{7,5},{8,10},{9,7},{10,... | collective-permute-start | bytes 3145736 | tf_op jit(solution)/shard_map/ppermute | solution.py:376
  26.9 11.0 %copy-start.8 = (bf16[4,128,1024]{2,1,0:T(8,128)(2,1)}, bf16[4,128,1024]{2,1,0:T(8,128)(2,1)S(1)}, u32[]{:S(2)}) copy-start(bf16[4,128,1024]{2,1,0:T(8,128)(2,1)S(1)} %collective-permute-done.refs_1_) | copy-start | bytes 3145732
  26.9 22.9 %collective-permute-start.1 = (bf16[4,128,1024]{2,1,0:T(8,128)(2,1)S(1)}, bf16[4,128,1024]{2,1,0:T(8,128)(2,1)}, u32[]{:S(2)}, u32[]{:S(2)}) collective-permute-start(bf16[4,128,1024]{2,1,0:T(8,128)(2,1)S(1)} %collective-permute-done.refs_1_), channel_id=1, source_target_pairs={{0,2},{1,15},{2,4},{3,1},{4,6},{5,3},{6,8},{7,5},{8,10},{9,7},{10,... | collective-permute-start | bytes 3145736 | tf_op jit(solution)/shard_map/ppermute | solution.py:376
  37.9 40.7 %all-to-all-start.1 = ((bf16[8,144,512]{2,1,0:T(8,128)(2,1)}), bf16[8,144,512]{2,1,0:T(8,128)(2,1)}, u32[]{:S(2)}, u32[]{:S(2)}) async-start(bf16[8,144,512]{2,1,0:T(8,128)(2,1)} %broadcast_in_dim.7), calls=%async_computation.1 | async-start | bytes 2359296 | tf_op jit(solution)/shard_map/all_to_all | solution.py:400
  46.3 45.8 %collective-permute-start.3 = (bf16[4,128,1024]{2,1,0:T(8,128)(2,1)}, bf16[4,128,1024]{2,1,0:T(8,128)(2,1)}, u32[]{:S(2)}, u32[]{:S(2)}) collective-permute-start(bf16[4,128,1024]{2,1,0:T(8,128)(2,1)} %collective-permute-done.2.refs_2_.refs_0_), channel_id=1, source_target_pairs={{0,2},{1,15},{2,4},{3,1},{4,6},{5,3},{6,8},{7,5},{8,10},{9,7},{10,... | collective-permute-start | bytes 3145736 | tf_op jit(solution)/shard_map/ppermute | solution.py:376
  49.9 50.1 %collective-permute-start.4 = (bf16[4,128,1024]{2,1,0:T(8,128)(2,1)}, bf16[4,128,1024]{2,1,0:T(8,128)(2,1)}, u32[]{:S(2)}, u32[]{:S(2)}) collective-permute-start(bf16[4,128,1024]{2,1,0:T(8,128)(2,1)} %collective-permute-done.1.refs_3_.refs_1_), channel_id=1, source_target_pairs={{0,2},{1,15},{2,4},{3,1},{4,6},{5,3},{6,8},{7,5},{8,10},{9,7},{10,... | collective-permute-start | bytes 3145736 | tf_op jit(solution)/shard_map/ppermute | solution.py:376
  55.0 32.3 %copy-start.13 = (s32[1,1,16,1]{2,3,1,0:T(1,128)S(1)}, s32[1,1,16,1]{2,3,1,0:T(1,128)}, u32[]{:S(2)}) copy-start(s32[1,1,16,1]{2,3,1,0:T(1,128)} %param.15) | copy-start | bytes 196
  55.0 32.3 %copy-start.14 = (s32[1,1,16,1]{2,3,1,0:T(1,128)S(1)}, s32[1,1,16,1]{2,3,1,0:T(1,128)}, u32[]{:S(2)}) copy-start(s32[1,1,16,1]{2,3,1,0:T(1,128)} %param.14) | copy-start | bytes 196
  78.6 8.7 %copy-start.9 = (bf16[4,128,1024]{2,1,0:T(8,128)(2,1)S(1)}, bf16[4,128,1024]{2,1,0:T(8,128)(2,1)}, u32[]{:S(2)}) copy-start(bf16[4,128,1024]{2,1,0:T(8,128)(2,1)} %copy-done.8) | copy-start | bytes 3145732
  87.3 4.8 %copy-start.6 = (bf16[3,128,512]{2,1,0:T(8,128)(2,1)}, bf16[3,128,512]{2,1,0:T(8,128)(2,1)S(1)}, u32[]{:S(2)}) copy-start(bf16[3,128,512]{2,1,0:T(8,128)(2,1)S(1)} %sibling_nodes.1.siblings_ref) | copy-start | bytes 1179652
  94.3 11.0 %collective-permute-start.5 = (bf16[3,128,1024]{2,1,0:T(8,128)(2,1)S(1)}, bf16[3,128,1024]{2,1,0:T(8,128)(2,1)S(1)}, u32[]{:S(2)}, u32[]{:S(2)}) collective-permute-start(bf16[3,128,1024]{2,1,0:T(8,128)(2,1)S(1)} %get-tuple-element.31), channel_id=1, source_target_pairs={{0,1},{1,0},{2,3},{3,2},{4,5},{5,4},{6,7},{7,6},{8,9},{9,8},{10,11... | collective-permute-start | bytes 2359304 | tf_op jit(solution)/shard_map/ppermute | solution.py:371
  98.0 15.4 %collective-permute-start.6 = (bf16[3,128,1024]{2,1,0:T(8,128)(2,1)S(1)}, bf16[3,128,1024]{2,1,0:T(8,128)(2,1)S(1)}, u32[]{:S(2)}, u32[]{:S(2)}) collective-permute-start(bf16[3,128,1024]{2,1,0:T(8,128)(2,1)S(1)} %get-tuple-element.29), channel_id=1, source_target_pairs={{0,2},{1,15},{2,4},{3,1},{4,6},{5,3},{6,8},{7,5},{8,10},{9,7},{10,... | collective-permute-start | bytes 2359304 | tf_op jit(solution)/shard_map/ppermute | solution.py:376
  101.9 17.6 %collective-permute-start.7 = (bf16[3,128,1024]{2,1,0:T(8,128)(2,1)S(1)}, bf16[3,128,1024]{2,1,0:T(8,128)(2,1)S(1)}, u32[]{:S(2)}, u32[]{:S(2)}) collective-permute-start(bf16[3,128,1024]{2,1,0:T(8,128)(2,1)S(1)} %copy_leaves.4), channel_id=1, source_target_pairs={{0,2},{1,15},{2,4},{3,1},{4,6},{5,3},{6,8},{7,5},{8,10},{9,7},{10,... | collective-permute-start | bytes 2359304 | tf_op jit(solution)/shard_map/ppermute | solution.py:376
  112.1 1.3 copy-start
  113.5 14.7 %copy-start.16 = (s32[1,1,4,3]{2,1,3,0:T(1,128)S(1)}, s32[1,1,4,3]{2,1,3,0:T(1,128)}, u32[]{:S(2)}) copy-start(s32[1,1,4,3]{2,1,3,0:T(1,128)} %param.13) | copy-start | bytes 148
  113.5 8.7 %copy-start.2 = (bf16[3,128,1024]{2,1,0:T(8,128)(2,1)}, bf16[3,128,1024]{2,1,0:T(8,128)(2,1)S(1)}, u32[]{:S(2)}) copy-start(bf16[3,128,1024]{2,1,0:T(8,128)(2,1)S(1)} %collective-permute-done.6.refs_1_) | copy-start | bytes 2359300
  119.5 2.7 %copy-start.4 = (bf16[3,128,1024]{2,1,0:T(8,128)(2,1)}, bf16[3,128,1024]{2,1,0:T(8,128)(2,1)S(1)}, u32[]{:S(2)}) copy-start(bf16[3,128,1024]{2,1,0:T(8,128)(2,1)S(1)} %collective-permute-done.7.refs_2_) | copy-start | bytes 2359300
  122.2 16.6 %collective-permute-start.8 = (bf16[3,128,1024]{2,1,0:T(8,128)(2,1)}, bf16[3,128,1024]{2,1,0:T(8,128)(2,1)S(1)}, u32[]{:S(2)}, u32[]{:S(2)}) collective-permute-start(bf16[3,128,1024]{2,1,0:T(8,128)(2,1)} %get-tuple-element.36), channel_id=1, source_target_pairs={{0,1},{1,0},{2,3},{3,2},{4,5},{5,4},{6,7},{7,6},{8,9},{9,8},{10,11... | collective-permute-start | bytes 2359304 | tf_op jit(solution)/shard_map/ppermute | solution.py:371
  126.2 12.7 %collective-permute-start.9 = (bf16[2,128,1024]{2,1,0:T(8,128)(2,1)}, bf16[2,128,1024]{2,1,0:T(8,128)(2,1)S(1)}, u32[]{:S(2)}, u32[]{:S(2)}) collective-permute-start(bf16[2,128,1024]{2,1,0:T(8,128)(2,1)} %get-tuple-element.34), channel_id=1, source_target_pairs={{0,2},{1,15},{2,4},{3,1},{4,6},{5,3},{6,8},{7,5},{8,10},{9,7},{10,... | collective-permute-start | bytes 1572872 | tf_op jit(solution)/shard_map/ppermute | solution.py:376
  128.3 1.6 %copy-start.1 = (f32[4096,128]{1,0:T(8,128)S(1)}, f32[4096,128]{1,0:T(8,128)}, u32[]{:S(2)}) copy-start(f32[4096,128]{1,0:T(8,128)} %copy-done) | copy-start | bytes 6291460
  129.9 1.0 copy-start.7
  130.9 8.0 %copy-start.3 = (bf16[3,128,1024]{2,1,0:T(8,128)(2,1)S(1)}, bf16[3,128,1024]{2,1,0:T(8,128)(2,1)}, u32[]{:S(2)}) copy-start(bf16[3,128,1024]{2,1,0:T(8,128)(2,1)} %copy-done.2) | copy-start | bytes 2359300
  130.9 8.0 %copy-start.5 = (bf16[3,128,1024]{2,1,0:T(8,128)(2,1)S(1)}, bf16[3,128,1024]{2,1,0:T(8,128)(2,1)}, u32[]{:S(2)}) copy-start(bf16[3,128,1024]{2,1,0:T(8,128)(2,1)} %copy-done.4) | copy-start | bytes 2359300
